TPU v7x, 256 devices: a whole 4x4x8 slice. The times are simulated.
256 devices in a mesh: bend: 2 (over core), head: 8 (over z), blk: 16 (over y, x).
Axes of the slice: x: 4, y: 4, z: 8, core: 2. Of those that a mesh axis runs over, the one named last changes fastest.
Arguments:
- queries: bfloat16 [32768, 1024], P(('bend', 'head', 'blk')), parts along dimension 0, may hold values from -6 to 6
- keys_in: bfloat16 [32768, 1024], P(('bend', 'head', 'blk')), parts along dimension 0, may hold values from -6 to 6
- values: bfloat16 [32768, 1024], P(('bend', 'head', 'blk')), parts along dimension 0, may hold values from -6 to 6
- d_out: bfloat16 [32768, 1024], P(('bend', 'head', 'blk')), parts along dimension 0, may hold values from -6 to 6
- token_count: int32 [2], P('bend'), parts along dimension 0, may hold values from 8192 to 16384
- block_ids: int32 [256], P('bend'), parts along dimension 0, may hold values from 0 to 127, each once
- neighbours: int32 [256, 10], P('bend'), parts along dimension 0, may hold values from 0 to 127, as said below
Outputs:
- grad_queries: bfloat16 [32768, 1024], P(('bend', 'head', 'blk')), parts along dimension 0
- grad_keys: bfloat16 [32768, 1024], P(('bend', 'head', 'blk')), parts along dimension 0
- grad_values: bfloat16 [32768, 1024], P(('bend', 'head', 'blk')), parts along dimension 0
There are 2 independent parts, one for each index of `bend`. A program takes and returns all parts, laid end to end along the dimension named above; each array names one. Nothing has to cross between parts.
Inputs may be any that keep to these rules, and one draw needn't show every extreme that they name: `neighbours`: column 0 of a row is the query block itself; the 10 entries of a row are distinct; every block appears in exactly 10 rows.
All inputs are finite; a program needn't handle non-finite values.
Results may differ from a plain program's by a relative error of at most 0.017.
Values may be sent and summed in bfloat16 or wider, within the bound.
No kernel may reach another device: no remote copies, remote signals or barrier semaphores. Data moves between devices by JAX's collectives and lax.ppermute only.
A program may use at most 128 MiB of HBM per device.

v0:
```python
import math

import jax
import jax.numpy as jnp
from jax import lax
from jax.sharding import PartitionSpec as P

HD = 64
BLK = 128


neg_fill = -1e30
row_target = 512


def lookup(entries, wanted):
    matches = wanted[..., None] == jnp.arange(entries.shape[0], dtype=jnp.int32)
    return jnp.sum(jnp.where(matches, entries, 0), axis=-1)


def lookup_rows(entries, wanted):
    matches = wanted[..., None] == jnp.arange(entries.shape[0], dtype=jnp.int32)
    return jnp.sum(jnp.where(matches[..., None], entries, 0), axis=-2)


def group_size(blocks, block_rows):
    target = max(1, min(blocks, row_target // block_rows))
    while blocks % target != 0:
        target = target - 1
    return target


def block_tables(block_ids, neighbours, blk_count, head_count, block_rows, shard_rows):
    per_shard = shard_rows // block_rows
    local_blocks = head_count * per_shard
    slot_ids = jnp.arange(blk_count * local_blocks, dtype=jnp.int32)
    source = slot_ids // local_blocks
    within = slot_ids % local_blocks
    stored = (within // per_shard * blk_count + source) * per_shard + within % per_shard
    global_slot = lookup(block_ids, stored)
    matches = global_slot[None, :] == slot_ids[:, None]
    slot_global = jnp.sum(jnp.where(matches, slot_ids[None, :], 0), axis=1)
    key_global = lookup_rows(neighbours, global_slot)
    key_slots = lookup(slot_global, key_global)
    offsets = jnp.arange(block_rows, dtype=jnp.int32)
    query_where = global_slot[:, None] * block_rows + offsets
    key_where = key_global[:, :, None] * block_rows + offsets
    return (key_slots, query_where, key_where)


def permitted(query_where, key_where, token_limit):
    inside = key_where[:, None] < token_limit
    itself = key_where[:, None] == query_where[:, :, None, None]
    return inside | itself


def head_masks(feature_width, head_width):
    heads_here = feature_width // head_width
    owner_head = jnp.arange(feature_width, dtype=jnp.int32) // head_width
    return owner_head[None, :] == jnp.arange(heads_here, dtype=jnp.int32)[:, None]


def attend_all(query_tile, key_tile, value_tile, grad_tile, allowed, masks, score_scale):
    heads_here = masks.shape[0]
    query_sum = jnp.zeros(query_tile.shape, jnp.float32)
    key_sum = jnp.zeros(key_tile.shape, jnp.float32)
    value_sum = jnp.zeros(key_tile.shape, jnp.float32)
    logs = []
    deltas = []
    for head in range(heads_here):
        column_mask = masks[head]
        query_head = jnp.where(column_mask, query_tile, jnp.zeros_like(query_tile))
        grad_head = jnp.where(column_mask, grad_tile, jnp.zeros_like(grad_tile))
        product = (
            jnp.einsum("gqf,gnkf->gqnk", query_head, key_tile, preferred_element_type=jnp.float32)
            * score_scale
        )
        largest = jnp.max(jnp.where(allowed, product, neg_fill), axis=(2, 3), keepdims=True)
        denominator = jnp.sum(
            jnp.where(allowed, jnp.exp(product - largest), 0.0), axis=(2, 3), keepdims=True
        )
        log_total = largest + jnp.log(denominator)
        probability = jnp.where(allowed, jnp.exp(product - log_total), 0.0)
        grad_probs = jnp.einsum(
            "gqf,gnkf->gqnk", grad_head, value_tile, preferred_element_type=jnp.float32
        )
        row_delta = jnp.sum(probability * grad_probs, axis=(2, 3), keepdims=True)
        grad_scores = (probability * (grad_probs - row_delta)).astype(jnp.bfloat16)
        prob_low = probability.astype(jnp.bfloat16)
        query_term = (
            jnp.einsum("gqnk,gnkf->gqf", grad_scores, key_tile, preferred_element_type=jnp.float32)
            * score_scale
        )
        query_sum = query_sum + jnp.where(column_mask, query_term, 0.0)
        key_sum = (
            key_sum
            + jnp.einsum(
                "gqnk,gqf->gnkf", grad_scores, query_head, preferred_element_type=jnp.float32
            )
            * score_scale
        )
        value_sum = value_sum + jnp.einsum(
            "gqnk,gqf->gnkf", prob_low, grad_head, preferred_element_type=jnp.float32
        )
        logs.append(log_total[:, :, 0, 0])
        deltas.append(row_delta[:, :, 0, 0])
    return (query_sum, key_sum, value_sum, jnp.stack(logs, axis=1), jnp.stack(deltas, axis=1))


def per_device(queries, keys_in, values, d_out, token_count, block_ids, neighbours):
    head_count = lax.axis_size("head")
    blk_count = lax.axis_size("blk")
    blk_index = lax.axis_index("blk")
    shard_rows = queries.shape[0]
    block_rows = BLK
    head_width = HD
    score_scale = 1.0 / math.sqrt(head_width)
    query_rows, key_rows, value_rows, grad_rows = (
        lax.all_to_all(queries, "head", split_axis=1, concat_axis=0, tiled=True),
        lax.all_to_all(keys_in, "head", split_axis=1, concat_axis=0, tiled=True),
        lax.all_to_all(values, "head", split_axis=1, concat_axis=0, tiled=True),
        lax.all_to_all(d_out, "head", split_axis=1, concat_axis=0, tiled=True),
    )
    feature_width = query_rows.shape[1]
    masks = head_masks(feature_width, head_width)
    local_blocks = query_rows.shape[0] // block_rows
    key_slots, query_where, key_where = block_tables(
        block_ids, neighbours, blk_count, head_count, block_rows, shard_rows
    )
    token_limit = token_count[0]
    first_slot = blk_index * local_blocks
    my_key_slots = lax.dynamic_slice_in_dim(key_slots, first_slot, local_blocks, 0)
    my_query_where = lax.dynamic_slice_in_dim(query_where, first_slot, local_blocks, 0)
    my_key_where = lax.dynamic_slice_in_dim(key_where, first_slot, local_blocks, 0)
    row_valid = (my_query_where < token_limit).reshape(-1, 1)
    grad_rows = jnp.where(row_valid, grad_rows, jnp.zeros_like(grad_rows))
    query_blocks = query_rows.reshape(local_blocks, block_rows, feature_width)
    grad_blocks = grad_rows.reshape(local_blocks, block_rows, feature_width)
    gathered_keys, gathered_values = (
        lax.all_gather(key_rows, "blk", axis=0, tiled=True),
        lax.all_gather(value_rows, "blk", axis=0, tiled=True),
    )
    key_blocks = gathered_keys.reshape(-1, block_rows, feature_width)
    value_blocks = gathered_values.reshape(-1, block_rows, feature_width)
    group_blocks = group_size(local_blocks, block_rows)
    steps_count = local_blocks // group_blocks

    def local_tiles(start_block):
        query_tile = lax.dynamic_slice_in_dim(query_blocks, start_block, group_blocks, 0)
        grad_tile = lax.dynamic_slice_in_dim(grad_blocks, start_block, group_blocks, 0)
        slot_tile = lax.dynamic_slice_in_dim(my_key_slots, start_block, group_blocks, 0)
        key_tile = jnp.take(key_blocks, slot_tile, axis=0)
        value_tile = jnp.take(value_blocks, slot_tile, axis=0)
        allowed = permitted(
            lax.dynamic_slice_in_dim(my_query_where, start_block, group_blocks, 0),
            lax.dynamic_slice_in_dim(my_key_where, start_block, group_blocks, 0),
            token_limit,
        )
        return (query_tile, grad_tile, slot_tile, key_tile, value_tile, allowed)

    def summed_step(running, step_index):
        query_tile, grad_tile, slot_tile, key_tile, value_tile, allowed = local_tiles(
            step_index * group_blocks
        )
        query_part, key_part, value_part, log_total, row_delta = attend_all(
            query_tile, key_tile, value_tile, grad_tile, allowed, masks, score_scale
        )
        flat_slots = slot_tile.reshape(-1)
        key_sum = running[0].at[flat_slots].add(key_part.reshape(-1, block_rows, feature_width))
        value_sum = running[1].at[flat_slots].add(value_part.reshape(-1, block_rows, feature_width))
        return ((key_sum, value_sum), query_part)

    zero_acc = jnp.zeros((key_blocks.shape[0], block_rows, feature_width), jnp.float32)
    (key_sum, value_sum), query_parts = lax.scan(
        summed_step, (zero_acc, zero_acc), jnp.arange(steps_count, dtype=jnp.int32)
    )
    key_mine, value_mine = (
        lax.psum_scatter(
            key_sum.astype(jnp.bfloat16), "blk", scatter_dimension=0, tiled=True
        ).astype(jnp.float32),
        lax.psum_scatter(
            value_sum.astype(jnp.bfloat16), "blk", scatter_dimension=0, tiled=True
        ).astype(jnp.float32),
    )
    query_grad_rows = query_parts.reshape(local_blocks * block_rows, feature_width).astype(
        jnp.bfloat16
    )
    key_grad_rows = key_mine.reshape(local_blocks * block_rows, feature_width).astype(jnp.bfloat16)
    value_grad_rows = value_mine.reshape(local_blocks * block_rows, feature_width).astype(
        jnp.bfloat16
    )
    gradients = (
        lax.all_to_all(query_grad_rows, "head", split_axis=0, concat_axis=1, tiled=True),
        lax.all_to_all(key_grad_rows, "head", split_axis=0, concat_axis=1, tiled=True),
        lax.all_to_all(value_grad_rows, "head", split_axis=0, concat_axis=1, tiled=True),
    )
    return (gradients[0], gradients[1], gradients[2])


def solution(mesh):
    return jax.shard_map(
        per_device,
        mesh=mesh,
        in_specs=(
            P(("bend", "head", "blk"), None),
            P(("bend", "head", "blk"), None),
            P(("bend", "head", "blk"), None),
            P(("bend", "head", "blk"), None),
            P("bend"),
            P("bend"),
            P("bend", None),
        ),
        out_specs=(
            P(("bend", "head", "blk"), None),
            P(("bend", "head", "blk"), None),
            P(("bend", "head", "blk"), None),
        ),
        check_vma=False,
    )
```

profile of v0, /device:TPU:1, one launch (start us, length us, event | category | flops | bytes accessed | tf_op | source)
XLA Modules:
  0.0 436.3 jit_solution(2051696868726736746)
XLA Ops:
  7.3 1.2 copy.58
  8.6 19.3 %all_to_all.118 = bf16[128,8,128]{2,0,1:T(8,128)(2,1)} all-to-all(bf16[128,8,128]{2,0,1:T(8,128)(2,1)S(1)} %copy.59), channel_id=1, replica_groups=mesh['bend'=2,'head'=8,'blk'=16] {'head'}, dimensions={1} | all-to-all | bytes 524288 | tf_op jit(solution)/shard_map/all_to_all | solution.py:120
  28.0 1.1 copy.61
  29.3 12.5 %all_to_all.119 = bf16[128,8,128]{2,0,1:T(8,128)(2,1)} all-to-all(bf16[128,8,128]{2,0,1:T(8,128)(2,1)S(1)} %copy.62), channel_id=1, replica_groups=mesh['bend'=2,'head'=8,'blk'=16] {'head'}, dimensions={1} | all-to-all | bytes 524288 | tf_op jit(solution)/shard_map/all_to_all | solution.py:121
  41.8 0.8 copy.60
  42.7 3.4 all-to-all-start.2
  48.3 0.8 copy.57
  49.3 6.1 %all-to-all-done.2 = bf16[128,8,128]{0,2,1:T(8,128)(2,1)S(1)} async-done(((bf16[128,8,128]{0,2,1:T(8,128)(2,1)}), bf16[128,8,128]{0,2,1:T(8,128)(2,1)S(1)}, u32[]{:S(2)}, u32[]{:S(2)}) %all-to-all-start.2) | async-done | bytes 262176 | tf_op jit(solution)/shard_map/all_to_all | solution.py:122
  55.5 3.4 all-to-all-start
  59.0 9.2 %all-to-all-done = bf16[128,8,128]{0,2,1:T(8,128)(2,1)S(1)} async-done(((bf16[128,8,128]{0,2,1:T(8,128)(2,1)}), bf16[128,8,128]{0,2,1:T(8,128)(2,1)S(1)}, u32[]{:S(2)}, u32[]{:S(2)}) %all-to-all-start) | async-done | bytes 262176 | tf_op jit(solution)/shard_map/all_to_all | solution.py:119
  68.2 14.6 %all-gather.3.cloned.1.call-done = bf16[16384,128]{1,0:T(8,128)(2,1)} async-done(((bf16[1024,128]{1,0:T(8,128)(2,1)}), bf16[16384,128]{1,0:T(8,128)(2,1)}) %all-gather.3.cloned.1.call-update) | async-done | bytes 4194320 | tf_op jit(solution)/shard_map/all_gather | solution.py:140
  82.8 58.7 %all-gather.5.cloned.1.call-done = bf16[16384,128]{1,0:T(8,128)(2,1)} async-done(((bf16[1024,128]{1,0:T(8,128)(2,1)}), bf16[16384,128]{1,0:T(8,128)(2,1)}) %all-gather.5.cloned.1.call-update) | async-done | bytes 4194320 | tf_op jit(solution)/shard_map/all_gather | solution.py:141
  141.6 4.3 broadcast_in_dim.133.clone
  145.9 4.3 broadcast_in_dim.133
  150.1 89.6 %while.15 = (s32[]{:T(128)}, f32[128,128,128]{2,1,0:T(8,128)}, f32[128,128,128]{2,1,0:T(8,128)}, bf16[2,4,128,128]{3,2,1,0:T(8,128)(2,1)}, s32[2]{0:T(128)S(1)},...) while((s32[]{:T(128)}, f32[128,128,128]{2,1,0:T(8,128)}, ...), condition=%wide.region_13.15_spmd.clone, body=%wide.region_4.14_spmd.clone.sunk | while | flops 1722487296 | bytes 108011192 | solution.py:174
  152.6 3.0 gather_fusion.1
  155.6 3.0 gather_fusion
  159.7 1.7 select_reduce_fusion.10
  161.4 2.1 select_reduce_fusion.11
  163.6 2.1 multiply_reduce_fusion.3
  165.7 2.7 multiply_convert_fusion.3
  168.4 1.5 fusion.99
  169.9 1.6 convolution_add_fusion.2
  172.1 1.3 fusion.101
  173.9 2.1 add_multiply_fusion.2
  176.0 10.0 %scatter_fusion = f32[128,128,128]{2,1,0:T(8,128)} fusion(f32[128,128,128]{2,1,0:T(8,128)} %get-tuple-element.380, s32[40]{0:T(128)S(1)} %fusion.95, f32[40,128,128]{2,1,0:T(8,128)} %bitcast.149), kind=kCustom, calls=%fused_computation.2.clone.1 | custom fusion | flops 655360 | bytes 7864480 | tf_op jit(solution)/shard_map/while/body/eval_jaxpr/scatter-add | solution.py:169
  186.0 8.9 %scatter_fusion.1 = f32[128,128,128]{2,1,0:T(8,128)} fusion(f32[128,128,128]{2,1,0:T(8,128)} %get-tuple-element.381, s32[40]{0:T(128)S(1)} %fusion.95, f32[40,128,128]{2,1,0:T(8,128)S(1)} %bitcast.148), kind=kCustom, calls=%fused_computation.3.clone.1 | custom fusion | flops 655360 | bytes 7864480 | tf_op jit(solution)/shard_map/while/body/eval_jaxpr/scatter-add | solution.py:170
  197.4 3.0 gather_fusion.1
  200.4 3.0 gather_fusion
  204.5 1.7 select_reduce_fusion.10
  206.2 2.1 select_reduce_fusion.11
  208.4 2.1 multiply_reduce_fusion.3
  210.5 2.7 multiply_convert_fusion.3
  213.1 1.5 fusion.99
  214.7 1.6 convolution_add_fusion.2
  216.9 1.3 fusion.101
  218.7 2.1 add_multiply_fusion.2
  220.8 10.0 %scatter_fusion = f32[128,128,128]{2,1,0:T(8,128)} fusion(f32[128,128,128]{2,1,0:T(8,128)} %get-tuple-element.380, s32[40]{0:T(128)S(1)} %fusion.95, f32[40,128,128]{2,1,0:T(8,128)} %bitcast.149), kind=kCustom, calls=%fused_computation.2.clone.1 | custom fusion | flops 655360 | bytes 7864480 | tf_op jit(solution)/shard_map/while/body/eval_jaxpr/scatter-add | solution.py:169
  230.8 9.0 %scatter_fusion.1 = f32[128,128,128]{2,1,0:T(8,128)} fusion(f32[128,128,128]{2,1,0:T(8,128)} %get-tuple-element.381, s32[40]{0:T(128)S(1)} %fusion.95, f32[40,128,128]{2,1,0:T(8,128)S(1)} %bitcast.148), kind=kCustom, calls=%fused_computation.3.clone.1 | custom fusion | flops 655360 | bytes 7864480 | tf_op jit(solution)/shard_map/while/body/eval_jaxpr/scatter-add | solution.py:170
  239.8 6.3 %convert_element_type.33 = bf16[128,128,128]{2,1,0:T(8,128)(2,1)} convert(f32[128,128,128]{2,1,0:T(8,128)} %get-tuple-element.94) | non-fusion elementwise | flops 2097152 | bytes 12582912 | tf_op jit(solution)/shard_map/convert_element_type | solution.py:179
  246.1 6.3 %convert_element_type.34 = bf16[128,128,128]{2,1,0:T(8,128)(2,1)} convert(f32[128,128,128]{2,1,0:T(8,128)} %get-tuple-element.95) | non-fusion elementwise | flops 2097152 | bytes 12582912 | tf_op jit(solution)/shard_map/convert_element_type | solution.py:182
  252.4 17.2 %all_to_all.120 = bf16[8,128,128]{2,1,0:T(8,128)(2,1)S(1)} all-to-all(bf16[8,128,128]{2,1,0:T(8,128)(2,1)} %bitcast.13), channel_id=1, replica_groups=mesh['bend'=2,'head'=8,'blk'=16] {'head'}, dimensions={0} | all-to-all | bytes 524288 | tf_op jit(solution)/shard_map/all_to_all | solution.py:193
  269.6 57.2 %reduce-scatter.3.cloned.1.call-done = bf16[8,128,128]{2,1,0:T(8,128)(2,1)} async-done(((bf16[128,128,128]{2,1,0:T(8,128)(2,1)}), bf16[8,128,128]{2,1,0:T(8,128)(2,1)}) %reduce-scatter.3.cloned.1.call-update) | async-done | bytes 262160 | tf_op jit(solution)/shard_map/reduce_scatter | solution.py:178
  326.9 6.7 %all-to-all-start.5 = ((bf16[8,128,128]{2,1,0:T(8,128)(2,1)}), bf16[8,128,128]{2,1,0:T(8,128)(2,1)S(1)}, u32[]{:S(2)}, u32[]{:S(2)}) async-start(bf16[8,128,128]{2,1,0:T(8,128)(2,1)} %reduce-scatter.3.cloned.1.call-done), calls=%async_computation.6 | async-start | bytes 524288 | tf_op jit(solution)/shard_map/all_to_all | solution.py:194
  333.6 79.3 %reduce-scatter.5.cloned.1.call-done = bf16[8,128,128]{2,1,0:T(8,128)(2,1)} async-done(((bf16[128,128,128]{2,1,0:T(8,128)(2,1)}), bf16[8,128,128]{2,1,0:T(8,128)(2,1)}) %reduce-scatter.5.cloned.1.call-update) | async-done | bytes 262160 | tf_op jit(solution)/shard_map/reduce_scatter | solution.py:181
  412.9 6.7 %all-to-all-start.6 = ((bf16[8,128,128]{2,1,0:T(8,128)(2,1)}), bf16[8,128,128]{2,1,0:T(8,128)(2,1)S(1)}, u32[]{:S(2)}, u32[]{:S(2)}) async-start(bf16[8,128,128]{2,1,0:T(8,128)(2,1)} %reduce-scatter.5.cloned.1.call-done), calls=%async_computation.8 | async-start | bytes 524288 | tf_op jit(solution)/shard_map/all_to_all | solution.py:195
  419.9 0.9 copy.69
  421.5 7.6 %all-to-all-done.6 = bf16[8,128,128]{2,1,0:T(8,128)(2,1)S(1)} async-done(((bf16[8,128,128]{2,1,0:T(8,128)(2,1)}), bf16[8,128,128]{2,1,0:T(8,128)(2,1)S(1)}, u32[]{:S(2)}, u32[]{:S(2)}) %all-to-all-start.6) | async-done | bytes 262176 | tf_op jit(solution)/shard_map/all_to_all | solution.py:195
  (89 shorter events, 12.0 us)
Async XLA Ops:
  7.2 34.7 %copy-start.2 = (bf16[128,1024]{1,0:T(8,128)(2,1)S(1)}, bf16[128,1024]{1,0:T(8,128)(2,1)}, u32[]{:S(2)}) copy-start(bf16[128,1024]{1,0:T(8,128)(2,1)} %param.14) | copy-start | bytes 786436
  7.2 39.6 %copy-start.5 = (s32[128]{0:T(128)S(1)}, s32[128]{0:T(128)}, u32[]{:S(2)}) copy-start(s32[128]{0:T(128)} %param.16) | copy-start | bytes 1540
  7.2 39.9 %copy-start.4 = (s32[128,10]{0,1:T(8,128)S(1)}, s32[128,10]{0,1:T(8,128)}, u32[]{:S(2)}) copy-start(s32[128,10]{0,1:T(8,128)} %param.17) | copy-start | bytes 15364
  7.2 41.1 %copy-start.3 = (bf16[128,1024]{1,0:T(8,128)(2,1)S(1)}, bf16[128,1024]{1,0:T(8,128)(2,1)}, u32[]{:S(2)}) copy-start(bf16[128,1024]{1,0:T(8,128)(2,1)} %param.11) | copy-start | bytes 786436
  7.2 75.6 %all-gather.3.cloned.1.call-start = ((), (), s32[]{:S(2)}) async-start(), calls=%async_computation.9 | async-start | bytes 4456448 | tf_op jit(solution)/shard_map/all_gather | solution.py:140
  27.9 113.6 %all-gather.5.cloned.1.call-start = ((), (), s32[]{:S(2)}) async-start(), calls=%async_computation.10 | async-start | bytes 4456448 | tf_op jit(solution)/shard_map/all_gather | solution.py:141
  42.7 12.8 %all-to-all-start.2 = ((bf16[128,8,128]{0,2,1:T(8,128)(2,1)}), bf16[128,8,128]{0,2,1:T(8,128)(2,1)S(1)}, u32[]{:S(2)}, u32[]{:S(2)}) async-start(bf16[128,8,128]{0,2,1:T(8,128)(2,1)} %bitcast.7), calls=%async_computation.2 | async-start | bytes 524288 | tf_op jit(solution)/shard_map/all_to_all | solution.py:122
  55.5 12.8 %all-to-all-start = ((bf16[128,8,128]{0,2,1:T(8,128)(2,1)}), bf16[128,8,128]{0,2,1:T(8,128)(2,1)S(1)}, u32[]{:S(2)}, u32[]{:S(2)}) async-start(bf16[128,8,128]{0,2,1:T(8,128)(2,1)} %bitcast.1), calls=%async_computation | async-start | bytes 524288 | tf_op jit(solution)/shard_map/all_to_all | solution.py:119
  58.9 268.0 %reduce-scatter.3.cloned.1.call-start = ((), (), s32[]{:S(2)}) async-start(), calls=%async_computation.11 | async-start | bytes 4456448 | tf_op jit(solution)/shard_map/reduce_scatter | solution.py:178
  158.6 1.2 copy-start
  169.9 1.6 copy-start.1
  203.4 1.2 copy-start
  214.7 1.6 copy-start.1
  246.1 166.9 %reduce-scatter.5.cloned.1.call-start = ((), (), s32[]{:S(2)}) async-start(), calls=%async_computation.12 | async-start | bytes 4456448 | tf_op jit(solution)/shard_map/reduce_scatter | solution.py:181
  326.9 86.1 %all-to-all-start.5 = ((bf16[8,128,128]{2,1,0:T(8,128)(2,1)}), bf16[8,128,128]{2,1,0:T(8,128)(2,1)S(1)}, u32[]{:S(2)}, u32[]{:S(2)}) async-start(bf16[8,128,128]{2,1,0:T(8,128)(2,1)} %reduce-scatter.3.cloned.1.call-done), calls=%async_computation.6 | async-start | bytes 524288 | tf_op jit(solution)/shard_map/all_to_all | solution.py:194
  412.9 16.1 %all-to-all-start.6 = ((bf16[8,128,128]{2,1,0:T(8,128)(2,1)}), bf16[8,128,128]{2,1,0:T(8,128)(2,1)S(1)}, u32[]{:S(2)}, u32[]{:S(2)}) async-start(bf16[8,128,128]{2,1,0:T(8,128)(2,1)} %reduce-scatter.5.cloned.1.call-done), calls=%async_computation.8 | async-start | bytes 524288 | tf_op jit(solution)/shard_map/all_to_all | solution.py:195
Sparse Core Ops, SparseCore 0:
  28.1 54.7 all-gather.2
  85.3 56.2 all-gather.4
  246.2 80.6 reduce-scatter.2
  330.8 82.0 reduce-scatter.4
where the time goes:
time: 440 us; the launch traced here: 436 us
  waiting for transfers between devices  233 us (53%)
  other arithmetic  62.7 us (14%)
  blocking collectives  49 us (11%)
  local copies, waits for them, and re-layouts  29.9 us (7%)
  matrix products  25.1 us (6%)
  starting transfers between devices  20.4 us (5%)
  between operations  14.6 us (3%)
    reduce_scatter x1, waiting for transfers between devices, per_device(): lax.psum_scatter(value_sum.astype(jnp.bfloat16), 'blk', scatter_dimension...  79.3 us
    all_gather x1, waiting for transfers between devices, per_device(): lax.all_gather(value_rows, 'blk', axis=0, tiled=True)  58.7 us
    reduce_scatter x1, waiting for transfers between devices, per_device(): lax.psum_scatter(key_sum.astype(jnp.bfloat16), 'blk', scatter_dimension=0...  57.2 us
    scatter-add x2, other arithmetic, summed_step(): running[0].at[flat_slots]  20 us
    all_to_all x1, blocking collectives, per_device(): lax.all_to_all(keys_in, 'head', split_axis=1, concat_axis=0, tiled=True)  19.3 us
    scatter-add x2, other arithmetic, summed_step(): running[1].at[flat_slots]  17.9 us
    all_to_all x1, blocking collectives, per_device(): lax.all_to_all(query_grad_rows, 'head', split_axis=0, concat_axis=1, tile...  17.2 us
    all_gather x1, waiting for transfers between devices, per_device(): lax.all_gather(key_rows, 'blk', axis=0, tiled=True)  14.6 us
  transfers between devices with their start and end apart: 8, of which 7 were waited for; matrix products, arithmetic and copies ran while one was open for 3% of the time, Pallas kernels for 0%

commit v1 on v0

v1 whole, which is shorter than its diff:
```python
import functools
import math

import jax
import jax.numpy as jnp
from jax import lax
from jax.experimental import pallas as pl
from jax.experimental.pallas import tpu as pltpu
from jax.sharding import Mesh, PartitionSpec as P

HD = 64
BLK = 128
HALF = 64
NBR = 10
HEADS = 16
NSRC = 32
NX = 4
SCALE = 1.0 / math.sqrt(HD)
C2 = SCALE * math.log2(math.e)
NEG = -1e30
BF = jnp.bfloat16
F32 = jnp.float32
NT = (((1,), (1,)), ((), ()))
NN = (((1,), (0,)), ((), ()))
VMEM = pl.BlockSpec(memory_space=pltpu.VMEM)
SMEM = pl.BlockSpec(memory_space=pltpu.SMEM)
ANY = pl.BlockSpec(memory_space=pl.ANY)
PARAMS = pltpu.CompilerParams(vmem_limit_bytes=40 * 2**20)


def cost(flops, nbytes):
    return pl.CostEstimate(flops=flops, bytes_accessed=nbytes, transcendentals=0)


def tables_kernel(row_ref, col_ref, nbr_ref, nbrt_ref, out_ref):
    n = 128
    sub = lax.broadcasted_iota(jnp.int32, (n, n), 0)
    lane = lax.broadcasted_iota(jnp.int32, (n, n), 1)
    b_of = (col_ref[:, 0:1] == lane).astype(F32).astype(BF)
    adj = jnp.zeros((n, n), F32)
    adj_t = jnp.zeros((n, n), F32)
    for k in range(NBR):
        adj = adj + (nbr_ref[:, k : k + 1] == lane).astype(F32)
        adj_t = adj_t + (nbrt_ref[k : k + 1, :] == sub).astype(F32)
    eye = (sub == lane).astype(F32)
    tri = (lane <= sub).astype(F32).astype(BF)

    def stored(a):
        right = lax.dot_general(a.astype(BF), b_of, NT, preferred_element_type=F32)
        return lax.dot_general(b_of, right.astype(BF), NN, preferred_element_type=F32) - eye

    out_ref[...] = jnp.zeros_like(out_ref)
    own = lax.broadcasted_iota(jnp.int32, (1, n), 1)
    for base, a in ((0, adj_t), (16, adj)):
        m = stored(a)
        rank = lax.dot_general(tri, m.astype(BF), NN, preferred_element_type=F32)
        out_ref[base : base + 1, :] = own
        for k in range(1, NBR):
            hit = jnp.where((rank == float(k)) & (m > 0.5), sub, 0)
            out_ref[base + k : base + k + 1, :] = jnp.sum(hit, axis=0, keepdims=True)
    out_ref[32:33, :] = row_ref[1:2, :] - row_ref[0:1, :] * BLK


def make_tables(block_ids, neighbours, token_count):
    row = jnp.concatenate(
        [block_ids[None, :], jnp.broadcast_to(token_count[:1, None], (1, 128)), jnp.zeros((6, 128), jnp.int32)], 0
    )
    nbrt = jnp.concatenate([neighbours.T, jnp.full((6, 128), -1, jnp.int32)], 0)
    return pl.pallas_call(
        tables_kernel,
        out_shape=jax.ShapeDtypeStruct((40, 128), jnp.int32),
        in_specs=[VMEM] * 4,
        out_specs=VMEM,
        compiler_params=PARAMS,
        name="tables",
    )(row, block_ids[:, None], neighbours, nbrt)


def pack_rows(out, base, a_ref, b_ref, row0, limit):
    rows = pl.ds(row0, HALF)
    keep = None
    if limit is not None:
        keep = (lax.broadcasted_iota(jnp.int32, (HALF, 128), 0) + row0) < limit
    for p in range(HEADS // 2):
        a = a_ref[rows, p * 128 : p * 128 + 128]
        b = b_ref[rows, p * 128 : p * 128 + 128]
        if keep is not None:
            b = jnp.where(keep, b.astype(F32), 0.0).astype(BF)
        out[base + 2 * p] = jnp.concatenate([a[:, :HD], b[:, :HD]], axis=1)
        out[base + 2 * p + 1] = jnp.concatenate([a[:, HD:], b[:, HD:]], axis=1)


def pack_other_kernel(meta, q_ref, k_ref, v_ref, g_ref, out_ref):
    row0 = pl.multiple_of((1 - meta[0]) * HALF, HALF)
    pack_rows(out_ref, 0, k_ref, v_ref, row0, None)
    pack_rows(out_ref, HEADS, q_ref, g_ref, row0, meta[1])


def pack_mine_kernel(meta, q_ref, k_ref, v_ref, g_ref, kv_ref, qg_ref):
    c = meta[0]
    row0 = pl.multiple_of(c * HALF, HALF)
    pack_rows(kv_ref, c * HEADS, k_ref, v_ref, row0, None)
    pack_rows(qg_ref, c * HEADS, q_ref, g_ref, row0, meta[1])


def unpack_kv_kernel(meta, full_ref, other_ref, k_ref, v_ref):
    c = meta[0]
    for src, base, half in ((full_ref, c * HEADS, c), (other_ref, 0, 1 - c)):
        rows = pl.ds(pl.multiple_of(half * HALF, HALF), HALF)
        for p in range(HEADS // 2):
            a = src[base + 2 * p]
            b = src[base + 2 * p + 1]
            k_ref[rows, p * 128 : p * 128 + 128] = jnp.concatenate([a[:, :HD], b[:, :HD]], axis=1)
            v_ref[rows, p * 128 : p * 128 + 128] = jnp.concatenate([a[:, HD:], b[:, HD:]], axis=1)


def unpack_q_kernel(meta, full_ref, other_ref, q_ref):
    c = meta[0]
    h2 = HALF // 2
    for src, base, half in ((full_ref, c * HEADS, c), (other_ref, 0, 1 - c)):
        lo = pl.ds(pl.multiple_of(half * HALF, HALF), h2)
        hi = pl.ds(pl.multiple_of(half * HALF + h2, h2), h2)
        for p in range(HEADS // 2):
            a = src[base + 2 * p]
            b = src[base + 2 * p + 1]
            q_ref[lo, p * 128 : p * 128 + 128] = jnp.concatenate([a[:, :HD], b[:, :HD]], axis=1)
            q_ref[hi, p * 128 : p * 128 + 128] = jnp.concatenate([a[:, HD:], b[:, HD:]], axis=1)


def fetch(pieces, dst, sems, c, x):
    half = NSRC // 2
    left, right, far = lax.rem(x + 3, NX), lax.rem(x + 1, NX), lax.rem(x + 2, NX)
    copies = []
    for side in range(2):
        o = c if side == 0 else 1 - c
        own, r1, l1, r2, l2 = pieces[5 * side : 5 * side + 5]
        for src, to in (
            (own, dst.at[o, x]),
            (r1, dst.at[o, left]),
            (l1, dst.at[o, right]),
            (r2, dst.at[o, far, pl.ds(0, half)]),
            (l2, dst.at[o, far, pl.ds(half, half)]),
        ):
            copies.append(pltpu.make_async_copy(src, to, sems.at[len(copies)]))
    return copies


def split_rows(tile):
    lane = lax.broadcasted_iota(jnp.int32, tile.shape, 1)
    wide = tile.astype(F32)
    top = jnp.where(lane < HD, wide, 0.0).astype(BF)
    bottom = jnp.where(lane >= HD, wide, 0.0).astype(BF)
    return jnp.concatenate([top, bottom], axis=0)


def query_kernel(meta, tab, qg_ref, *refs):
    pieces, (dq_ref, stat_ref, held, tiles, scores, sems) = refs[:10], refs[10:]
    c, x = meta[0], meta[2]
    copies = fetch(pieces, held, sems, c, x)
    for copy in copies:
        copy.start()
    for copy in copies:
        copy.wait()
    lane = lax.broadcasted_iota(jnp.int32, (HALF, 128), 1)
    sub = lax.broadcasted_iota(jnp.int32, (HALF, 128), 0)
    mine = lane == sub + c * HALF

    def step(s, carry):
        t = s * NX + x
        limits = []
        for k in range(NBR):
            u = tab[k, t]
            ux, us = lax.rem(u, NX), lax.div(u, NX)
            tiles[k * BLK : k * BLK + HALF] = held[0, ux, us]
            tiles[k * BLK + HALF : (k + 1) * BLK] = held[1, ux, us]
            limits.append(tab[32, u])
        lhs = split_rows(qg_ref[s])
        top = jnp.full((HALF, 128), NEG, F32)
        for j in range(NBR // 2):
            both = lax.dot_general(lhs, tiles[j * 256 : j * 256 + 256], NT, preferred_element_type=F32)
            for i in range(2):
                k = 2 * j + i
                ok = lane < limits[k]
                if k == 0:
                    ok = ok | mine
                sc = jnp.where(ok, both[:HALF, i * 128 : i * 128 + 128], NEG)
                scores[0, k] = sc
                scores[1, k] = both[HALF:, i * 128 : i * 128 + 128]
                top = jnp.maximum(top, sc)
        top = jnp.max(top, axis=1, keepdims=True) * C2
        total = jnp.zeros((HALF, 128), F32)
        dot = jnp.zeros((HALF, 128), F32)
        for k in range(NBR):
            p = jnp.exp2(scores[0, k] * C2 - top)
            scores[0, k] = p
            total = total + p
            dot = dot + p * scores[1, k]
        total = jnp.sum(total, axis=1, keepdims=True)
        delta = jnp.sum(dot, axis=1, keepdims=True) / total
        acc = jnp.zeros((HALF, 128), F32)
        for j in range(NBR // 2):
            ds = jnp.concatenate(
                [(scores[0, k] * (scores[1, k] - delta)).astype(BF) for k in (2 * j, 2 * j + 1)], axis=1
            )
            acc = acc + lax.dot_general(ds, tiles[j * 256 : j * 256 + 256], NN, preferred_element_type=F32)
        dq = (acc * (SCALE / total)).astype(BF)
        dq_ref[s] = jnp.concatenate([dq[: HALF // 2, :HD], dq[HALF // 2 :, :HD]], axis=1)
        lse = top + jnp.log2(total)
        stat = jnp.where(lane == sub, lse, 0.0) + jnp.where(lane == sub + HALF, delta, 0.0)
        stat_ref[pl.ds(s, 1), :] = jnp.sum(stat, axis=0, keepdims=True)
        return carry

    lax.fori_loop(0, NSRC, step, 0)


def key_kernel(meta, tab, kv_ref, stats_ref, *refs):
    pieces, (dkv_ref, held, tiles, lses, deltas, sems) = refs[:10], refs[10:]
    c, x = meta[0], meta[2]
    copies = fetch(pieces, held, sems, c, x)
    for copy in copies:
        copy.start()
    lane_n = lax.broadcasted_iota(jnp.int32, (NSRC, 128), 1)
    for i in range(NX):
        a, b = stats_ref[0, i], stats_ref[1, i]
        lses[i] = jnp.where(lane_n < HALF, a, pltpu.roll(b, HALF, 1))
        deltas[i] = jnp.where(lane_n < HALF, pltpu.roll(a, HALF, 1), b)
    for copy in copies:
        copy.wait()
    lane = lax.broadcasted_iota(jnp.int32, (HALF, 128), 1)
    sub = lax.broadcasted_iota(jnp.int32, (HALF, 128), 0) + c * HALF
    mine = lane == sub

    def step(s, carry):
        t = s * NX + x
        ok = sub < tab[32, t]
        where = []
        for k in range(NBR):
            u = tab[16 + k, t]
            ux, us = lax.rem(u, NX), lax.div(u, NX)
            tiles[k * BLK : k * BLK + HALF] = held[0, ux, us]
            tiles[k * BLK + HALF : (k + 1) * BLK] = held[1, ux, us]
            where.append((ux, us))
        lhs = split_rows(kv_ref[s])
        acc = jnp.zeros((BLK, 128), F32)
        for j in range(NBR // 2):
            both = lax.dot_general(lhs, tiles[j * 256 : j * 256 + 256], NT, preferred_element_type=F32)
            ps, ds = [], []
            for i in range(2):
                k = 2 * j + i
                ux, us = where[k]
                lse = lses[ux, pl.ds(us, 1), :]
                delta = deltas[ux, pl.ds(us, 1), :]
                p = jnp.exp2(both[:HALF, i * 128 : i * 128 + 128] * C2 - lse)
                p = jnp.where((ok | mine) if k == 0 else ok, p, 0.0)
                ps.append(p.astype(BF))
                ds.append((p * (both[HALF:, i * 128 : i * 128 + 128] - delta)).astype(BF))
            weights = jnp.concatenate([jnp.concatenate(ds, axis=1), jnp.concatenate(ps, axis=1)], axis=0)
            acc = acc + lax.dot_general(
                weights, tiles[j * 256 : j * 256 + 256], NN, preferred_element_type=F32
            )
        dkv_ref[s] = jnp.where(lane < HD, acc[:HALF] * SCALE, acc[HALF:]).astype(BF)
        return carry

    lax.fori_loop(0, NSRC, step, 0)


def ring(step):
    return [(i, (i + step) % NX) for i in range(NX)]


SWAP = [(0, 1), (1, 0)]


def gather_pieces(own):
    half = NSRC // 2
    r1 = lax.ppermute(own, "x", ring(1))
    l1 = lax.ppermute(own, "x", ring(-1))
    r2 = lax.ppermute(r1[:half], "x", ring(1))
    l2 = lax.ppermute(l1[half:], "x", ring(-1))
    pieces = (own, r1, l1, r2, l2)
    return pieces + tuple(lax.ppermute(a, "bend", SWAP) for a in pieces)


def per_device(queries, keys_in, values, d_out, token_count, block_ids, neighbours):
    c = lax.axis_index("bend")
    z = lax.axis_index("z")
    y = lax.axis_index("y")
    x = lax.axis_index("x")
    t_self = z * 16 + y * 4 + x
    limit = token_count[0] - lax.dynamic_index_in_dim(block_ids, t_self, 0, False) * BLK
    meta = jnp.stack([c, limit, x, c, c, c, c, c]).astype(jnp.int32)
    other_role = (z // 4) != c

    tile = (HEADS, HALF, 128)
    sent = pl.pallas_call(
        pack_other_kernel,
        out_shape=jax.ShapeDtypeStruct((2 * HEADS, HALF, 128), BF),
        in_specs=[SMEM] + [VMEM] * 4,
        out_specs=VMEM,
        compiler_params=PARAMS,
        cost_estimate=cost(0, 2**20),
        name="pack_other",
    )(meta, queries, keys_in, values, d_out)
    came = lax.ppermute(sent, "bend", SWAP)
    kv_out, qg_out = pl.pallas_call(
        pack_mine_kernel,
        out_shape=(jax.ShapeDtypeStruct((NSRC, HALF, 128), BF),) * 2,
        in_specs=[SMEM] + [VMEM] * 4,
        out_specs=(VMEM, VMEM),
        compiler_params=PARAMS,
        cost_estimate=cost(0, 2**20),
        name="pack_mine",
    )(meta, queries, keys_in, values, d_out)
    kv_out = lax.dynamic_update_slice_in_dim(kv_out, came[:HEADS], (1 - c) * HEADS, 0)
    qg_out = lax.dynamic_update_slice_in_dim(qg_out, came[HEADS:], (1 - c) * HEADS, 0)

    tab = make_tables(block_ids, neighbours, token_count)
    tab_other = lax.ppermute(tab, "bend", SWAP)
    tab = jnp.where(other_role, tab_other, tab)

    kv = lax.all_to_all(kv_out, ("z", "y"), 0, 0, tiled=True)
    qg = lax.all_to_all(qg_out, ("z", "y"), 0, 0, tiled=True)

    kv_pieces = gather_pieces(kv)
    qg_pieces = gather_pieces(qg)

    held = pltpu.VMEM((2, NX, NSRC, HALF, 128), BF)
    tiles = pltpu.VMEM((NBR * BLK, 128), BF)
    sems = pltpu.SemaphoreType.DMA((10,))
    dq, stat = pl.pallas_call(
        query_kernel,
        out_shape=(
            jax.ShapeDtypeStruct((NSRC, HALF // 2, 128), BF),
            jax.ShapeDtypeStruct((NSRC, 128), F32),
        ),
        in_specs=[SMEM, SMEM, VMEM] + [ANY] * 10,
        out_specs=(VMEM, VMEM),
        scratch_shapes=[held, tiles, pltpu.VMEM((2, NBR, HALF, 128), F32), sems],
        compiler_params=PARAMS,
        cost_estimate=cost(4 * 10**9, 5 * 2**20),
        name="query_side",
    )(meta, tab, qg, *kv_pieces)

    pair = lax.ppermute(stat, "bend", SWAP)
    stats = jnp.where(c == 0, jnp.stack([stat, pair]), jnp.stack([pair, stat]))
    shifted = [stats] + [lax.ppermute(stats, "x", ring(k)) for k in (1, 2, 3)]
    stats = jnp.stack([lax.select_n(lax.rem(x - i + NX, NX), *shifted) for i in range(NX)], axis=1)

    dkv = pl.pallas_call(
        key_kernel,
        out_shape=jax.ShapeDtypeStruct((NSRC, HALF, 128), BF),
        in_specs=[SMEM, SMEM, VMEM, VMEM] + [ANY] * 10,
        out_specs=VMEM,
        scratch_shapes=[
            held,
            tiles,
            pltpu.VMEM((NX, NSRC, 128), F32),
            pltpu.VMEM((NX, NSRC, 128), F32),
            sems,
        ],
        compiler_params=PARAMS,
        cost_estimate=cost(4 * 10**9, 5 * 2**20),
        name="key_side",
    )(meta, tab, kv, stats, *qg_pieces)

    dq_back = lax.all_to_all(dq, ("z", "y"), 0, 0, tiled=True)
    dq_other = lax.ppermute(
        lax.dynamic_slice_in_dim(dq_back, (1 - c) * HEADS, HEADS, 0), "bend", SWAP
    )
    grad_queries = pl.pallas_call(
        unpack_q_kernel,
        out_shape=jax.ShapeDtypeStruct(queries.shape, BF),
        in_specs=[SMEM, VMEM, VMEM],
        out_specs=VMEM,
        compiler_params=PARAMS,
        cost_estimate=cost(0, 2**19),
        name="unpack_q",
    )(meta, dq_back, dq_other)

    dkv_back = lax.all_to_all(dkv, ("z", "y"), 0, 0, tiled=True)
    dkv_other = lax.ppermute(
        lax.dynamic_slice_in_dim(dkv_back, (1 - c) * HEADS, HEADS, 0), "bend", SWAP
    )
    grad_keys, grad_values = pl.pallas_call(
        unpack_kv_kernel,
        out_shape=(jax.ShapeDtypeStruct(queries.shape, BF),) * 2,
        in_specs=[SMEM, VMEM, VMEM],
        out_specs=(VMEM, VMEM),
        compiler_params=PARAMS,
        cost_estimate=cost(0, 2**20),
        name="unpack_kv",
    )(meta, dkv_back, dkv_other)
    return grad_queries, grad_keys, grad_values


def solution(mesh):
    devices = mesh.devices.reshape(2, 8, 4, 4)
    fine = Mesh(devices, ("bend", "z", "y", "x"))
    rows = P(("bend", "z", "y", "x"), None)
    return jax.shard_map(
        per_device,
        mesh=fine,
        in_specs=(rows, rows, rows, rows, P("bend"), P("bend"), P("bend", None)),
        out_specs=(rows, rows, rows),
        check_vma=False,
    )
```

time: 440 us -> 194 us (0.44)
  waiting for transfers between devices: 233 us -> 29.6 us
  other arithmetic: 62.7 us -> 0.12 us
  Pallas kernels: 0 us -> 54.6 us
  starting transfers between devices: 20.4 us -> 50.7 us
  matrix products: 25.1 us -> 0 us
  local copies, waits for them, and re-layouts: 29.9 us -> 8.34 us
  between operations: 14.6 us -> 2.12 us
    reduce_scatter x2 -> x0, waiting for transfers between devices: 137 us -> none  [the longest x1 79.3 us: per_device(): lax.psum_scatter(value_sum.astype(jnp.bfloat16), 'blk', scatter_dimension...]
    all_gather x2 -> x0, waiting for transfers between devices: 73.4 us -> none  [the longest x1 58.7 us: per_device(): lax.all_gather(value_rows, 'blk', axis=0, tiled=True)]
    pallas_call x0 -> x7, Pallas kernels: none -> 54.6 us  [the longest x1 26.7 us: per_device(): pl.pallas_call(query_kernel, out_shape=(jax.ShapeDtypeStruct((NSRC, HALF...]
    ppermute x0 -> x26, starting transfers between devices: none -> 40.7 us  [the longest x10 14 us: gather_pieces(): return pieces + tuple((lax.ppermute(a, 'bend', SWAP) for a in pieces))]
    scatter-add x4 -> x0, other arithmetic: 37.8 us -> none  [the longest x2 20 us: summed_step(): running[0].at[flat_slots]]
    dot_general x20 -> x0, matrix products: 25.1 us -> none  [the longest x4 6.21 us: attend_all(): jnp.einsum('gqnk,gqf->gnkf', prob_low, grad_head, preferred_element_type=...]
    convert_element_type x4 -> x0, other arithmetic: 17.9 us -> none  [the longest x1 6.3 us: per_device(): value_sum.astype(jnp.bfloat16)]
    gather x4 -> x0, local copies, waits for them, and re-layouts: 12 us -> none  [the longest x2 5.98 us: local_tiles(): value_tile = jnp.take(value_blocks, slot_tile, axis=0)]
  transfers between devices with their start and end apart: 8 -> 28, of which waited for: 7 -> 9; matrix products, arithmetic and copies ran while one was open for 3% -> 1% of each run, Pallas kernels for 0% -> 16%
where the time goes in v1:
time: 194 us
  Pallas kernels  54.6 us (28%)
  starting transfers between devices  50.7 us (26%)
  blocking collectives  48.4 us (25%)
  waiting for transfers between devices  29.6 us (15%)
  local copies, waits for them, and re-layouts  8.34 us (4%)
  between operations  2.12 us (1%)
    pallas_call x1, Pallas kernels, per_device(): pl.pallas_call(query_kernel, out_shape=(jax.ShapeDtypeStruct((NSRC, HALF...  26.7 us
    all_to_all x1, blocking collectives, per_device(): kv = lax.all_to_all(kv_out, ('z', 'y'), 0, 0, tiled=True)  25.8 us
    all_to_all x1, blocking collectives, per_device(): dkv_back = lax.all_to_all(dkv, ('z', 'y'), 0, 0, tiled=True)  22.6 us
    pallas_call x1, Pallas kernels, per_device(): pl.pallas_call(key_kernel, out_shape=jax.ShapeDtypeStruct((NSRC, HALF, 12...  21.9 us
    ppermute x10, starting transfers between devices, gather_pieces(): return pieces + tuple((lax.ppermute(a, 'bend', SWAP) for a in pieces))  14 us
    all_to_all x1, waiting for transfers between devices, per_device(): qg = lax.all_to_all(qg_out, ('z', 'y'), 0, 0, tiled=True)  12.5 us
    all_to_all x1, waiting for transfers between devices, per_device(): dq_back = lax.all_to_all(dq, ('z', 'y'), 0, 0, tiled=True)  8.53 us
    unnamed x13, local copies, waits for them, and re-layouts  5.14 us
  transfers between devices with their start and end apart: 28, of which 9 were waited for; matrix products, arithmetic and copies ran while one was open for 1% of the time, Pallas kernels for 16%

profile of v1, /device:TPU:1, one launch (start us, length us, event | category | flops | bytes accessed | tf_op | source)
XLA Modules:
  0.0 193.9 jit_solution(10505110204794247661)
XLA Ops:
  1.3 0.6 copy-done.5
  1.9 0.6 dynamic_slice.10
  3.3 1.0 copy-done
  4.2 0.9 copy-done.1
  5.2 0.9 copy-done.2
  6.1 0.9 copy-done.3
  7.1 0.7 pack_other.1
  7.8 3.3 %collective-permute-start.1 = (bf16[32,64,128]{2,1,0:T(8,128)(2,1)S(1)}, bf16[32,64,128]{2,1,0:T(8,128)(2,1)S(1)}, u32[]{:S(2)}, u32[]{:S(2)}) collective-permute-start(bf16[32,64,128]{2,1,0:T(8,128)(2,1)S(1)} %pack_other.1), channel_id=1, source_target_pairs={{0,128},{128,0},{1,129},{129,1},{2,130},{130,2},{3,131},{131,3},{4... | collective-permute-start | bytes 1572872 | tf_op jit(solution)/shard_map/ppermute | solution.py:304
  11.2 1.6 pack_mine.1
  12.7 0.7 slice_dynamic-update-slice_fusion
  13.5 25.8 %all_to_all.20.refs_0_.kv_ref = bf16[32,64,128]{2,1,0:T(8,128)(2,1)S(1)} all-to-all(bf16[32,64,128]{2,1,0:T(8,128)(2,1)S(1)} %get-tuple-element.15), channel_id=1, replica_groups=mesh['bend'=2,'z'=8,'y'=4,'x'=4] {'z','y'}, dimensions={0} | all-to-all | bytes 1048576 | tf_op jit(solution)/shard_map/all_to_all | solution.py:321
  39.3 5.0 %all-to-all-start = ((bf16[32,64,128]{2,1,0:T(8,128)(2,1)}), bf16[32,64,128]{2,1,0:T(8,128)(2,1)S(1)}, u32[]{:S(2)}, u32[]{:S(2)}) async-start(bf16[32,64,128]{2,1,0:T(8,128)(2,1)} %get-tuple-element.16), calls=%async_computation | async-start | bytes 1048576 | tf_op jit(solution)/shard_map/all_to_all | solution.py:322
  44.3 1.3 collective-permute-start.2
  45.6 1.5 collective-permute-start.3
  47.1 12.5 %all-to-all-done.qg_ref.refs_0_ = bf16[32,64,128]{2,1,0:T(8,128)(2,1)S(1)} async-done(((bf16[32,64,128]{2,1,0:T(8,128)(2,1)}), bf16[32,64,128]{2,1,0:T(8,128)(2,1)S(1)}, u32[]{:S(2)}, u32[]{:S(2)}) %all-to-all-start) | async-done | bytes 524320 | tf_op jit(solution)/shard_map/all_to_all | solution.py:322
  59.6 1.2 collective-permute-start.16
  60.8 1.5 collective-permute-start.17
  62.5 0.6 copy-done.4
  63.3 0.8 tables.1
  64.1 4.2 %collective-permute-start = (s32[40,128]{1,0:T(8,128)S(1)}, s32[40,128]{1,0:T(8,128)S(1)}, u32[]{:S(2)}, u32[]{:S(2)}) collective-permute-start(s32[40,128]{1,0:T(8,128)S(1)} %tables.1), channel_id=1, source_target_pairs={{0,128},{128,0},{1,129},{129,1},{2,130},{130,2},{3,131},{131,3},{4... | collective-permute-start | bytes 61448 | tf_op jit(solution)/shard_map/ppermute | solution.py:318
  68.6 0.6 collective-permute-done
  69.1 2.2 %collective-permute-start.5 = (bf16[16,64,128]{2,1,0:T(8,128)(2,1)S(1)}, bf16[16,64,128]{2,1,0:T(8,128)(2,1)}, u32[]{:S(2)}, u32[]{:S(2)}) collective-permute-start(bf16[16,64,128]{2,1,0:T(8,128)(2,1)S(1)} %slice.27), channel_id=1, source_target_pairs={{0,3},{1,0},{2,1},{3,2},{4,7},{5,4},{6,5},{7,6},{8,11},{9,8},{10,9... | collective-permute-start | bytes 786440 | tf_op jit(solution)/shard_map/ppermute | solution.py:279
  71.3 6.0 %collective-permute-start.7 = (bf16[32,64,128]{2,1,0:T(8,128)(2,1)S(1)}, bf16[32,64,128]{2,1,0:T(8,128)(2,1)}, u32[]{:S(2)}, u32[]{:S(2)}) collective-permute-start(bf16[32,64,128]{2,1,0:T(8,128)(2,1)S(1)} %collective-permute-done.2.refs_1_), channel_id=1, source_target_pairs={{0,128},{128,0},{1,129},{129,1},{2,130},{130,2},{3,131},{131,3},{4... | collective-permute-start | bytes 1572872 | tf_op jit(solution)/shard_map/ppermute | solution.py:281
  77.3 0.6 collective-permute-start.8
  78.2 2.6 %collective-permute-start.9 = (bf16[16,64,128]{2,1,0:T(8,128)(2,1)}, bf16[16,64,128]{2,1,0:T(8,128)(2,1)}, u32[]{:S(2)}, u32[]{:S(2)}) collective-permute-start(bf16[16,64,128]{2,1,0:T(8,128)(2,1)} %collective-permute-done.4.refs_3_), channel_id=1, source_target_pairs={{0,128},{128,0},{1,129},{129,1},{2,130},{130,2},{3,131},{131,3},{4... | collective-permute-start | bytes 786440 | tf_op jit(solution)/shard_map/ppermute | solution.py:281
  80.9 0.7 slice.28
  81.6 0.7 slice.29
  82.3 1.2 collective-permute-start.18
  83.5 1.7 collective-permute-start.19
  85.2 26.7 %query_side.1 = (bf16[32,32,128]{2,1,0:T(8,128)(2,1)}, f32[32,128]{1,0:T(8,128)S(1)}) custom-call(s32[8]{0:T(128)S(1)} %stack.49.meta, s32[40,128]{1,0:T(8,128)S(1)} %broadcast_select_fusion.tab, bf16[32,64,128]{2,1,0:T(8,128)(2,1)S(1)} %all-to-all-done.qg_ref.refs_0_, bf16[32,64,128]{2,1,0:T(8,128)(2,1)S(1)} %all_to_all.20.refs_0_.kv_ref, ...), custom_call_target="tpu_custom_call" | custom-call | flops 4000000000 | bytes 5242880 | tf_op jit(solution)/shard_map/query_side/pallas_call | solution.py:330
  112.0 0.9 collective-permute-start.12
  113.0 0.4 collective-permute-start.21
  114.1 0.8 collective-permute-start.14
  114.9 1.1 collective-permute-start.15
  116.0 2.4 %collective-permute-done.14 = f32[2,32,128]{2,1,0:T(8,128)S(1)} collective-permute-done((f32[2,32,128]{2,1,0:T(8,128)S(1)}, f32[2,32,128]{2,1,0:T(8,128)S(1)}, u32[]{:S(2)}, u32[]{:S(2)}) %collective-permute-start.14) | collective-permute-done | bytes 32800 | tf_op jit(solution)/shard_map/ppermute | solution.py:346
  118.4 1.3 collective-permute-start.23
  119.7 2.7 %collective-permute-done.13 = f32[2,32,128]{2,1,0:T(8,128)S(1)} collective-permute-done((f32[2,32,128]{2,1,0:T(8,128)S(1)}, f32[2,32,128]{2,1,0:T(8,128)S(1)}, u32[]{:S(2)}, u32[]{:S(2)}) %collective-permute-start.13) | collective-permute-done | bytes 32800 | tf_op jit(solution)/shard_map/ppermute | solution.py:346
  122.4 2.5 %collective-permute-start.24 = (bf16[16,64,128]{2,1,0:T(8,128)(2,1)}, bf16[16,64,128]{2,1,0:T(8,128)(2,1)S(1)}, u32[]{:S(2)}, u32[]{:S(2)}) collective-permute-start(bf16[16,64,128]{2,1,0:T(8,128)(2,1)} %collective-permute-done.19.refs_4_), channel_id=1, source_target_pairs={{0,128},{128,0},{1,129},{129,1},{2,130},{130,2},{3,131},{131,3},{4... | collective-permute-start | bytes 786440 | tf_op jit(solution)/shard_map/ppermute | solution.py:281
  124.9 1.3 collective-permute-done.24.refs_9_
  126.2 21.9 %key_side.1 = bf16[32,64,128]{2,1,0:T(8,128)(2,1)S(1)} custom-call(s32[8]{0:T(128)S(1)} %stack.49.meta, s32[40,128]{1,0:T(8,128)S(1)} %broadcast_select_fusion.tab, bf16[32,64,128]{2,1,0:T(8,128)(2,1)S(1)} %all_to_all.20.refs_0_.kv_ref, f32[2,4,32,128]{3,2,1,0:T(8,128)S(1)} %pad_maximum_fusion.stats_ref, ...), custom_call_target="tpu_custom_call" | custom-call | flops 4000000000 | bytes 5242880 | tf_op jit(solution)/shard_map/key_side/pallas_call | solution.py:349
  148.1 22.6 %all_to_all.21.full_ref = bf16[32,64,128]{2,1,0:T(8,128)(2,1)S(1)} all-to-all(bf16[32,64,128]{2,1,0:T(8,128)(2,1)S(1)} %key_side.1), channel_id=1, replica_groups=mesh['bend'=2,'z'=8,'y'=4,'x'=4] {'z','y'}, dimensions={0} | all-to-all | bytes 1048576 | tf_op jit(solution)/shard_map/all_to_all | solution.py:380
  170.7 5.0 %all-to-all-start.2 = ((bf16[32,32,128]{2,1,0:T(8,128)(2,1)}), bf16[32,32,128]{2,1,0:T(8,128)(2,1)S(1)}, u32[]{:S(2)}, u32[]{:S(2)}) async-start(bf16[32,32,128]{2,1,0:T(8,128)(2,1)} %get-tuple-element.11), calls=%async_computation.2 | async-start | bytes 524288 | tf_op jit(solution)/shard_map/all_to_all | solution.py:366
  175.8 1.8 collective-permute-start.25
  177.6 8.5 %all-to-all-done.2.full_ref = bf16[32,32,128]{2,1,0:T(8,128)(2,1)S(1)} async-done(((bf16[32,32,128]{2,1,0:T(8,128)(2,1)}), bf16[32,32,128]{2,1,0:T(8,128)(2,1)S(1)}, u32[]{:S(2)}, u32[]{:S(2)}) %all-to-all-start.2) | async-done | bytes 262176 | tf_op jit(solution)/shard_map/all_to_all | solution.py:366
  186.1 3.8 %collective-permute-start.11 = (bf16[16,32,128]{2,1,0:T(8,128)(2,1)S(1)}, bf16[16,32,128]{2,1,0:T(8,128)(2,1)S(1)}, u32[]{:S(2)}, u32[]{:S(2)}) collective-permute-start(bf16[16,32,128]{2,1,0:T(8,128)(2,1)S(1)} %constant_dynamic-slice_fusion.1), channel_id=1, source_target_pairs={{0,128},{128,0},{1,129},{129,1},{2,130},{130,2},{3,131},{131,3},{4... | collective-permute-start | bytes 393224 | tf_op jit(solution)/shard_map/ppermute | solution.py:367
  190.0 1.0 collective-permute-done.11.other_ref
  191.0 1.4 unpack_q.1
  192.4 1.5 unpack_kv.1
  (49 shorter events, 2.0 us)
Async XLA Ops:
  1.3 0.7 copy-start.5
  3.3 1.0 copy-start
  4.2 0.9 copy-start.1
  5.2 0.9 copy-start.2
  6.1 0.9 copy-start.3
  7.8 4.9 %collective-permute-start.1 = (bf16[32,64,128]{2,1,0:T(8,128)(2,1)S(1)}, bf16[32,64,128]{2,1,0:T(8,128)(2,1)S(1)}, u32[]{:S(2)}, u32[]{:S(2)}) collective-permute-start(bf16[32,64,128]{2,1,0:T(8,128)(2,1)S(1)} %pack_other.1), channel_id=1, source_target_pairs={{0,128},{128,0},{1,129},{129,1},{2,130},{130,2},{3,131},{131,3},{4... | collective-permute-start | bytes 1572872 | tf_op jit(solution)/shard_map/ppermute | solution.py:304
  39.3 20.3 %all-to-all-start = ((bf16[32,64,128]{2,1,0:T(8,128)(2,1)}), bf16[32,64,128]{2,1,0:T(8,128)(2,1)S(1)}, u32[]{:S(2)}, u32[]{:S(2)}) async-start(bf16[32,64,128]{2,1,0:T(8,128)(2,1)} %get-tuple-element.16), calls=%async_computation | async-start | bytes 1048576 | tf_op jit(solution)/shard_map/all_to_all | solution.py:322
  44.3 24.0 %collective-permute-start.2 = (bf16[32,64,128]{2,1,0:T(8,128)(2,1)S(1)}, bf16[32,64,128]{2,1,0:T(8,128)(2,1)S(1)}, u32[]{:S(2)}, u32[]{:S(2)}) collective-permute-start(bf16[32,64,128]{2,1,0:T(8,128)(2,1)S(1)} %all_to_all.20.refs_0_.kv_ref), channel_id=1, source_target_pairs={{0,1},{1,2},{2,3},{3,0},{4,5},{5,6},{6,7},{7,4},{8,9},{9,10},{10,1... | collective-permute-start | bytes 1572872 | tf_op jit(solution)/shard_map/ppermute | solution.py:276
  45.6 22.8 %collective-permute-start.3 = (bf16[32,64,128]{2,1,0:T(8,128)(2,1)S(1)}, bf16[32,64,128]{2,1,0:T(8,128)(2,1)S(1)}, u32[]{:S(2)}, u32[]{:S(2)}) collective-permute-start(bf16[32,64,128]{2,1,0:T(8,128)(2,1)S(1)} %all_to_all.20.refs_0_.kv_ref), channel_id=1, source_target_pairs={{0,3},{1,0},{2,1},{3,2},{4,7},{5,4},{6,5},{7,6},{8,11},{9,8},{10,9... | collective-permute-start | bytes 1572872 | tf_op jit(solution)/shard_map/ppermute | solution.py:277
  59.6 11.7 %collective-permute-start.16 = (bf16[32,64,128]{2,1,0:T(8,128)(2,1)S(1)}, bf16[32,64,128]{2,1,0:T(8,128)(2,1)S(1)}, u32[]{:S(2)}, u32[]{:S(2)}) collective-permute-start(bf16[32,64,128]{2,1,0:T(8,128)(2,1)S(1)} %all-to-all-done.qg_ref.refs_0_), channel_id=1, source_target_pairs={{0,1},{1,2},{2,3},{3,0},{4,5},{5,6},{6,7},{7,4},{8,9},{9,10},{10,1... | collective-permute-start | bytes 1572872 | tf_op jit(solution)/shard_map/ppermute | solution.py:276
  60.8 16.6 %collective-permute-start.17 = (bf16[32,64,128]{2,1,0:T(8,128)(2,1)S(1)}, bf16[32,64,128]{2,1,0:T(8,128)(2,1)S(1)}, u32[]{:S(2)}, u32[]{:S(2)}) collective-permute-start(bf16[32,64,128]{2,1,0:T(8,128)(2,1)S(1)} %all-to-all-done.qg_ref.refs_0_), channel_id=1, source_target_pairs={{0,3},{1,0},{2,1},{3,2},{4,7},{5,4},{6,5},{7,6},{8,11},{9,8},{10,9... | collective-permute-start | bytes 1572872 | tf_op jit(solution)/shard_map/ppermute | solution.py:277
  62.4 0.7 copy-start.4
  64.1 5.1 %collective-permute-start = (s32[40,128]{1,0:T(8,128)S(1)}, s32[40,128]{1,0:T(8,128)S(1)}, u32[]{:S(2)}, u32[]{:S(2)}) collective-permute-start(s32[40,128]{1,0:T(8,128)S(1)} %tables.1), channel_id=1, source_target_pairs={{0,128},{128,0},{1,129},{129,1},{2,130},{130,2},{3,131},{131,3},{4... | collective-permute-start | bytes 61448 | tf_op jit(solution)/shard_map/ppermute | solution.py:318
  68.3 14.0 %collective-permute-start.6 = (bf16[32,64,128]{2,1,0:T(8,128)(2,1)S(1)}, bf16[32,64,128]{2,1,0:T(8,128)(2,1)}, u32[]{:S(2)}, u32[]{:S(2)}) collective-permute-start(bf16[32,64,128]{2,1,0:T(8,128)(2,1)S(1)} %all_to_all.20.refs_0_.kv_ref), channel_id=1, source_target_pairs={{0,128},{128,0},{1,129},{129,1},{2,130},{130,2},{3,131},{131,3},{4... | collective-permute-start | bytes 1572872 | tf_op jit(solution)/shard_map/ppermute | solution.py:281
  68.4 9.8 %collective-permute-start.4 = (bf16[16,64,128]{2,1,0:T(8,128)(2,1)S(1)}, bf16[16,64,128]{2,1,0:T(8,128)(2,1)}, u32[]{:S(2)}, u32[]{:S(2)}) collective-permute-start(bf16[16,64,128]{2,1,0:T(8,128)(2,1)S(1)} %slice.26), channel_id=1, source_target_pairs={{0,1},{1,2},{2,3},{3,0},{4,5},{5,6},{6,7},{7,4},{8,9},{9,10},{10,1... | collective-permute-start | bytes 786440 | tf_op jit(solution)/shard_map/ppermute | solution.py:278
  69.1 11.7 %collective-permute-start.5 = (bf16[16,64,128]{2,1,0:T(8,128)(2,1)S(1)}, bf16[16,64,128]{2,1,0:T(8,128)(2,1)}, u32[]{:S(2)}, u32[]{:S(2)}) collective-permute-start(bf16[16,64,128]{2,1,0:T(8,128)(2,1)S(1)} %slice.27), channel_id=1, source_target_pairs={{0,3},{1,0},{2,1},{3,2},{4,7},{5,4},{6,5},{7,6},{8,11},{9,8},{10,9... | collective-permute-start | bytes 786440 | tf_op jit(solution)/shard_map/ppermute | solution.py:279
  71.3 13.9 %collective-permute-start.7 = (bf16[32,64,128]{2,1,0:T(8,128)(2,1)S(1)}, bf16[32,64,128]{2,1,0:T(8,128)(2,1)}, u32[]{:S(2)}, u32[]{:S(2)}) collective-permute-start(bf16[32,64,128]{2,1,0:T(8,128)(2,1)S(1)} %collective-permute-done.2.refs_1_), channel_id=1, source_target_pairs={{0,128},{128,0},{1,129},{129,1},{2,130},{130,2},{3,131},{131,3},{4... | collective-permute-start | bytes 1572872 | tf_op jit(solution)/shard_map/ppermute | solution.py:281
  77.3 7.9 %collective-permute-start.8 = (bf16[32,64,128]{2,1,0:T(8,128)(2,1)S(1)}, bf16[32,64,128]{2,1,0:T(8,128)(2,1)}, u32[]{:S(2)}, u32[]{:S(2)}) collective-permute-start(bf16[32,64,128]{2,1,0:T(8,128)(2,1)S(1)} %collective-permute-done.3.refs_2_), channel_id=1, source_target_pairs={{0,128},{128,0},{1,129},{129,1},{2,130},{130,2},{3,131},{131,3},{4... | collective-permute-start | bytes 1572872 | tf_op jit(solution)/shard_map/ppermute | solution.py:281
  78.2 5.3 %collective-permute-start.9 = (bf16[16,64,128]{2,1,0:T(8,128)(2,1)}, bf16[16,64,128]{2,1,0:T(8,128)(2,1)}, u32[]{:S(2)}, u32[]{:S(2)}) collective-permute-start(bf16[16,64,128]{2,1,0:T(8,128)(2,1)} %collective-permute-done.4.refs_3_), channel_id=1, source_target_pairs={{0,128},{128,0},{1,129},{129,1},{2,130},{130,2},{3,131},{131,3},{4... | collective-permute-start | bytes 786440 | tf_op jit(solution)/shard_map/ppermute | solution.py:281
  80.8 4.4 %collective-permute-start.10 = (bf16[16,64,128]{2,1,0:T(8,128)(2,1)}, bf16[16,64,128]{2,1,0:T(8,128)(2,1)}, u32[]{:S(2)}, u32[]{:S(2)}) collective-permute-start(bf16[16,64,128]{2,1,0:T(8,128)(2,1)} %collective-permute-done.5.refs_4_), channel_id=1, source_target_pairs={{0,128},{128,0},{1,129},{129,1},{2,130},{130,2},{3,131},{131,3},{4... | collective-permute-start | bytes 786440 | tf_op jit(solution)/shard_map/ppermute | solution.py:281
  82.3 31.8 %collective-permute-start.18 = (bf16[16,64,128]{2,1,0:T(8,128)(2,1)}, bf16[16,64,128]{2,1,0:T(8,128)(2,1)}, u32[]{:S(2)}, u32[]{:S(2)}) collective-permute-start(bf16[16,64,128]{2,1,0:T(8,128)(2,1)} %slice.28), channel_id=1, source_target_pairs={{0,1},{1,2},{2,3},{3,0},{4,5},{5,6},{6,7},{7,4},{8,9},{9,10},{10,1... | collective-permute-start | bytes 786440 | tf_op jit(solution)/shard_map/ppermute | solution.py:278
  83.5 31.4 %collective-permute-start.19 = (bf16[16,64,128]{2,1,0:T(8,128)(2,1)}, bf16[16,64,128]{2,1,0:T(8,128)(2,1)}, u32[]{:S(2)}, u32[]{:S(2)}) collective-permute-start(bf16[16,64,128]{2,1,0:T(8,128)(2,1)} %slice.29), channel_id=1, source_target_pairs={{0,3},{1,0},{2,1},{3,2},{4,7},{5,4},{6,5},{7,6},{8,11},{9,8},{10,9... | collective-permute-start | bytes 786440 | tf_op jit(solution)/shard_map/ppermute | solution.py:279
  112.0 1.7 collective-permute-start.12
  112.9 12.0 %collective-permute-start.20 = (bf16[32,64,128]{2,1,0:T(8,128)(2,1)S(1)}, bf16[32,64,128]{2,1,0:T(8,128)(2,1)S(1)}, u32[]{:S(2)}, u32[]{:S(2)}) collective-permute-start(bf16[32,64,128]{2,1,0:T(8,128)(2,1)S(1)} %all-to-all-done.qg_ref.refs_0_), channel_id=1, source_target_pairs={{0,128},{128,0},{1,129},{129,1},{2,130},{130,2},{3,131},{131,3},{4... | collective-permute-start | bytes 1572872 | tf_op jit(solution)/shard_map/ppermute | solution.py:281
  113.0 13.3 %collective-permute-start.21 = (bf16[32,64,128]{2,1,0:T(8,128)(2,1)S(1)}, bf16[32,64,128]{2,1,0:T(8,128)(2,1)S(1)}, u32[]{:S(2)}, u32[]{:S(2)}) collective-permute-start(bf16[32,64,128]{2,1,0:T(8,128)(2,1)S(1)} %collective-permute-done.16.refs_1_), channel_id=1, source_target_pairs={{0,128},{128,0},{1,129},{129,1},{2,130},{130,2},{3,131},{131,3},{4... | collective-permute-start | bytes 1572872 | tf_op jit(solution)/shard_map/ppermute | solution.py:281
  113.7 12.5 %collective-permute-start.22 = (bf16[32,64,128]{2,1,0:T(8,128)(2,1)S(1)}, bf16[32,64,128]{2,1,0:T(8,128)(2,1)}, u32[]{:S(2)}, u32[]{:S(2)}) collective-permute-start(bf16[32,64,128]{2,1,0:T(8,128)(2,1)S(1)} %collective-permute-done.17.refs_2_), channel_id=1, source_target_pairs={{0,128},{128,0},{1,129},{129,1},{2,130},{130,2},{3,131},{131,3},{4... | collective-permute-start | bytes 1572872 | tf_op jit(solution)/shard_map/ppermute | solution.py:281
  114.1 4.4 %collective-permute-start.14 = (f32[2,32,128]{2,1,0:T(8,128)S(1)}, f32[2,32,128]{2,1,0:T(8,128)S(1)}, u32[]{:S(2)}, u32[]{:S(2)}) collective-permute-start(f32[2,32,128]{2,1,0:T(8,128)S(1)} %maximum_select_fusion), channel_id=1, source_target_pairs={{0,2},{1,3},{2,0},{3,1},{4,6},{5,7},{6,4},{7,5},{8,10},{9,11},{10,... | collective-permute-start | bytes 98312 | tf_op jit(solution)/shard_map/ppermute | solution.py:346
  114.9 3.5 %collective-permute-start.15 = (f32[2,32,128]{2,1,0:T(8,128)S(1)}, f32[2,32,128]{2,1,0:T(8,128)S(1)}, u32[]{:S(2)}, u32[]{:S(2)}) collective-permute-start(f32[2,32,128]{2,1,0:T(8,128)S(1)} %maximum_select_fusion), channel_id=1, source_target_pairs={{0,3},{1,0},{2,1},{3,2},{4,7},{5,4},{6,5},{7,6},{8,11},{9,8},{10,9... | collective-permute-start | bytes 98312 | tf_op jit(solution)/shard_map/ppermute | solution.py:346
  118.4 4.0 %collective-permute-start.13 = (f32[2,32,128]{2,1,0:T(8,128)S(1)}, f32[2,32,128]{2,1,0:T(8,128)S(1)}, u32[]{:S(2)}, u32[]{:S(2)}) collective-permute-start(f32[2,32,128]{2,1,0:T(8,128)S(1)} %maximum_select_fusion), channel_id=1, source_target_pairs={{0,1},{1,2},{2,3},{3,0},{4,5},{5,6},{6,7},{7,4},{8,9},{9,10},{10,1... | collective-permute-start | bytes 98312 | tf_op jit(solution)/shard_map/ppermute | solution.py:346
  118.4 6.5 %collective-permute-start.23 = (bf16[16,64,128]{2,1,0:T(8,128)(2,1)}, bf16[16,64,128]{2,1,0:T(8,128)(2,1)S(1)}, u32[]{:S(2)}, u32[]{:S(2)}) collective-permute-start(bf16[16,64,128]{2,1,0:T(8,128)(2,1)} %collective-permute-done.18.refs_3_), channel_id=1, source_target_pairs={{0,128},{128,0},{1,129},{129,1},{2,130},{130,2},{3,131},{131,3},{4... | collective-permute-start | bytes 786440 | tf_op jit(solution)/shard_map/ppermute | solution.py:281
  122.4 3.8 %collective-permute-start.24 = (bf16[16,64,128]{2,1,0:T(8,128)(2,1)}, bf16[16,64,128]{2,1,0:T(8,128)(2,1)S(1)}, u32[]{:S(2)}, u32[]{:S(2)}) collective-permute-start(bf16[16,64,128]{2,1,0:T(8,128)(2,1)} %collective-permute-done.19.refs_4_), channel_id=1, source_target_pairs={{0,128},{128,0},{1,129},{129,1},{2,130},{130,2},{3,131},{131,3},{4... | collective-permute-start | bytes 786440 | tf_op jit(solution)/shard_map/ppermute | solution.py:281
  170.7 15.4 %all-to-all-start.2 = ((bf16[32,32,128]{2,1,0:T(8,128)(2,1)}), bf16[32,32,128]{2,1,0:T(8,128)(2,1)S(1)}, u32[]{:S(2)}, u32[]{:S(2)}) async-start(bf16[32,32,128]{2,1,0:T(8,128)(2,1)} %get-tuple-element.11), calls=%async_computation.2 | async-start | bytes 524288 | tf_op jit(solution)/shard_map/all_to_all | solution.py:366
  175.8 16.6 %collective-permute-start.25 = (bf16[16,64,128]{2,1,0:T(8,128)(2,1)S(1)}, bf16[16,64,128]{2,1,0:T(8,128)(2,1)S(1)}, u32[]{:S(2)}, u32[]{:S(2)}) collective-permute-start(bf16[16,64,128]{2,1,0:T(8,128)(2,1)S(1)} %constant_dynamic-slice_fusion), channel_id=1, source_target_pairs={{0,128},{128,0},{1,129},{129,1},{2,130},{130,2},{3,131},{131,3},{4... | collective-permute-start | bytes 786440 | tf_op jit(solution)/shard_map/ppermute | solution.py:381
  186.1 4.8 %collective-permute-start.11 = (bf16[16,32,128]{2,1,0:T(8,128)(2,1)S(1)}, bf16[16,32,128]{2,1,0:T(8,128)(2,1)S(1)}, u32[]{:S(2)}, u32[]{:S(2)}) collective-permute-start(bf16[16,32,128]{2,1,0:T(8,128)(2,1)S(1)} %constant_dynamic-slice_fusion.1), channel_id=1, source_target_pairs={{0,128},{128,0},{1,129},{129,1},{2,130},{130,2},{3,131},{131,3},{4... | collective-permute-start | bytes 393224 | tf_op jit(solution)/shard_map/ppermute | solution.py:367

commit v2 on v1

v2 whole, which is shorter than its diff:
```python
import functools
import math

import jax
import jax.numpy as jnp
from jax import lax
from jax.experimental import pallas as pl
from jax.experimental.pallas import tpu as pltpu
from jax.sharding import Mesh, PartitionSpec as P

HD = 64
BLK = 128
HALF = 64
NBR = 10
HEADS = 16
NSRC = 32
NX = 4
UNROLL = 8
SCALE = 1.0 / math.sqrt(HD)
C2 = SCALE * math.log2(math.e)
NEG = -1e30
BF = jnp.bfloat16
F32 = jnp.float32
NT = (((1,), (1,)), ((), ()))
NN = (((1,), (0,)), ((), ()))
VMEM = pl.BlockSpec(memory_space=pltpu.VMEM)
SMEM = pl.BlockSpec(memory_space=pltpu.SMEM)
ANY = pl.BlockSpec(memory_space=pl.ANY)
HBM = pl.BlockSpec(memory_space=pltpu.HBM)
PARAMS = pltpu.CompilerParams(vmem_limit_bytes=60 * 2**20)
SMALL = pltpu.CompilerParams(vmem_limit_bytes=16 * 2**20)


def cost(flops, nbytes):
    return pl.CostEstimate(flops=flops, bytes_accessed=nbytes, transcendentals=0)


def tables_kernel(row_ref, col_ref, nbr_ref, nbrt_ref, out_ref):
    n = 128
    sub = lax.broadcasted_iota(jnp.int32, (n, n), 0)
    lane = lax.broadcasted_iota(jnp.int32, (n, n), 1)
    b_of = (col_ref[:, 0:1] == lane).astype(F32).astype(BF)
    adj = jnp.zeros((n, n), F32)
    adj_t = jnp.zeros((n, n), F32)
    for k in range(NBR):
        adj = adj + (nbr_ref[:, k : k + 1] == lane).astype(F32)
        adj_t = adj_t + (nbrt_ref[k : k + 1, :] == sub).astype(F32)
    eye = (sub == lane).astype(F32)
    tri = (lane <= sub).astype(F32).astype(BF)

    def stored(a):
        right = lax.dot_general(a.astype(BF), b_of, NT, preferred_element_type=F32)
        return lax.dot_general(b_of, right.astype(BF), NN, preferred_element_type=F32) - eye

    out_ref[...] = jnp.zeros_like(out_ref)
    own = lax.broadcasted_iota(jnp.int32, (1, n), 1)
    for base, a in ((0, adj_t), (16, adj)):
        m = stored(a)
        rank = lax.dot_general(tri, m.astype(BF), NN, preferred_element_type=F32)
        out_ref[base : base + 1, :] = own
        for k in range(1, NBR):
            hit = jnp.where((rank == float(k)) & (m > 0.5), sub, 0)
            out_ref[base + k : base + k + 1, :] = jnp.sum(hit, axis=0, keepdims=True)
    out_ref[32:33, :] = row_ref[1:2, :] - row_ref[0:1, :] * BLK


def make_tables(block_ids, neighbours, token_count):
    row = jnp.concatenate(
        [block_ids[None, :], jnp.broadcast_to(token_count[:1, None], (1, 128)), jnp.zeros((6, 128), jnp.int32)], 0
    )
    nbrt = jnp.concatenate([neighbours.T, jnp.full((6, 128), -1, jnp.int32)], 0)
    return pl.pallas_call(
        tables_kernel,
        out_shape=jax.ShapeDtypeStruct((40, 128), jnp.int32),
        in_specs=[VMEM] * 4,
        out_specs=VMEM,
        compiler_params=PARAMS,
        name="tables",
    )(row, block_ids[:, None], neighbours, nbrt)


def pack_half(half, ids, count, arrays, bufs, sems, kv_out, qg_out, base):
    row0 = pl.multiple_of(half * HALF, HALF)
    copies = [
        pltpu.make_async_copy(arrays[i].at[pl.ds(row0, HALF)], bufs.at[i], sems.at[i]) for i in (1, 2, 0, 3)
    ]
    for copy in copies:
        copy.start()
    t = lax.axis_index("z") * 16 + lax.axis_index("y") * 4 + lax.axis_index("x")
    limit = count[0] - ids[t] * BLK - row0
    keep = lax.broadcasted_iota(jnp.int32, (HALF, 128), 0) < limit
    for copy in copies:
        copy.wait()
    for p in range(HEADS // 2):
        cols = slice(p * 128, p * 128 + 128)
        q, k, v, g = (bufs[i, :, cols] for i in range(4))
        g = jnp.where(keep, g.astype(F32), 0.0).astype(BF)
        for out, m, n in ((kv_out, k, v), (qg_out, q, g)):
            out[base + 2 * p] = jnp.concatenate([m[:, :HD], n[:, :HD]], axis=1)
            out[base + 2 * p + 1] = jnp.concatenate([m[:, HD:], n[:, HD:]], axis=1)


def pack_other_kernel(ids, count, q_ref, k_ref, v_ref, g_ref, out_ref, bufs, sems):
    half = 1 - lax.axis_index("bend")
    kv_ref, qg_ref = out_ref.at[pl.ds(0, HEADS)], out_ref.at[pl.ds(HEADS, HEADS)]
    pack_half(half, ids, count, (q_ref, k_ref, v_ref, g_ref), bufs, sems, kv_ref, qg_ref, 0)


def pack_mine_kernel(ids, count, q_ref, k_ref, v_ref, g_ref, kv_ref, qg_ref, bufs, sems):
    half = lax.axis_index("bend")
    pack_half(half, ids, count, (q_ref, k_ref, v_ref, g_ref), bufs, sems, kv_ref, qg_ref, half * HEADS)


def unpack_kernel(full_ref, other_ref, q_ref, k_ref, v_ref):
    c = lax.axis_index("bend")
    h2 = HALF // 2
    for src, base, half in ((full_ref, c * HEADS, c), (other_ref, 0, 1 - c)):
        rows = pl.ds(pl.multiple_of(half * HALF, HALF), HALF)
        lo = pl.ds(pl.multiple_of(half * HALF, HALF), h2)
        hi = pl.ds(pl.multiple_of(half * HALF + h2, h2), h2)
        for p in range(HEADS // 2):
            cols = slice(p * 128, p * 128 + 128)
            a, b = src[base + 2 * p, :HALF], src[base + 2 * p + 1, :HALF]
            k_ref[rows, cols] = jnp.concatenate([a[:, :HD], b[:, :HD]], axis=1)
            v_ref[rows, cols] = jnp.concatenate([a[:, HD:], b[:, HD:]], axis=1)
            a, b = src[base + 2 * p, HALF:], src[base + 2 * p + 1, HALF:]
            q_ref[lo, cols] = jnp.concatenate([a[:, :HD], b[:, :HD]], axis=1)
            q_ref[hi, cols] = jnp.concatenate([a[:, HD:], b[:, HD:]], axis=1)


def fetch(pieces, dst, sems, c, x):
    half = NSRC // 2
    left, right, far = lax.rem(x + 3, NX), lax.rem(x + 1, NX), lax.rem(x + 2, NX)
    copies = []
    for side in range(2):
        o = c if side == 0 else 1 - c
        own, r1, l1, r2, l2 = pieces[5 * side : 5 * side + 5]
        for src, to in (
            (own, dst.at[o, x]),
            (r1, dst.at[o, left]),
            (l1, dst.at[o, right]),
            (r2, dst.at[o, far, pl.ds(0, half)]),
            (l2, dst.at[o, far, pl.ds(half, half)]),
        ):
            copies.append(pltpu.make_async_copy(src, to, sems.at[len(copies)]))
    return copies


def split_rows(tile):
    lane = lax.broadcasted_iota(jnp.int32, (HALF, 128), 1)
    low = (lane < HD).astype(F32).astype(BF)
    return jnp.concatenate([tile * low, tile * (1 - low)], axis=0)


def places(tab, base, t):
    out = []
    for k in range(NBR):
        u = tab[base + k, t]
        out.append((lax.rem(u, NX), lax.div(u, NX), u))
    return out


def load_pieces(pieces, held, sems):
    c, x = lax.axis_index("bend"), lax.axis_index("x")
    copies = fetch(pieces, held, sems, c, x)
    for copy in copies:
        copy.start()
    return c, x, copies


def gather_tiles(held, tiles, u, where):
    for k in range(NBR):
        for h in range(2):
            tiles[u, (2 * k + h) * HALF : (2 * k + h + 1) * HALF] = held[h, where[k][0], where[k][1]]


def skewed(stages):
    for r in range(UNROLL + len(stages) - 1):
        for n in range(len(stages)):
            if 0 <= r - n < UNROLL:
                stages[n](r - n)


def query_kernel(tab, qg_ref, *refs):
    pieces, (dq_ref, row_ref, held, tiles, scores, grads, sems) = refs[:10], refs[10:]
    c, x, copies = load_pieces(pieces, held, sems)
    for copy in copies:
        copy.wait()
    lane = lax.broadcasted_iota(jnp.int32, (HALF, 128), 1)
    sub = lax.broadcasted_iota(jnp.int32, (HALF, 128), 0)
    lane_row = lax.broadcasted_iota(jnp.int32, (1, 128), 1)
    mine = lane == sub + c * HALF

    def step(i, carry):
        ss = [i * UNROLL + u for u in range(UNROLL)]
        where = [places(tab, 0, s * NX + x) for s in ss]
        tops, totals = {}, {}

        def products(u):
            gather_tiles(held, tiles, u, where[u])
            lhs = split_rows(qg_ref[ss[u]])
            top = jnp.full((HALF, 128), NEG, F32)
            for j in range(NBR // 2):
                both = lax.dot_general(
                    lhs, tiles[u, j * 256 : j * 256 + 256], NT, preferred_element_type=F32
                )
                for i in range(2):
                    k = 2 * j + i
                    sc = both[:HALF, i * 128 : i * 128 + 128] * C2
                    limit = tab[32, where[u][k][2]]
                    if k == 0:
                        sc = jnp.where((lane < limit) | mine, sc, NEG)
                    else:
                        sc = sc + jnp.where(lane_row < limit, 0.0, NEG)
                    scores[u, 0, k] = sc
                    scores[u, 1, k] = both[HALF:, i * 128 : i * 128 + 128]
                    top = jnp.maximum(top, sc)
            tops[u] = jnp.max(top, axis=1, keepdims=True)

        def weights(u):
            total = jnp.zeros((HALF, 128), F32)
            dot = jnp.zeros((HALF, 128), F32)
            for k in range(NBR):
                p = jnp.exp2(scores[u, 0, k] - tops[u])
                scores[u, 0, k] = p
                total = total + p
                dot = dot + p * scores[u, 1, k]
            total = jnp.sum(total, axis=1, keepdims=True)
            totals[u] = total, jnp.sum(dot, axis=1, keepdims=True) / total

        def gradient(u):
            total, delta = totals[u]
            for k in range(NBR):
                grads[u, :, k * 128 : k * 128 + 128] = (scores[u, 0, k] * (scores[u, 1, k] - delta)).astype(BF)
            acc = lax.dot_general(grads[u], tiles[u], NN, preferred_element_type=F32)
            dq = (acc * (SCALE / total)).astype(BF)
            dq_ref[ss[u]] = jnp.concatenate([dq[: HALF // 2, :HD], dq[HALF // 2 :, :HD]], axis=1)
            lse = tops[u] + jnp.log2(total)
            row = jnp.where(lane == sub, lse, 0.0) + jnp.where(lane == sub + HALF, delta, 0.0)
            row = jnp.sum(row, axis=0, keepdims=True)
            for i in range(2 * NX):
                row_ref[i, pl.ds(ss[u], 1), :] = row

        skewed((products, weights, gradient))
        return carry

    lax.fori_loop(0, NSRC // UNROLL, step, 0)


def key_kernel(tab, kv_ref, dq_ref, stats_ref, *refs):
    pieces, (out_ref, held, tiles, scores, pairs, lses, deltas, sems) = refs[:10], refs[10:]
    c, x, copies = load_pieces(pieces, held, sems)
    lane_n = lax.broadcasted_iota(jnp.int32, (NSRC, 128), 1)
    for i in range(NX):
        a, b = stats_ref[i], stats_ref[NX + i]
        lse = jnp.where(lane_n < HALF, a, pltpu.roll(b, HALF, 1))
        delta = jnp.where(lane_n < HALF, pltpu.roll(a, HALF, 1), b)
        for s in range(NSRC):
            lses[i, s] = jnp.broadcast_to(lse[s : s + 1], (8, 128))
            deltas[i, s] = jnp.broadcast_to(delta[s : s + 1], (8, 128))
    out_ref[:, HALF:] = dq_ref[...]
    for copy in copies:
        copy.wait()
    lane = lax.broadcasted_iota(jnp.int32, (HALF, 128), 1)
    sub = lax.broadcasted_iota(jnp.int32, (HALF, 128), 0) + c * HALF
    mine = lane == sub

    def step(i, carry):
        ss = [i * UNROLL + u for u in range(UNROLL)]
        where = [places(tab, 16, s * NX + x) for s in ss]

        def products(u):
            gather_tiles(held, tiles, u, where[u])
            lhs = split_rows(kv_ref[ss[u]])
            for j in range(NBR // 2):
                both = lax.dot_general(
                    lhs, tiles[u, j * 256 : j * 256 + 256], NT, preferred_element_type=F32
                )
                for i in range(2):
                    k = 2 * j + i
                    scores[u, 0, k] = both[:HALF, i * 128 : i * 128 + 128]
                    scores[u, 1, k] = both[HALF:, i * 128 : i * 128 + 128]

        def weights(u):
            ok = sub < tab[32, ss[u] * NX + x]
            for k in range(NBR):
                ux, us, _ = where[u][k]
                lse = jnp.concatenate([lses[ux, us]] * 8, axis=0)
                delta = jnp.concatenate([deltas[ux, us]] * 8, axis=0)
                p = jnp.exp2(scores[u, 0, k] * C2 - lse)
                p = jnp.where((ok | mine) if k == 0 else ok, p, 0.0)
                pairs[u, :HALF, k * 128 : k * 128 + 128] = (p * (scores[u, 1, k] - delta)).astype(BF)
                pairs[u, HALF:, k * 128 : k * 128 + 128] = p.astype(BF)

        def gradient(u):
            acc = lax.dot_general(pairs[u], tiles[u], NN, preferred_element_type=F32)
            out_ref[ss[u], :HALF] = jnp.where(lane < HD, acc[:HALF] * SCALE, acc[HALF:]).astype(BF)

        skewed((products, weights, gradient))
        return carry

    lax.fori_loop(0, NSRC // UNROLL, step, 0)


def ring(step):
    return [(i, (i + step) % NX) for i in range(NX)]


SWAP = [(0, 1), (1, 0)]


def swap(a):
    return lax.ppermute(a, "bend", SWAP)


def first_step(own):
    return lax.ppermute(own, "x", ring(1)), lax.ppermute(own, "x", ring(-1))


def second_step(own, r1, l1):
    half = NSRC // 2
    r2 = lax.ppermute(r1[:half], "x", ring(1))
    l2 = lax.ppermute(l1[half:], "x", ring(-1))
    return own, r1, l1, r2, l2


def per_device(queries, keys_in, values, d_out, token_count, block_ids, neighbours):
    c = lax.axis_index("bend")
    other_role = (lax.axis_index("z") // 4) != c

    bufs = [pltpu.VMEM((4, HALF, HEADS * HD), BF), pltpu.SemaphoreType.DMA((4,))]
    sent = pl.pallas_call(
        pack_other_kernel,
        out_shape=jax.ShapeDtypeStruct((2 * HEADS, HALF, 128), BF),
        in_specs=[SMEM] * 2 + [HBM] * 4,
        out_specs=VMEM,
        scratch_shapes=bufs,
        compiler_params=PARAMS,
        cost_estimate=cost(0, 2**20),
        name="pack_other",
    )(block_ids, token_count, queries, keys_in, values, d_out)
    came = swap(sent)
    kv_out, qg_out = pl.pallas_call(
        pack_mine_kernel,
        out_shape=(jax.ShapeDtypeStruct((NSRC, HALF, 128), BF),) * 2,
        in_specs=[SMEM] * 2 + [HBM] * 4,
        out_specs=(VMEM, VMEM),
        scratch_shapes=bufs,
        compiler_params=PARAMS,
        cost_estimate=cost(0, 2**20),
        name="pack_mine",
    )(block_ids, token_count, queries, keys_in, values, d_out)
    theirs = (1 - c) * HEADS
    kv_out = lax.dynamic_update_slice_in_dim(kv_out, came[:HEADS], theirs, 0)
    qg_out = lax.dynamic_update_slice_in_dim(qg_out, came[HEADS:], theirs, 0)
    kv = lax.all_to_all(kv_out, ("z", "y"), 0, 0, tiled=True)
    kv, qg_out = lax.optimization_barrier((kv, qg_out))
    qg = lax.all_to_all(qg_out, ("z", "y"), 0, 0, tiled=True)

    tab = make_tables(block_ids, neighbours, token_count)
    tab = jnp.where(other_role, swap(tab), tab)

    r1, l1, tab = lax.optimization_barrier(first_step(kv) + (tab,))
    kv_pieces = second_step(kv, r1, l1)
    kv_pieces += tuple(swap(a) for a in kv_pieces)
    late = lax.optimization_barrier((qg,) + kv_pieces[3:5])
    qg_first = first_step(late[0])

    held = pltpu.VMEM((2, NX, NSRC, HALF, 128), BF)
    tiles = pltpu.VMEM((UNROLL, NBR * BLK, 128), BF)
    scores = pltpu.VMEM((UNROLL, 2, NBR, HALF, 128), F32)
    stat = pltpu.VMEM((NX, NSRC, 8, 128), F32)
    sems = pltpu.SemaphoreType.DMA((10,))
    dq, rows = pl.pallas_call(
        query_kernel,
        out_shape=(
            jax.ShapeDtypeStruct((NSRC, HALF // 2, 128), BF),
            jax.ShapeDtypeStruct((2 * NX, NSRC, 128), F32),
        ),
        in_specs=[SMEM, VMEM] + [ANY] * 10,
        out_specs=(VMEM, VMEM),
        scratch_shapes=[held, tiles, scores, pltpu.VMEM((UNROLL, HALF, NBR * BLK), BF), sems],
        compiler_params=PARAMS,
        cost_estimate=cost(6 * 10**9, 20 * 2**20),
        name="query_side",
    )(tab, qg, *kv_pieces)
    stats = lax.all_to_all(rows, ("bend", "x"), 0, 0, tiled=True)

    qg_first = lax.optimization_barrier(qg_first + (rows,))[:2]
    qg_pieces = second_step(qg, *qg_first)
    *qg_last, stats = lax.optimization_barrier(qg_pieces[3:] + (stats,))
    qg_pieces = qg_pieces[:3] + tuple(qg_last)
    qg_pieces += tuple(swap(a) for a in qg_pieces)

    grads = pl.pallas_call(
        key_kernel,
        out_shape=jax.ShapeDtypeStruct((NSRC, HALF + HALF // 2, 128), BF),
        in_specs=[SMEM, VMEM, VMEM, VMEM] + [ANY] * 10,
        out_specs=VMEM,
        scratch_shapes=[held, tiles, scores, pltpu.VMEM((UNROLL, BLK, NBR * BLK), BF), stat, stat, sems],
        compiler_params=PARAMS,
        cost_estimate=cost(6 * 10**9, 20 * 2**20),
        name="key_side",
    )(tab, kv, dq, stats, *qg_pieces)

    back = lax.all_to_all(grads, ("z", "y"), 0, 0, tiled=True)
    other = swap(lax.dynamic_slice_in_dim(back, theirs, HEADS, 0))
    return pl.pallas_call(
        unpack_kernel,
        out_shape=(jax.ShapeDtypeStruct(queries.shape, BF),) * 3,
        in_specs=[VMEM] * 2,
        out_specs=(VMEM, VMEM, VMEM),
        compiler_params=SMALL,
        cost_estimate=cost(0, 2**20),
        name="unpack",
    )(back, other)


def solution(mesh):
    devices = mesh.devices.reshape(2, 8, 4, 4)
    fine = Mesh(devices, ("bend", "z", "y", "x"))
    rows = P(("bend", "z", "y", "x"), None)
    return jax.shard_map(
        per_device,
        mesh=fine,
        in_specs=(rows, rows, rows, rows, P("bend"), P("bend"), P("bend", None)),
        out_specs=(rows, rows, rows),
        check_vma=False,
    )
```

time: 194 us -> 146 us (0.75)
  starting transfers between devices: 50.7 us -> 28.1 us
  Pallas kernels: 54.6 us -> 33.1 us
  waiting for transfers between devices: 29.6 us -> 9.4 us
  blocking collectives: 48.4 us -> 65.4 us
  local copies, waits for them, and re-layouts: 8.34 us -> 6.24 us
    ppermute x26 -> x21, starting transfers between devices: 40.7 us -> 23.2 us  [the longest x13 12.7 us: swap(): return lax.ppermute(a, 'bend', SWAP)]
    all_to_all x1 -> x2, blocking collectives: 22.6 us -> 39.2 us  [the longest x1 30.9 us: per_device(): back = lax.all_to_all(grads, ('z', 'y'), 0, 0, tiled=True)]
    pallas_call x1, Pallas kernels: 26.7 us -> 12.9 us  [per_device(): pl.pallas_call(query_kernel, out_shape=(jax.ShapeDtypeStruct((NSRC, HALF...]
    pallas_call x3 -> x2, Pallas kernels: 24.8 us -> 12.1 us  [the longest x1 11 us: per_device(): pl.pallas_call(key_kernel, out_shape=jax.ShapeDtypeStruct((NSRC, HALF + H...]
    all_to_all x1, waiting for transfers between devices: 12.5 us -> 0.01 us  [per_device(): qg = lax.all_to_all(qg_out, ('z', 'y'), 0, 0, tiled=True)]
    all_to_all x1 -> x0, waiting for transfers between devices: 8.53 us -> none  [per_device(): dq_back = lax.all_to_all(dq, ('z', 'y'), 0, 0, tiled=True)]
    all_to_all x1 -> x0, starting transfers between devices: 5.01 us -> none  [per_device(): dq_back = lax.all_to_all(dq, ('z', 'y'), 0, 0, tiled=True)]
    pallas_call x1, Pallas kernels: 0.75 us -> 2.85 us  [per_device(): pl.pallas_call(pack_other_kernel, out_shape=jax.ShapeDtypeStruct((2 * HEA...]
  transfers between devices with their start and end apart: 28 -> 22, of which waited for: 9 -> 6; matrix products, arithmetic and copies ran while one was open for 1% -> 2% of each run, Pallas kernels for 16% -> 13%
where the time goes in v2:
time: 146 us; the launch traced here: 145 us
  blocking collectives  65.4 us (45%)
  Pallas kernels  33.1 us (23%)
  starting transfers between devices  28.1 us (19%)
  waiting for transfers between devices  9.4 us (6%)
  local copies, waits for them, and re-layouts  6.24 us (4%)
  between operations  1.59 us (1%)
    all_to_all x1, blocking collectives, per_device(): back = lax.all_to_all(grads, ('z', 'y'), 0, 0, tiled=True)  30.9 us
    all_to_all x1, blocking collectives, per_device(): kv = lax.all_to_all(kv_out, ('z', 'y'), 0, 0, tiled=True)  26.3 us
    pallas_call x1, Pallas kernels, per_device(): pl.pallas_call(query_kernel, out_shape=(jax.ShapeDtypeStruct((NSRC, HALF...  12.9 us
    ppermute x13, starting transfers between devices, swap(): return lax.ppermute(a, 'bend', SWAP)  12.7 us
    pallas_call x1, Pallas kernels, per_device(): pl.pallas_call(key_kernel, out_shape=jax.ShapeDtypeStruct((NSRC, HALF + H...  11 us
    all_to_all x1, blocking collectives, per_device(): stats = lax.all_to_all(rows, ('bend', 'x'), 0, 0, tiled=True)  8.3 us
    ppermute x2, starting transfers between devices, second_step(): l2 = lax.ppermute(l1[half:], 'x', ring(-1))  5.47 us
    ppermute x2, waiting for transfers between devices, second_step(): r2 = lax.ppermute(r1[:half], 'x', ring(1))  5.47 us
  transfers between devices with their start and end apart: 22, of which 6 were waited for; matrix products, arithmetic and copies ran while one was open for 2% of the time, Pallas kernels for 13%

profile of v2, /device:TPU:1, one launch (start us, length us, event | category | flops | bytes accessed | tf_op | source)
XLA Modules:
  0.0 145.2 jit_solution(13946533649772671459)
XLA Ops:
  1.3 2.8 %pack_other.1 = bf16[32,64,128]{2,1,0:T(8,128)(2,1)} custom-call(s32[128]{0:T(128)} %ids.3, s32[1]{0:T(128)S(6)} %copy.14.count, bf16[128,1024]{1,0:T(8,128)(2,1)} %q_ref.3, bf16[128,1024]{1,0:T(8,128)(2,1)} %k_ref.3, bf16[128,1024]{1,0:T(8,128)(2,1)} %v_ref.3, bf16[128,1024]{1,0:T(8,128)(2,1)} %g_ref.3), custom_call_target="tpu_custom_call" | custom-call | bytes 1048576 | tf_op jit(solution)/shard_map/pack_other/pallas_call | solution.py:332
  4.1 3.3 %collective-permute-start = (bf16[32,64,128]{2,1,0:T(8,128)(2,1)}, bf16[32,64,128]{2,1,0:T(8,128)(2,1)S(1)}, u32[]{:S(2)}, u32[]{:S(2)}) collective-permute-start(bf16[32,64,128]{2,1,0:T(8,128)(2,1)} %pack_other.1), channel_id=1, source_target_pairs={{0,128},{128,0},{1,129},{129,1},{2,130},{130,2},{3,131},{131,3},{4... | collective-permute-start | bytes 1572872 | tf_op jit(solution)/shard_map/ppermute | solution.py:313
  7.5 3.0 %pack_mine.1 = (bf16[32,64,128]{2,1,0:T(8,128)(2,1)}, bf16[32,64,128]{2,1,0:T(8,128)(2,1)}) custom-call(s32[128]{0:T(128)} %ids.3, s32[1]{0:T(128)S(6)} %copy.14.count, bf16[128,1024]{1,0:T(8,128)(2,1)} %q_ref.3, bf16[128,1024]{1,0:T(8,128)(2,1)} %k_ref.3, bf16[128,1024]{1,0:T(8,128)(2,1)} %v_ref.3, bf16[128,1024]{1,0:T(8,128)(2,1)} %g_ref.3), custom_call_target="tpu_custom_call" | custom-call | bytes 1048576 | tf_op jit(solution)/shard_map/pack_mine/pallas_call | solution.py:343
  10.5 0.9 slice_dynamic-update-slice_fusion
  11.3 26.3 %all_to_all.20.refs_0_.kv_ref = bf16[32,64,128]{2,1,0:T(8,128)(2,1)S(1)} all-to-all(bf16[32,64,128]{2,1,0:T(8,128)(2,1)} %get-tuple-element.34), channel_id=1, replica_groups=mesh['bend'=2,'z'=8,'y'=4,'x'=4] {'z','y'}, dimensions={0} | all-to-all | bytes 1048576 | tf_op jit(solution)/shard_map/all_to_all | solution.py:356
  37.6 1.2 collective-permute-start.1
  38.8 1.5 %collective-permute-start.2 = (bf16[32,64,128]{2,1,0:T(8,128)(2,1)S(1)}, bf16[32,64,128]{2,1,0:T(8,128)(2,1)S(1)}, u32[]{:S(2)}, u32[]{:S(2)}) collective-permute-start(bf16[32,64,128]{2,1,0:T(8,128)(2,1)S(1)} %all_to_all.20.refs_0_.kv_ref), channel_id=1, source_target_pairs={{0,3},{1,0},{2,1},{3,2},{4,7},{5,4},{6,5},{7,6},{8,11},{9,8},{10,9... | collective-permute-start | bytes 1572872 | tf_op jit(solution)/shard_map/ppermute | solution.py:317
  40.3 5.0 %all-to-all-start.1 = ((bf16[32,64,128]{2,1,0:T(8,128)(2,1)}), bf16[32,64,128]{2,1,0:T(8,128)(2,1)S(1)}, u32[]{:S(2)}, u32[]{:S(2)}) async-start(bf16[32,64,128]{2,1,0:T(8,128)(2,1)} %get-tuple-element.22), calls=%async_computation.1 | async-start | bytes 1048576 | tf_op jit(solution)/shard_map/all_to_all | solution.py:358
  45.3 0.1 pad.3.clone
  45.4 0.7 copy-done.10
  46.0 0.7 copy.10.col_ref
  46.8 0.7 copy.11.nbr_ref
  47.5 0.6 concatenate.7.nbrt_ref
  48.1 0.7 add_add_fusion.row_ref
  48.8 2.3 %tables.1 = s32[40,128]{1,0:T(8,128)} custom-call(s32[8,128]{1,0:T(8,128)} %add_add_fusion.row_ref, s32[128,1]{1,0:T(8,128)} %copy.10.col_ref, s32[128,10]{1,0:T(8,128)} %copy.11.nbr_ref, s32[16,128]{1,0:T(8,128)} %concatenate.7.nbrt_ref), custom_call_target="tpu_custom_call" | custom-call | tf_op jit(solution)/shard_map/tables/pallas_call | solution.py:72
  51.1 2.2 %collective-permute-start.3 = (s32[40,128]{1,0:T(8,128)}, s32[40,128]{1,0:T(8,128)S(1)}, u32[]{:S(2)}, u32[]{:S(2)}) collective-permute-start(s32[40,128]{1,0:T(8,128)} %tables.1), channel_id=1, source_target_pairs={{0,128},{128,0},{1,129},{129,1},{2,130},{130,2},{3,131},{131,3},{4... | collective-permute-start | bytes 61448 | tf_op jit(solution)/shard_map/ppermute | solution.py:313
  53.2 1.1 collective-permute-done.3
  54.3 0.6 broadcast_select_fusion.tab
  54.9 0.3 collective-permute-start.6
  55.3 0.1 collective-permute-start.4
  55.4 2.7 %collective-permute-start.5 = (bf16[16,64,128]{2,1,0:T(8,128)(2,1)S(1)}, bf16[16,64,128]{2,1,0:T(8,128)(2,1)}, u32[]{:S(2)}, u32[]{:S(2)}) collective-permute-start(bf16[16,64,128]{2,1,0:T(8,128)(2,1)S(1)} %slice.21), channel_id=1, source_target_pairs={{0,3},{1,0},{2,1},{3,2},{4,7},{5,4},{6,5},{7,6},{8,11},{9,8},{10,9... | collective-permute-start | bytes 786440 | tf_op jit(solution)/shard_map/ppermute | solution.py:323
  58.1 0.7 collective-permute-start.7
  58.9 5.5 %collective-permute-done.4.refs_3_ = bf16[16,64,128]{2,1,0:T(8,128)(2,1)S(1)} collective-permute-done((bf16[16,64,128]{2,1,0:T(8,128)(2,1)S(1)}, bf16[16,64,128]{2,1,0:T(8,128)(2,1)S(1)}, u32[]{:S(2)}, u32[]{:S(2)}) %collective-permute-start.4) | collective-permute-done | bytes 262176 | tf_op jit(solution)/shard_map/ppermute | solution.py:322
  64.3 1.0 collective-permute-start.9
  65.3 0.1 collective-permute-start.10
  65.4 0.2 collective-permute-start.11
  65.6 1.0 collective-permute-done.9.refs_8_
  66.6 2.0 %collective-permute-start.12 = (bf16[32,64,128]{2,1,0:T(8,128)(2,1)S(1)}, bf16[32,64,128]{2,1,0:T(8,128)(2,1)S(1)}, u32[]{:S(2)}, u32[]{:S(2)}) collective-permute-start(bf16[32,64,128]{2,1,0:T(8,128)(2,1)S(1)} %all-to-all-done.1.qg_ref.refs_0_), channel_id=1, source_target_pairs={{0,3},{1,0},{2,1},{3,2},{4,7},{5,4},{6,5},{7,6},{8,11},{9,8},{10,9... | collective-permute-start | bytes 1572872 | tf_op jit(solution)/shard_map/ppermute | solution.py:317
  68.6 0.7 copy-done.12
  69.4 12.9 %query_side.1 = (bf16[32,32,128]{2,1,0:T(8,128)(2,1)}, f32[8,32,128]{2,1,0:T(8,128)}) custom-call(s32[40,128]{1,0:T(8,128)} %broadcast_select_fusion.tab, bf16[32,64,128]{2,1,0:T(8,128)(2,1)} %copy-done.1, bf16[32,64,128]{2,1,0:T(8,128)(2,1)} %copy-done, bf16[32,64,128]{2,1,0:T(8,128)(2,1)} %copy-done.3, bf16[32,64,128]{2,1,0:T(8,128)(2,1)} %copy-done.4, ...), custom_call_target="tpu_custom_call" | custom-call | flops 6000000000 | bytes 20971520 | tf_op jit(solution)/shard_map/query_side/pallas_call | solution.py:374
  82.4 0.1 collective-permute-start.13
  82.5 2.7 %collective-permute-start.14 = (bf16[16,64,128]{2,1,0:T(8,128)(2,1)S(1)}, bf16[16,64,128]{2,1,0:T(8,128)(2,1)S(1)}, u32[]{:S(2)}, u32[]{:S(2)}) collective-permute-start(bf16[16,64,128]{2,1,0:T(8,128)(2,1)S(1)} %slice.23), channel_id=1, source_target_pairs={{0,3},{1,0},{2,1},{3,2},{4,7},{5,4},{6,5},{7,6},{8,11},{9,8},{10,9... | collective-permute-start | bytes 786440 | tf_op jit(solution)/shard_map/ppermute | solution.py:323
  85.2 1.1 collective-permute-start.15
  86.4 0.1 collective-permute-start.16
  86.5 0.4 collective-permute-start.17
  86.9 8.3 %all_to_all.21.stats_ref = f32[8,32,128]{2,1,0:T(8,128)} all-to-all(f32[8,32,128]{2,1,0:T(8,128)S(1)} %copy-done.7), channel_id=1, replica_groups=mesh['bend'=2,'z'=8,'y'=4,'x'=4] {'bend','x'}, dimensions={0} | all-to-all | bytes 262144 | tf_op jit(solution)/shard_map/all_to_all | solution.py:387
  95.2 0.5 collective-permute-start.18
  95.7 0.1 collective-permute-start.19
  95.9 0.9 copy-done.15
  96.7 0.1 collective-permute-done.18.refs_8_
  96.9 0.4 collective-permute-done.19.refs_9_
  97.3 0.3 copy-done.19
  97.6 0.4 copy-done.20
  98.0 11.0 %key_side.1 = bf16[32,96,128]{2,1,0:T(8,128)(2,1)} custom-call(s32[40,128]{1,0:T(8,128)} %broadcast_select_fusion.tab, bf16[32,64,128]{2,1,0:T(8,128)(2,1)} %copy-done, bf16[32,32,128]{2,1,0:T(8,128)(2,1)} %get-tuple-element.25.dq_ref, f32[8,32,128]{2,1,0:T(8,128)} %all_to_all.21.stats_ref, bf16[32,64,128]{2,1,0:T(8,128)(2,1)} %copy-done.1, ...), custom_call_target="tpu_custom_call" | custom-call | flops 6000000000 | bytes 20971520 | tf_op jit(solution)/shard_map/key_side/pallas_call | solution.py:395
  109.0 30.9 %all_to_all.22.full_ref = bf16[32,96,128]{2,1,0:T(8,128)(2,1)S(1)} all-to-all(bf16[32,96,128]{2,1,0:T(8,128)(2,1)} %key_side.1), channel_id=1, replica_groups=mesh['bend'=2,'z'=8,'y'=4,'x'=4] {'z','y'}, dimensions={0} | all-to-all | bytes 1572864 | tf_op jit(solution)/shard_map/all_to_all | solution.py:406
  139.8 2.9 %collective-permute-start.20 = (bf16[16,96,128]{2,1,0:T(8,128)(2,1)S(1)}, bf16[16,96,128]{2,1,0:T(8,128)(2,1)S(1)}, u32[]{:S(2)}, u32[]{:S(2)}) collective-permute-start(bf16[16,96,128]{2,1,0:T(8,128)(2,1)S(1)} %constant_dynamic-slice_fusion), channel_id=1, source_target_pairs={{0,128},{128,0},{1,129},{129,1},{2,130},{130,2},{3,131},{131,3},{4... | collective-permute-start | bytes 1179656 | tf_op jit(solution)/shard_map/ppermute | solution.py:313
  142.7 1.3 collective-permute-done.20.other_ref
  144.1 1.1 unpack.1
  (61 shorter events, 0.3 us)
Async XLA Ops:
  4.1 6.3 %collective-permute-start = (bf16[32,64,128]{2,1,0:T(8,128)(2,1)}, bf16[32,64,128]{2,1,0:T(8,128)(2,1)S(1)}, u32[]{:S(2)}, u32[]{:S(2)}) collective-permute-start(bf16[32,64,128]{2,1,0:T(8,128)(2,1)} %pack_other.1), channel_id=1, source_target_pairs={{0,128},{128,0},{1,129},{129,1},{2,130},{130,2},{3,131},{131,3},{4... | collective-permute-start | bytes 1572872 | tf_op jit(solution)/shard_map/ppermute | solution.py:313
  37.6 17.3 %copy-start = (bf16[32,64,128]{2,1,0:T(8,128)(2,1)}, bf16[32,64,128]{2,1,0:T(8,128)(2,1)S(1)}, u32[]{:S(2)}) copy-start(bf16[32,64,128]{2,1,0:T(8,128)(2,1)S(1)} %all_to_all.20.refs_0_.kv_ref) | copy-start | bytes 1572868
  37.6 17.7 %collective-permute-start.1 = (bf16[32,64,128]{2,1,0:T(8,128)(2,1)S(1)}, bf16[32,64,128]{2,1,0:T(8,128)(2,1)S(1)}, u32[]{:S(2)}, u32[]{:S(2)}) collective-permute-start(bf16[32,64,128]{2,1,0:T(8,128)(2,1)S(1)} %all_to_all.20.refs_0_.kv_ref), channel_id=1, source_target_pairs={{0,1},{1,2},{2,3},{3,0},{4,5},{5,6},{6,7},{7,4},{8,9},{9,10},{10,1... | collective-permute-start | bytes 1572872 | tf_op jit(solution)/shard_map/ppermute | solution.py:317
  38.8 16.5 %collective-permute-start.2 = (bf16[32,64,128]{2,1,0:T(8,128)(2,1)S(1)}, bf16[32,64,128]{2,1,0:T(8,128)(2,1)S(1)}, u32[]{:S(2)}, u32[]{:S(2)}) collective-permute-start(bf16[32,64,128]{2,1,0:T(8,128)(2,1)S(1)} %all_to_all.20.refs_0_.kv_ref), channel_id=1, source_target_pairs={{0,3},{1,0},{2,1},{3,2},{4,7},{5,4},{6,5},{7,6},{8,11},{9,8},{10,9... | collective-permute-start | bytes 1572872 | tf_op jit(solution)/shard_map/ppermute | solution.py:317
  40.3 25.1 %all-to-all-start.1 = ((bf16[32,64,128]{2,1,0:T(8,128)(2,1)}), bf16[32,64,128]{2,1,0:T(8,128)(2,1)S(1)}, u32[]{:S(2)}, u32[]{:S(2)}) async-start(bf16[32,64,128]{2,1,0:T(8,128)(2,1)} %get-tuple-element.22), calls=%async_computation.1 | async-start | bytes 1048576 | tf_op jit(solution)/shard_map/all_to_all | solution.py:358
  45.4 0.7 copy-start.10
  46.0 0.7 copy-start.9
  51.1 3.2 %copy-start.8 = (s32[40,128]{1,0:T(8,128)S(1)}, s32[40,128]{1,0:T(8,128)}, u32[]{:S(2)}) copy-start(s32[40,128]{1,0:T(8,128)} %tables.1) | copy-start | bytes 61444
  51.1 3.2 %collective-permute-start.3 = (s32[40,128]{1,0:T(8,128)}, s32[40,128]{1,0:T(8,128)S(1)}, u32[]{:S(2)}, u32[]{:S(2)}) collective-permute-start(s32[40,128]{1,0:T(8,128)} %tables.1), channel_id=1, source_target_pairs={{0,128},{128,0},{1,129},{129,1},{2,130},{130,2},{3,131},{131,3},{4... | collective-permute-start | bytes 61448 | tf_op jit(solution)/shard_map/ppermute | solution.py:313
  54.9 10.5 %collective-permute-start.6 = (bf16[32,64,128]{2,1,0:T(8,128)(2,1)S(1)}, bf16[32,64,128]{2,1,0:T(8,128)(2,1)S(1)}, u32[]{:S(2)}, u32[]{:S(2)}) collective-permute-start(bf16[32,64,128]{2,1,0:T(8,128)(2,1)S(1)} %all_to_all.20.refs_0_.kv_ref), channel_id=1, source_target_pairs={{0,128},{128,0},{1,129},{129,1},{2,130},{130,2},{3,131},{131,3},{4... | collective-permute-start | bytes 1572872 | tf_op jit(solution)/shard_map/ppermute | solution.py:313
  55.2 13.3 %copy-start.3 = (bf16[32,64,128]{2,1,0:T(8,128)(2,1)}, bf16[32,64,128]{2,1,0:T(8,128)(2,1)S(1)}, u32[]{:S(2)}) copy-start(bf16[32,64,128]{2,1,0:T(8,128)(2,1)S(1)} %collective-permute-done.1.refs_1_) | copy-start | bytes 1572868
  55.2 13.3 %copy-start.4 = (bf16[32,64,128]{2,1,0:T(8,128)(2,1)}, bf16[32,64,128]{2,1,0:T(8,128)(2,1)S(1)}, u32[]{:S(2)}) copy-start(bf16[32,64,128]{2,1,0:T(8,128)(2,1)S(1)} %collective-permute-done.2.refs_2_) | copy-start | bytes 1572868
  55.3 9.0 %collective-permute-start.4 = (bf16[16,64,128]{2,1,0:T(8,128)(2,1)S(1)}, bf16[16,64,128]{2,1,0:T(8,128)(2,1)S(1)}, u32[]{:S(2)}, u32[]{:S(2)}) collective-permute-start(bf16[16,64,128]{2,1,0:T(8,128)(2,1)S(1)} %slice.20), channel_id=1, source_target_pairs={{0,1},{1,2},{2,3},{3,0},{4,5},{5,6},{6,7},{7,4},{8,9},{9,10},{10,1... | collective-permute-start | bytes 786440 | tf_op jit(solution)/shard_map/ppermute | solution.py:322
  55.4 9.9 %collective-permute-start.5 = (bf16[16,64,128]{2,1,0:T(8,128)(2,1)S(1)}, bf16[16,64,128]{2,1,0:T(8,128)(2,1)}, u32[]{:S(2)}, u32[]{:S(2)}) collective-permute-start(bf16[16,64,128]{2,1,0:T(8,128)(2,1)S(1)} %slice.21), channel_id=1, source_target_pairs={{0,3},{1,0},{2,1},{3,2},{4,7},{5,4},{6,5},{7,6},{8,11},{9,8},{10,9... | collective-permute-start | bytes 786440 | tf_op jit(solution)/shard_map/ppermute | solution.py:323
  58.1 10.4 %collective-permute-start.7 = (bf16[32,64,128]{2,1,0:T(8,128)(2,1)S(1)}, bf16[32,64,128]{2,1,0:T(8,128)(2,1)S(1)}, u32[]{:S(2)}, u32[]{:S(2)}) collective-permute-start(bf16[32,64,128]{2,1,0:T(8,128)(2,1)S(1)} %collective-permute-done.1.refs_1_), channel_id=1, source_target_pairs={{0,128},{128,0},{1,129},{129,1},{2,130},{130,2},{3,131},{131,3},{4... | collective-permute-start | bytes 1572872 | tf_op jit(solution)/shard_map/ppermute | solution.py:313
  58.9 9.7 %collective-permute-start.8 = (bf16[32,64,128]{2,1,0:T(8,128)(2,1)S(1)}, bf16[32,64,128]{2,1,0:T(8,128)(2,1)}, u32[]{:S(2)}, u32[]{:S(2)}) collective-permute-start(bf16[32,64,128]{2,1,0:T(8,128)(2,1)S(1)} %collective-permute-done.2.refs_2_), channel_id=1, source_target_pairs={{0,128},{128,0},{1,129},{129,1},{2,130},{130,2},{3,131},{131,3},{4... | collective-permute-start | bytes 1572872 | tf_op jit(solution)/shard_map/ppermute | solution.py:313
  64.3 4.3 %copy-start.16 = (bf16[16,64,128]{2,1,0:T(8,128)(2,1)}, bf16[16,64,128]{2,1,0:T(8,128)(2,1)S(1)}, u32[]{:S(2)}) copy-start(bf16[16,64,128]{2,1,0:T(8,128)(2,1)S(1)} %collective-permute-done.4.refs_3_) | copy-start | bytes 786436
  64.3 2.3 %collective-permute-start.9 = (bf16[16,64,128]{2,1,0:T(8,128)(2,1)S(1)}, bf16[16,64,128]{2,1,0:T(8,128)(2,1)}, u32[]{:S(2)}, u32[]{:S(2)}) collective-permute-start(bf16[16,64,128]{2,1,0:T(8,128)(2,1)S(1)} %collective-permute-done.4.refs_3_), channel_id=1, source_target_pairs={{0,128},{128,0},{1,129},{129,1},{2,130},{130,2},{3,131},{131,3},{4... | collective-permute-start | bytes 786440 | tf_op jit(solution)/shard_map/ppermute | solution.py:313
  65.3 3.3 %collective-permute-start.10 = (bf16[16,64,128]{2,1,0:T(8,128)(2,1)}, bf16[16,64,128]{2,1,0:T(8,128)(2,1)}, u32[]{:S(2)}, u32[]{:S(2)}) collective-permute-start(bf16[16,64,128]{2,1,0:T(8,128)(2,1)} %collective-permute-done.5.refs_4_), channel_id=1, source_target_pairs={{0,128},{128,0},{1,129},{129,1},{2,130},{130,2},{3,131},{131,3},{4... | collective-permute-start | bytes 786440 | tf_op jit(solution)/shard_map/ppermute | solution.py:313
  65.4 3.2 %copy-start.1 = (bf16[32,64,128]{2,1,0:T(8,128)(2,1)}, bf16[32,64,128]{2,1,0:T(8,128)(2,1)S(1)}, u32[]{:S(2)}) copy-start(bf16[32,64,128]{2,1,0:T(8,128)(2,1)S(1)} %all-to-all-done.1.qg_ref.refs_0_) | copy-start | bytes 1572868
  65.4 3.2 %copy-start.11 = (bf16[32,64,128]{2,1,0:T(8,128)(2,1)}, bf16[32,64,128]{2,1,0:T(8,128)(2,1)S(1)}, u32[]{:S(2)}) copy-start(bf16[32,64,128]{2,1,0:T(8,128)(2,1)S(1)} %collective-permute-done.6.refs_5_) | copy-start | bytes 1572868
  65.4 16.9 %collective-permute-start.11 = (bf16[32,64,128]{2,1,0:T(8,128)(2,1)S(1)}, bf16[32,64,128]{2,1,0:T(8,128)(2,1)S(1)}, u32[]{:S(2)}, u32[]{:S(2)}) collective-permute-start(bf16[32,64,128]{2,1,0:T(8,128)(2,1)S(1)} %all-to-all-done.1.qg_ref.refs_0_), channel_id=1, source_target_pairs={{0,1},{1,2},{2,3},{3,0},{4,5},{5,6},{6,7},{7,4},{8,9},{9,10},{10,1... | collective-permute-start | bytes 1572872 | tf_op jit(solution)/shard_map/ppermute | solution.py:317
  66.6 15.7 %collective-permute-start.12 = (bf16[32,64,128]{2,1,0:T(8,128)(2,1)S(1)}, bf16[32,64,128]{2,1,0:T(8,128)(2,1)S(1)}, u32[]{:S(2)}, u32[]{:S(2)}) collective-permute-start(bf16[32,64,128]{2,1,0:T(8,128)(2,1)S(1)} %all-to-all-done.1.qg_ref.refs_0_), channel_id=1, source_target_pairs={{0,3},{1,0},{2,1},{3,2},{4,7},{5,4},{6,5},{7,6},{8,11},{9,8},{10,9... | collective-permute-start | bytes 1572872 | tf_op jit(solution)/shard_map/ppermute | solution.py:317
  68.6 0.8 copy-start.12
  82.3 4.1 %copy-start.5 = (bf16[32,64,128]{2,1,0:T(8,128)(2,1)}, bf16[32,64,128]{2,1,0:T(8,128)(2,1)S(1)}, u32[]{:S(2)}) copy-start(bf16[32,64,128]{2,1,0:T(8,128)(2,1)S(1)} %collective-permute-done.11.refs_1_) | copy-start | bytes 1572868
  82.3 4.2 %copy-start.6 = (bf16[32,64,128]{2,1,0:T(8,128)(2,1)}, bf16[32,64,128]{2,1,0:T(8,128)(2,1)S(1)}, u32[]{:S(2)}) copy-start(bf16[32,64,128]{2,1,0:T(8,128)(2,1)S(1)} %collective-permute-done.12.refs_2_) | copy-start | bytes 1572868
  82.3 2.9 %copy-start.2 = (bf16[32,64,128]{2,1,0:T(8,128)(2,1)S(1)}, bf16[32,64,128]{2,1,0:T(8,128)(2,1)}, u32[]{:S(2)}) copy-start(bf16[32,64,128]{2,1,0:T(8,128)(2,1)} %copy-done.1) | copy-start | bytes 1572868
  82.4 4.5 %copy-start.7 = (f32[8,32,128]{2,1,0:T(8,128)S(1)}, f32[8,32,128]{2,1,0:T(8,128)}, u32[]{:S(2)}) copy-start(f32[8,32,128]{2,1,0:T(8,128)} %get-tuple-element.27) | copy-start | bytes 393220
  82.4 12.8 %collective-permute-start.13 = (bf16[16,64,128]{2,1,0:T(8,128)(2,1)S(1)}, bf16[16,64,128]{2,1,0:T(8,128)(2,1)S(1)}, u32[]{:S(2)}, u32[]{:S(2)}) collective-permute-start(bf16[16,64,128]{2,1,0:T(8,128)(2,1)S(1)} %slice.22), channel_id=1, source_target_pairs={{0,1},{1,2},{2,3},{3,0},{4,5},{5,6},{6,7},{7,4},{8,9},{9,10},{10,1... | collective-permute-start | bytes 786440 | tf_op jit(solution)/shard_map/ppermute | solution.py:322
  82.5 12.7 %collective-permute-start.14 = (bf16[16,64,128]{2,1,0:T(8,128)(2,1)S(1)}, bf16[16,64,128]{2,1,0:T(8,128)(2,1)S(1)}, u32[]{:S(2)}, u32[]{:S(2)}) collective-permute-start(bf16[16,64,128]{2,1,0:T(8,128)(2,1)S(1)} %slice.23), channel_id=1, source_target_pairs={{0,3},{1,0},{2,1},{3,2},{4,7},{5,4},{6,5},{7,6},{8,11},{9,8},{10,9... | collective-permute-start | bytes 786440 | tf_op jit(solution)/shard_map/ppermute | solution.py:323
  85.2 10.6 %collective-permute-start.15 = (bf16[32,64,128]{2,1,0:T(8,128)(2,1)S(1)}, bf16[32,64,128]{2,1,0:T(8,128)(2,1)S(1)}, u32[]{:S(2)}, u32[]{:S(2)}) collective-permute-start(bf16[32,64,128]{2,1,0:T(8,128)(2,1)S(1)} %copy-done.2), channel_id=1, source_target_pairs={{0,128},{128,0},{1,129},{129,1},{2,130},{130,2},{3,131},{131,3},{4... | collective-permute-start | bytes 1572872 | tf_op jit(solution)/shard_map/ppermute | solution.py:313
  86.4 9.4 %collective-permute-start.16 = (bf16[32,64,128]{2,1,0:T(8,128)(2,1)S(1)}, bf16[32,64,128]{2,1,0:T(8,128)(2,1)S(1)}, u32[]{:S(2)}, u32[]{:S(2)}) collective-permute-start(bf16[32,64,128]{2,1,0:T(8,128)(2,1)S(1)} %collective-permute-done.11.refs_1_), channel_id=1, source_target_pairs={{0,128},{128,0},{1,129},{129,1},{2,130},{130,2},{3,131},{131,3},{4... | collective-permute-start | bytes 1572872 | tf_op jit(solution)/shard_map/ppermute | solution.py:313
  86.5 9.4 %collective-permute-start.17 = (bf16[32,64,128]{2,1,0:T(8,128)(2,1)S(1)}, bf16[32,64,128]{2,1,0:T(8,128)(2,1)S(1)}, u32[]{:S(2)}, u32[]{:S(2)}) collective-permute-start(bf16[32,64,128]{2,1,0:T(8,128)(2,1)S(1)} %collective-permute-done.12.refs_2_), channel_id=1, source_target_pairs={{0,128},{128,0},{1,129},{129,1},{2,130},{130,2},{3,131},{131,3},{4... | collective-permute-start | bytes 1572872 | tf_op jit(solution)/shard_map/ppermute | solution.py:313
  95.2 2.0 %copy-start.17 = (bf16[16,64,128]{2,1,0:T(8,128)(2,1)}, bf16[16,64,128]{2,1,0:T(8,128)(2,1)S(1)}, u32[]{:S(2)}) copy-start(bf16[16,64,128]{2,1,0:T(8,128)(2,1)S(1)} %collective-permute-done.13.refs_3_) | copy-start | bytes 786436
  95.2 2.0 %copy-start.18 = (bf16[16,64,128]{2,1,0:T(8,128)(2,1)}, bf16[16,64,128]{2,1,0:T(8,128)(2,1)S(1)}, u32[]{:S(2)}) copy-start(bf16[16,64,128]{2,1,0:T(8,128)(2,1)S(1)} %collective-permute-done.14.refs_4_) | copy-start | bytes 786436
  95.2 1.6 %collective-permute-start.18 = (bf16[16,64,128]{2,1,0:T(8,128)(2,1)S(1)}, bf16[16,64,128]{2,1,0:T(8,128)(2,1)S(1)}, u32[]{:S(2)}, u32[]{:S(2)}) collective-permute-start(bf16[16,64,128]{2,1,0:T(8,128)(2,1)S(1)} %collective-permute-done.13.refs_3_), channel_id=1, source_target_pairs={{0,128},{128,0},{1,129},{129,1},{2,130},{130,2},{3,131},{131,3},{4... | collective-permute-start | bytes 786440 | tf_op jit(solution)/shard_map/ppermute | solution.py:313
  95.7 1.5 %collective-permute-start.19 = (bf16[16,64,128]{2,1,0:T(8,128)(2,1)S(1)}, bf16[16,64,128]{2,1,0:T(8,128)(2,1)S(1)}, u32[]{:S(2)}, u32[]{:S(2)}) collective-permute-start(bf16[16,64,128]{2,1,0:T(8,128)(2,1)S(1)} %collective-permute-done.14.refs_4_), channel_id=1, source_target_pairs={{0,128},{128,0},{1,129},{129,1},{2,130},{130,2},{3,131},{131,3},{4... | collective-permute-start | bytes 786440 | tf_op jit(solution)/shard_map/ppermute | solution.py:313
  95.8 1.4 copy-start.13
  95.8 1.4 copy-start.14
  95.8 0.9 copy-start.15
  96.9 0.7 copy-start.19
  97.2 0.7 copy-start.20
  139.8 4.2 %collective-permute-start.20 = (bf16[16,96,128]{2,1,0:T(8,128)(2,1)S(1)}, bf16[16,96,128]{2,1,0:T(8,128)(2,1)S(1)}, u32[]{:S(2)}, u32[]{:S(2)}) collective-permute-start(bf16[16,96,128]{2,1,0:T(8,128)(2,1)S(1)} %constant_dynamic-slice_fusion), channel_id=1, source_target_pairs={{0,128},{128,0},{1,129},{129,1},{2,130},{130,2},{3,131},{131,3},{4... | collective-permute-start | bytes 1179656 | tf_op jit(solution)/shard_map/ppermute | solution.py:313

commit v3 on v2

--- a/solution.py
+++ b/solution.py
@@ -15,7 +15,8 @@
 HEADS = 16
 NSRC = 32
 NX = 4
-UNROLL = 8
+UNROLL = 16
+SLOTS = 8
 SCALE = 1.0 / math.sqrt(HD)
 C2 = SCALE * math.log2(math.e)
 NEG = -1e30
@@ -35,80 +36,75 @@
     return pl.CostEstimate(flops=flops, bytes_accessed=nbytes, transcendentals=0)
 
 
-def tables_kernel(row_ref, col_ref, nbr_ref, nbrt_ref, out_ref):
+def tables_kernel(count, row_ref, nbrt_ref, out_ref):
     n = 128
     sub = lax.broadcasted_iota(jnp.int32, (n, n), 0)
     lane = lax.broadcasted_iota(jnp.int32, (n, n), 1)
-    b_of = (col_ref[:, 0:1] == lane).astype(F32).astype(BF)
-    adj = jnp.zeros((n, n), F32)
+    placed = (row_ref[...] == sub).astype(F32)
     adj_t = jnp.zeros((n, n), F32)
     for k in range(NBR):
-        adj = adj + (nbr_ref[:, k : k + 1] == lane).astype(F32)
         adj_t = adj_t + (nbrt_ref[k : k + 1, :] == sub).astype(F32)
     eye = (sub == lane).astype(F32)
     tri = (lane <= sub).astype(F32).astype(BF)
-
-    def stored(a):
-        right = lax.dot_general(a.astype(BF), b_of, NT, preferred_element_type=F32)
-        return lax.dot_general(b_of, right.astype(BF), NN, preferred_element_type=F32) - eye
-
+    right = lax.dot_general(adj_t.astype(BF), placed.astype(BF), NN, preferred_element_type=F32)
+    near_t = lax.dot_general(placed.T.astype(BF), right.astype(BF), NN, preferred_element_type=F32) - eye
     out_ref[...] = jnp.zeros_like(out_ref)
     own = lax.broadcasted_iota(jnp.int32, (1, n), 1)
-    for base, a in ((0, adj_t), (16, adj)):
-        m = stored(a)
+    for base, m in ((0, near_t), (16, near_t.T)):
         rank = lax.dot_general(tri, m.astype(BF), NN, preferred_element_type=F32)
         out_ref[base : base + 1, :] = own
         for k in range(1, NBR):
             hit = jnp.where((rank == float(k)) & (m > 0.5), sub, 0)
             out_ref[base + k : base + k + 1, :] = jnp.sum(hit, axis=0, keepdims=True)
-    out_ref[32:33, :] = row_ref[1:2, :] - row_ref[0:1, :] * BLK
+    out_ref[32:33, :] = count[0] - row_ref[...] * BLK
 
 
 def make_tables(block_ids, neighbours, token_count):
-    row = jnp.concatenate(
-        [block_ids[None, :], jnp.broadcast_to(token_count[:1, None], (1, 128)), jnp.zeros((6, 128), jnp.int32)], 0
-    )
-    nbrt = jnp.concatenate([neighbours.T, jnp.full((6, 128), -1, jnp.int32)], 0)
     return pl.pallas_call(
         tables_kernel,
         out_shape=jax.ShapeDtypeStruct((40, 128), jnp.int32),
-        in_specs=[VMEM] * 4,
+        in_specs=[SMEM, VMEM, VMEM],
         out_specs=VMEM,
-        compiler_params=PARAMS,
+        compiler_params=SMALL,
         name="tables",
-    )(row, block_ids[:, None], neighbours, nbrt)
-
-
-def pack_half(half, ids, count, arrays, bufs, sems, kv_out, qg_out, base):
-    row0 = pl.multiple_of(half * HALF, HALF)
-    copies = [
-        pltpu.make_async_copy(arrays[i].at[pl.ds(row0, HALF)], bufs.at[i], sems.at[i]) for i in (1, 2, 0, 3)
-    ]
+    )(token_count, block_ids[None, :], neighbours.T)
+
+
+def pack_kernel(masked, ids, count, a_ref, b_ref, sent_ref, mine_ref, bufs, sems):
+    copies = [pltpu.make_async_copy(src, bufs.at[i], sems.at[i]) for i, src in enumerate((a_ref, b_ref))]
     for copy in copies:
         copy.start()
+    c = lax.axis_index("bend")
     t = lax.axis_index("z") * 16 + lax.axis_index("y") * 4 + lax.axis_index("x")
-    limit = count[0] - ids[t] * BLK - row0
-    keep = lax.broadcasted_iota(jnp.int32, (HALF, 128), 0) < limit
+    limit = count[0] - ids[t] * BLK
+    row = lax.broadcasted_iota(jnp.int32, (HALF, 128), 0)
     for copy in copies:
         copy.wait()
-    for p in range(HEADS // 2):
-        cols = slice(p * 128, p * 128 + 128)
-        q, k, v, g = (bufs[i, :, cols] for i in range(4))
-        g = jnp.where(keep, g.astype(F32), 0.0).astype(BF)
-        for out, m, n in ((kv_out, k, v), (qg_out, q, g)):
+    for out, base, half in ((sent_ref, 0, 1 - c), (mine_ref, c * HEADS, c)):
+        row0 = pl.multiple_of(half * HALF, HALF)
+        for p in range(HEADS // 2):
+            cols = slice(p * 128, p * 128 + 128)
+            m, n = (bufs[i, pl.ds(row0, HALF), cols] for i in range(2))
+            if masked:
+                n = jnp.where(row + row0 < limit, n.astype(F32), 0.0).astype(BF)
             out[base + 2 * p] = jnp.concatenate([m[:, :HD], n[:, :HD]], axis=1)
             out[base + 2 * p + 1] = jnp.concatenate([m[:, HD:], n[:, HD:]], axis=1)
 
 
-def pack_other_kernel(ids, count, q_ref, k_ref, v_ref, g_ref, out_ref, bufs, sems):
-    half = 1 - lax.axis_index("bend")
-    kv_ref, qg_ref = out_ref.at[pl.ds(0, HEADS)], out_ref.at[pl.ds(HEADS, HEADS)]
-    pack_half(half, ids, count, (q_ref, k_ref, v_ref, g_ref), bufs, sems, kv_ref, qg_ref, 0)
-
-
-def pack_mine_kernel(ids, count, q_ref, k_ref, v_ref, g_ref, kv_ref, qg_ref, bufs, sems):
-    half = lax.axis_index("bend")
-    pack_half(half, ids, count, (q_ref, k_ref, v_ref, g_ref), bufs, sems, kv_ref, qg_ref, half * HEADS)
+def pack(name, masked, ids, count, a, b):
+    return pl.pallas_call(
+        functools.partial(pack_kernel, masked),
+        out_shape=(
+            jax.ShapeDtypeStruct((HEADS, HALF, 128), BF),
+            jax.ShapeDtypeStruct((NSRC, HALF, 128), BF),
+        ),
+        in_specs=[SMEM] * 2 + [HBM] * 2,
+        out_specs=(VMEM, VMEM),
+        scratch_shapes=[pltpu.VMEM((2, BLK, HEADS * HD), BF), pltpu.SemaphoreType.DMA((2,))],
+        compiler_params=PARAMS,
+        cost_estimate=cost(0, 2**20),
+        name=name,
+    )(ids, count, a, b)
 
 
 def unpack_kernel(full_ref, other_ref, q_ref, k_ref, v_ref):
@@ -171,7 +167,7 @@
 def gather_tiles(held, tiles, u, where):
     for k in range(NBR):
         for h in range(2):
-            tiles[u, (2 * k + h) * HALF : (2 * k + h + 1) * HALF] = held[h, where[k][0], where[k][1]]
+            tiles[u % SLOTS, (2 * k + h) * HALF : (2 * k + h + 1) * HALF] = held[h, where[k][0], where[k][1]]
 
 
 def skewed(stages):
@@ -202,7 +198,7 @@
             top = jnp.full((HALF, 128), NEG, F32)
             for j in range(NBR // 2):
                 both = lax.dot_general(
-                    lhs, tiles[u, j * 256 : j * 256 + 256], NT, preferred_element_type=F32
+                    lhs, tiles[u % SLOTS, j * 256 : j * 256 + 256], NT, preferred_element_type=F32
                 )
                 for i in range(2):
                     k = 2 * j + i
@@ -212,8 +208,8 @@
                         sc = jnp.where((lane < limit) | mine, sc, NEG)
                     else:
                         sc = sc + jnp.where(lane_row < limit, 0.0, NEG)
-                    scores[u, 0, k] = sc
-                    scores[u, 1, k] = both[HALF:, i * 128 : i * 128 + 128]
+                    scores[u % SLOTS, 0, k] = sc
+                    scores[u % SLOTS, 1, k] = both[HALF:, i * 128 : i * 128 + 128]
                     top = jnp.maximum(top, sc)
             tops[u] = jnp.max(top, axis=1, keepdims=True)
 
@@ -221,18 +217,18 @@
             total = jnp.zeros((HALF, 128), F32)
             dot = jnp.zeros((HALF, 128), F32)
             for k in range(NBR):
-                p = jnp.exp2(scores[u, 0, k] - tops[u])
-                scores[u, 0, k] = p
+                p = jnp.exp2(scores[u % SLOTS, 0, k] - tops[u])
+                scores[u % SLOTS, 0, k] = p
                 total = total + p
-                dot = dot + p * scores[u, 1, k]
+                dot = dot + p * scores[u % SLOTS, 1, k]
             total = jnp.sum(total, axis=1, keepdims=True)
             totals[u] = total, jnp.sum(dot, axis=1, keepdims=True) / total
 
         def gradient(u):
             total, delta = totals[u]
             for k in range(NBR):
-                grads[u, :, k * 128 : k * 128 + 128] = (scores[u, 0, k] * (scores[u, 1, k] - delta)).astype(BF)
-            acc = lax.dot_general(grads[u], tiles[u], NN, preferred_element_type=F32)
+                grads[u % SLOTS, :, k * 128 : k * 128 + 128] = (scores[u % SLOTS, 0, k] * (scores[u % SLOTS, 1, k] - delta)).astype(BF)
+            acc = lax.dot_general(grads[u % SLOTS], tiles[u % SLOTS], NN, preferred_element_type=F32)
             dq = (acc * (SCALE / total)).astype(BF)
             dq_ref[ss[u]] = jnp.concatenate([dq[: HALF // 2, :HD], dq[HALF // 2 :, :HD]], axis=1)
             lse = tops[u] + jnp.log2(total)
@@ -274,12 +270,12 @@
             lhs = split_rows(kv_ref[ss[u]])
             for j in range(NBR // 2):
                 both = lax.dot_general(
-                    lhs, tiles[u, j * 256 : j * 256 + 256], NT, preferred_element_type=F32
+                    lhs, tiles[u % SLOTS, j * 256 : j * 256 + 256], NT, preferred_element_type=F32
                 )
                 for i in range(2):
                     k = 2 * j + i
-                    scores[u, 0, k] = both[:HALF, i * 128 : i * 128 + 128]
-                    scores[u, 1, k] = both[HALF:, i * 128 : i * 128 + 128]
+                    scores[u % SLOTS, 0, k] = both[:HALF, i * 128 : i * 128 + 128]
+                    scores[u % SLOTS, 1, k] = both[HALF:, i * 128 : i * 128 + 128]
 
         def weights(u):
             ok = sub < tab[32, ss[u] * NX + x]
@@ -287,13 +283,13 @@
                 ux, us, _ = where[u][k]
                 lse = jnp.concatenate([lses[ux, us]] * 8, axis=0)
                 delta = jnp.concatenate([deltas[ux, us]] * 8, axis=0)
-                p = jnp.exp2(scores[u, 0, k] * C2 - lse)
+                p = jnp.exp2(scores[u % SLOTS, 0, k] * C2 - lse)
                 p = jnp.where((ok | mine) if k == 0 else ok, p, 0.0)
-                pairs[u, :HALF, k * 128 : k * 128 + 128] = (p * (scores[u, 1, k] - delta)).astype(BF)
-                pairs[u, HALF:, k * 128 : k * 128 + 128] = p.astype(BF)
+                pairs[u % SLOTS, :HALF, k * 128 : k * 128 + 128] = (p * (scores[u % SLOTS, 1, k] - delta)).astype(BF)
+                pairs[u % SLOTS, HALF:, k * 128 : k * 128 + 128] = p.astype(BF)
 
         def gradient(u):
-            acc = lax.dot_general(pairs[u], tiles[u], NN, preferred_element_type=F32)
+            acc = lax.dot_general(pairs[u % SLOTS], tiles[u % SLOTS], NN, preferred_element_type=F32)
             out_ref[ss[u], :HALF] = jnp.where(lane < HD, acc[:HALF] * SCALE, acc[HALF:]).astype(BF)
 
         skewed((products, weights, gradient))
@@ -328,33 +324,15 @@
     c = lax.axis_index("bend")
     other_role = (lax.axis_index("z") // 4) != c
 
-    bufs = [pltpu.VMEM((4, HALF, HEADS * HD), BF), pltpu.SemaphoreType.DMA((4,))]
-    sent = pl.pallas_call(
-        pack_other_kernel,
-        out_shape=jax.ShapeDtypeStruct((2 * HEADS, HALF, 128), BF),
-        in_specs=[SMEM] * 2 + [HBM] * 4,
-        out_specs=VMEM,
-        scratch_shapes=bufs,
-        compiler_params=PARAMS,
-        cost_estimate=cost(0, 2**20),
-        name="pack_other",
-    )(block_ids, token_count, queries, keys_in, values, d_out)
-    came = swap(sent)
-    kv_out, qg_out = pl.pallas_call(
-        pack_mine_kernel,
-        out_shape=(jax.ShapeDtypeStruct((NSRC, HALF, 128), BF),) * 2,
-        in_specs=[SMEM] * 2 + [HBM] * 4,
-        out_specs=(VMEM, VMEM),
-        scratch_shapes=bufs,
-        compiler_params=PARAMS,
-        cost_estimate=cost(0, 2**20),
-        name="pack_mine",
-    )(block_ids, token_count, queries, keys_in, values, d_out)
     theirs = (1 - c) * HEADS
-    kv_out = lax.dynamic_update_slice_in_dim(kv_out, came[:HEADS], theirs, 0)
-    qg_out = lax.dynamic_update_slice_in_dim(qg_out, came[HEADS:], theirs, 0)
+    kv_sent, kv_mine = pack("pack_kv", False, block_ids, token_count, keys_in, values)
+    kv_came = swap(kv_sent)
+    qg_sent, qg_mine = pack("pack_qg", True, block_ids, token_count, queries, d_out)
+    kv_out = lax.dynamic_update_slice_in_dim(kv_mine, kv_came, theirs, 0)
+    kv_out, qg_sent, qg_mine = lax.optimization_barrier((kv_out, qg_sent, qg_mine))
     kv = lax.all_to_all(kv_out, ("z", "y"), 0, 0, tiled=True)
-    kv, qg_out = lax.optimization_barrier((kv, qg_out))
+    kv, qg_sent = lax.optimization_barrier((kv, qg_sent))
+    qg_out = lax.dynamic_update_slice_in_dim(qg_mine, swap(qg_sent), theirs, 0)
     qg = lax.all_to_all(qg_out, ("z", "y"), 0, 0, tiled=True)
 
     tab = make_tables(block_ids, neighbours, token_count)
@@ -367,8 +345,8 @@
     qg_first = first_step(late[0])
 
     held = pltpu.VMEM((2, NX, NSRC, HALF, 128), BF)
-    tiles = pltpu.VMEM((UNROLL, NBR * BLK, 128), BF)
-    scores = pltpu.VMEM((UNROLL, 2, NBR, HALF, 128), F32)
+    tiles = pltpu.VMEM((SLOTS, NBR * BLK, 128), BF)
+    scores = pltpu.VMEM((SLOTS, 2, NBR, HALF, 128), F32)
     stat = pltpu.VMEM((NX, NSRC, 8, 128), F32)
     sems = pltpu.SemaphoreType.DMA((10,))
     dq, rows = pl.pallas_call(
@@ -379,7 +357,7 @@
         ),
         in_specs=[SMEM, VMEM] + [ANY] * 10,
         out_specs=(VMEM, VMEM),
-        scratch_shapes=[held, tiles, scores, pltpu.VMEM((UNROLL, HALF, NBR * BLK), BF), sems],
+        scratch_shapes=[held, tiles, scores, pltpu.VMEM((SLOTS, HALF, NBR * BLK), BF), sems],
         compiler_params=PARAMS,
         cost_estimate=cost(6 * 10**9, 20 * 2**20),
         name="query_side",
@@ -397,7 +375,7 @@
         out_shape=jax.ShapeDtypeStruct((NSRC, HALF + HALF // 2, 128), BF),
         in_specs=[SMEM, VMEM, VMEM, VMEM] + [ANY] * 10,
         out_specs=VMEM,
-        scratch_shapes=[held, tiles, scores, pltpu.VMEM((UNROLL, BLK, NBR * BLK), BF), stat, stat, sems],
+        scratch_shapes=[held, tiles, scores, pltpu.VMEM((SLOTS, BLK, NBR * BLK), BF), stat, stat, sems],
         compiler_params=PARAMS,
         cost_estimate=cost(6 * 10**9, 20 * 2**20),
         name="key_side",

time: 146 us -> 139 us (0.952)
  blocking collectives: 65.4 us -> 61.2 us
  starting transfers between devices: 28.1 us -> 32.1 us
  local copies, waits for them, and re-layouts: 6.24 us -> 2.65 us
  Pallas kernels: 33.1 us -> 29.8 us
    all_to_all x1, blocking collectives: 30.9 us -> 26.8 us  [per_device(): back = lax.all_to_all(grads, ('z', 'y'), 0, 0, tiled=True)]
    ppermute x13 -> x14, starting transfers between devices: 12.7 us -> 16.5 us  [swap(): return lax.ppermute(a, 'bend', SWAP)]
    ppermute x4, waiting for transfers between devices: 0.01 us -> 2.7 us  [first_step(): return (lax.ppermute(own, 'x', ring(1)), lax.ppermute(own, 'x', ring(-1)))]
    unnamed x43 -> x42, local copies, waits for them, and re-layouts: 3.79 us -> 1.77 us
    pallas_call x1, Pallas kernels: 2.27 us -> 0.59 us  [make_tables(): pl.pallas_call(tables_kernel, out_shape=jax.ShapeDtypeStruct((40, 128), j...]
    ppermute x2, waiting for transfers between devices: 5.47 us -> 3.88 us  [second_step(): r2 = lax.ppermute(r1[:half], 'x', ring(1))]
    ppermute x13 -> x14, waiting for transfers between devices: 3.92 us -> 3.99 us  [swap(): return lax.ppermute(a, 'bend', SWAP)]
  transfers between devices with their start and end apart: 22 -> 23, of which waited for: 6 -> 7; matrix products, arithmetic and copies ran while one was open for 2% -> 1% of each run, Pallas kernels for 13% -> 11%
where the time goes in v3:
time: 139 us
  blocking collectives  61.2 us (44%)
  starting transfers between devices  32.1 us (23%)
  Pallas kernels  29.8 us (21%)
  waiting for transfers between devices  10.6 us (8%)
  local copies, waits for them, and re-layouts  2.65 us (2%)
  between operations  1.58 us (1%)
    all_to_all x1, blocking collectives, per_device(): back = lax.all_to_all(grads, ('z', 'y'), 0, 0, tiled=True)  26.8 us
    all_to_all x1, blocking collectives, per_device(): kv = lax.all_to_all(kv_out, ('z', 'y'), 0, 0, tiled=True)  26.1 us
    ppermute x14, starting transfers between devices, swap(): return lax.ppermute(a, 'bend', SWAP)  16.5 us
    pallas_call x1, Pallas kernels, per_device(): pl.pallas_call(query_kernel, out_shape=(jax.ShapeDtypeStruct((NSRC, HALF...  12 us
    pallas_call x1, Pallas kernels, per_device(): pl.pallas_call(key_kernel, out_shape=jax.ShapeDtypeStruct((NSRC, HALF + H...  10.6 us
    all_to_all x1, blocking collectives, per_device(): stats = lax.all_to_all(rows, ('bend', 'x'), 0, 0, tiled=True)  8.29 us
    pallas_call x2, Pallas kernels, pack(): pl.pallas_call(functools.partial(pack_kernel, masked), out_shape=(jax.Sha...  5.46 us
    ppermute x4, starting transfers between devices, first_step(): return (lax.ppermute(own, 'x', ring(1)), lax.ppermute(own, 'x', ring(-1)))  5.43 us
  transfers between devices with their start and end apart: 23, of which 7 were waited for; matrix products, arithmetic and copies ran while one was open for 1% of the time, Pallas kernels for 11%

profile of v3, /device:TPU:1, one launch (start us, length us, event | category | flops | bytes accessed | tf_op | source)
XLA Modules:
  0.0 138.6 jit_solution(12775687543666816233)
XLA Ops:
  1.3 2.7 %pack_kv.1 = (bf16[16,64,128]{2,1,0:T(8,128)(2,1)}, bf16[32,64,128]{2,1,0:T(8,128)(2,1)}) custom-call(s32[128]{0:T(128)} %ids.3, s32[1]{0:T(128)S(6)} %copy.12.count, bf16[128,1024]{1,0:T(8,128)(2,1)} %a_ref.2, bf16[128,1024]{1,0:T(8,128)(2,1)} %b_ref.2), custom_call_target="tpu_custom_call" | custom-call | bytes 1048576 | tf_op jit(solution)/shard_map/pack_kv/pallas_call | solution.py:95
  4.0 3.3 %collective-permute-start = (bf16[16,64,128]{2,1,0:T(8,128)(2,1)}, bf16[16,64,128]{2,1,0:T(8,128)(2,1)S(1)}, u32[]{:S(2)}, u32[]{:S(2)}) collective-permute-start(bf16[16,64,128]{2,1,0:T(8,128)(2,1)} %get-tuple-element.24), channel_id=1, source_target_pairs={{0,128},{128,0},{1,129},{129,1},{2,130},{130,2},{3,131},{131,3},{4... | collective-permute-start | bytes 786440 | tf_op jit(solution)/shard_map/ppermute | solution.py:309
  7.4 2.7 %pack_qg.1 = (bf16[16,64,128]{2,1,0:T(8,128)(2,1)}, bf16[32,64,128]{2,1,0:T(8,128)(2,1)}) custom-call(s32[128]{0:T(128)} %ids.3, s32[1]{0:T(128)S(6)} %copy.12.count, bf16[128,1024]{1,0:T(8,128)(2,1)} %a_ref.3, bf16[128,1024]{1,0:T(8,128)(2,1)} %b_ref.3), custom_call_target="tpu_custom_call" | custom-call | bytes 1048576 | tf_op jit(solution)/shard_map/pack_qg/pallas_call | solution.py:95
  10.2 0.0 copy-start.20
  10.2 26.1 %all_to_all.20.refs_0_.kv_ref = bf16[32,64,128]{2,1,0:T(8,128)(2,1)S(1)} all-to-all(bf16[32,64,128]{2,1,0:T(8,128)(2,1)S(1)} %constant_dynamic-update-slice_fusion.1), channel_id=1, replica_groups=mesh['bend'=2,'z'=8,'y'=4,'x'=4] {'z','y'}, dimensions={0} | all-to-all | bytes 1048576 | tf_op jit(solution)/shard_map/all_to_all | solution.py:333
  36.3 1.9 %collective-permute-start.4 = (bf16[16,64,128]{2,1,0:T(8,128)(2,1)S(1)}, bf16[16,64,128]{2,1,0:T(8,128)(2,1)S(1)}, u32[]{:S(2)}, u32[]{:S(2)}) collective-permute-start(bf16[16,64,128]{2,1,0:T(8,128)(2,1)S(1)} %copy-done.20), channel_id=1, source_target_pairs={{0,128},{128,0},{1,129},{129,1},{2,130},{130,2},{3,131},{131,3},{4... | collective-permute-start | bytes 786440 | tf_op jit(solution)/shard_map/ppermute | solution.py:309
  38.2 1.2 collective-permute-start.1
  39.5 1.5 %collective-permute-start.2 = (bf16[32,64,128]{2,1,0:T(8,128)(2,1)S(1)}, bf16[32,64,128]{2,1,0:T(8,128)(2,1)S(1)}, u32[]{:S(2)}, u32[]{:S(2)}) collective-permute-start(bf16[32,64,128]{2,1,0:T(8,128)(2,1)S(1)} %all_to_all.20.refs_0_.kv_ref), channel_id=1, source_target_pairs={{0,3},{1,0},{2,1},{3,2},{4,7},{5,4},{6,5},{7,6},{8,11},{9,8},{10,9... | collective-permute-start | bytes 1572872 | tf_op jit(solution)/shard_map/ppermute | solution.py:313
  40.9 0.7 constant_dynamic-update-slice_fusion
  41.7 4.5 %all-to-all-start.1 = ((bf16[32,64,128]{2,1,0:T(8,128)(2,1)}), bf16[32,64,128]{2,1,0:T(8,128)(2,1)S(1)}, u32[]{:S(2)}, u32[]{:S(2)}) async-start(bf16[32,64,128]{2,1,0:T(8,128)(2,1)} %constant_dynamic-update-slice_fusion), calls=%async_computation.1 | async-start | bytes 1048576 | tf_op jit(solution)/shard_map/all_to_all | solution.py:336
  46.2 0.0 copy-start.1
  46.3 0.6 copy-done.1
  46.9 0.6 tables.1
  47.5 1.0 collective-permute-start.3
  48.5 0.8 collective-permute-done.3
  49.3 0.6 broadcast_select_fusion.tab
  49.9 0.3 collective-permute-start.7
  50.3 2.7 %collective-permute-done.1.refs_1_ = bf16[32,64,128]{2,1,0:T(8,128)(2,1)S(1)} collective-permute-done((bf16[32,64,128]{2,1,0:T(8,128)(2,1)S(1)}, bf16[32,64,128]{2,1,0:T(8,128)(2,1)S(1)}, u32[]{:S(2)}, u32[]{:S(2)}) %collective-permute-start.1) | collective-permute-done | bytes 524320 | tf_op jit(solution)/shard_map/ppermute | solution.py:313
  53.0 1.0 collective-permute-start.5
  54.0 1.9 %collective-permute-start.6 = (bf16[16,64,128]{2,1,0:T(8,128)(2,1)S(1)}, bf16[16,64,128]{2,1,0:T(8,128)(2,1)}, u32[]{:S(2)}, u32[]{:S(2)}) collective-permute-start(bf16[16,64,128]{2,1,0:T(8,128)(2,1)S(1)} %slice.13), channel_id=1, source_target_pairs={{0,3},{1,0},{2,1},{3,2},{4,7},{5,4},{6,5},{7,6},{8,11},{9,8},{10,9... | collective-permute-start | bytes 786440 | tf_op jit(solution)/shard_map/ppermute | solution.py:319
  55.8 1.4 %collective-permute-start.8 = (bf16[32,64,128]{2,1,0:T(8,128)(2,1)S(1)}, bf16[32,64,128]{2,1,0:T(8,128)(2,1)}, u32[]{:S(2)}, u32[]{:S(2)}) collective-permute-start(bf16[32,64,128]{2,1,0:T(8,128)(2,1)S(1)} %collective-permute-done.1.refs_1_), channel_id=1, source_target_pairs={{0,128},{128,0},{1,129},{129,1},{2,130},{130,2},{3,131},{131,3},{4... | collective-permute-start | bytes 1572872 | tf_op jit(solution)/shard_map/ppermute | solution.py:309
  57.3 0.1 collective-permute-start.9
  57.4 3.9 %collective-permute-done.5.refs_3_ = bf16[16,64,128]{2,1,0:T(8,128)(2,1)S(1)} collective-permute-done((bf16[16,64,128]{2,1,0:T(8,128)(2,1)S(1)}, bf16[16,64,128]{2,1,0:T(8,128)(2,1)S(1)}, u32[]{:S(2)}, u32[]{:S(2)}) %collective-permute-start.5) | collective-permute-done | bytes 262176 | tf_op jit(solution)/shard_map/ppermute | solution.py:318
  61.2 1.8 %collective-permute-start.10 = (bf16[16,64,128]{2,1,0:T(8,128)(2,1)S(1)}, bf16[16,64,128]{2,1,0:T(8,128)(2,1)}, u32[]{:S(2)}, u32[]{:S(2)}) collective-permute-start(bf16[16,64,128]{2,1,0:T(8,128)(2,1)S(1)} %collective-permute-done.5.refs_3_), channel_id=1, source_target_pairs={{0,128},{128,0},{1,129},{129,1},{2,130},{130,2},{3,131},{131,3},{4... | collective-permute-start | bytes 786440 | tf_op jit(solution)/shard_map/ppermute | solution.py:309
  63.0 0.1 collective-permute-start.11
  63.1 0.8 collective-permute-start.12
  63.9 0.4 collective-permute-done.10.refs_8_
  64.3 2.0 %collective-permute-start.13 = (bf16[32,64,128]{2,1,0:T(8,128)(2,1)S(1)}, bf16[32,64,128]{2,1,0:T(8,128)(2,1)S(1)}, u32[]{:S(2)}, u32[]{:S(2)}) collective-permute-start(bf16[32,64,128]{2,1,0:T(8,128)(2,1)S(1)} %all-to-all-done.1.qg_ref.refs_0_), channel_id=1, source_target_pairs={{0,3},{1,0},{2,1},{3,2},{4,7},{5,4},{6,5},{7,6},{8,11},{9,8},{10,9... | collective-permute-start | bytes 1572872 | tf_op jit(solution)/shard_map/ppermute | solution.py:313
  66.3 12.0 %query_side.1 = (bf16[32,32,128]{2,1,0:T(8,128)(2,1)}, f32[8,32,128]{2,1,0:T(8,128)}) custom-call(s32[40,128]{1,0:T(8,128)} %broadcast_select_fusion.tab, bf16[32,64,128]{2,1,0:T(8,128)(2,1)} %copy-done.3, bf16[32,64,128]{2,1,0:T(8,128)(2,1)} %copy-done.2, bf16[32,64,128]{2,1,0:T(8,128)(2,1)} %copy-done.6, bf16[32,64,128]{2,1,0:T(8,128)(2,1)} %copy-done.7, ...), custom_call_target="tpu_custom_call" | custom-call | flops 6000000000 | bytes 20971520 | tf_op jit(solution)/shard_map/query_side/pallas_call | solution.py:352
  78.4 0.0 copy-start.10
  78.4 0.1 collective-permute-start.14
  78.5 2.7 %collective-permute-start.15 = (bf16[16,64,128]{2,1,0:T(8,128)(2,1)S(1)}, bf16[16,64,128]{2,1,0:T(8,128)(2,1)S(1)}, u32[]{:S(2)}, u32[]{:S(2)}) collective-permute-start(bf16[16,64,128]{2,1,0:T(8,128)(2,1)S(1)} %slice.15), channel_id=1, source_target_pairs={{0,3},{1,0},{2,1},{3,2},{4,7},{5,4},{6,5},{7,6},{8,11},{9,8},{10,9... | collective-permute-start | bytes 786440 | tf_op jit(solution)/shard_map/ppermute | solution.py:319
  81.3 2.6 %collective-permute-start.16 = (bf16[32,64,128]{2,1,0:T(8,128)(2,1)S(1)}, bf16[32,64,128]{2,1,0:T(8,128)(2,1)S(1)}, u32[]{:S(2)}, u32[]{:S(2)}) collective-permute-start(bf16[32,64,128]{2,1,0:T(8,128)(2,1)S(1)} %copy-done.4), channel_id=1, source_target_pairs={{0,128},{128,0},{1,129},{129,1},{2,130},{130,2},{3,131},{131,3},{4... | collective-permute-start | bytes 1572872 | tf_op jit(solution)/shard_map/ppermute | solution.py:309
  83.8 0.1 collective-permute-start.17
  83.9 0.4 collective-permute-start.18
  84.3 8.3 %all_to_all.21.stats_ref = f32[8,32,128]{2,1,0:T(8,128)} all-to-all(f32[8,32,128]{2,1,0:T(8,128)S(1)} %copy-done.10), channel_id=1, replica_groups=mesh['bend'=2,'z'=8,'y'=4,'x'=4] {'bend','x'}, dimensions={0} | all-to-all | bytes 262144 | tf_op jit(solution)/shard_map/all_to_all | solution.py:365
  92.7 0.0 copy-start.17
  92.7 0.5 collective-permute-start.19
  93.1 0.1 collective-permute-start.20
  93.3 1.0 collective-permute-done.19.refs_8_
  94.3 0.4 collective-permute-done.20.refs_9_
  94.7 0.3 copy-done.18
  95.0 0.7 copy-done.19
  95.8 10.6 %key_side.1 = bf16[32,96,128]{2,1,0:T(8,128)(2,1)} custom-call(s32[40,128]{1,0:T(8,128)} %broadcast_select_fusion.tab, bf16[32,64,128]{2,1,0:T(8,128)(2,1)} %copy-done.2, bf16[32,32,128]{2,1,0:T(8,128)(2,1)} %get-tuple-element.35.dq_ref, f32[8,32,128]{2,1,0:T(8,128)} %all_to_all.21.stats_ref, bf16[32,64,128]{2,1,0:T(8,128)(2,1)} %copy-done.3, ...), custom_call_target="tpu_custom_call" | custom-call | flops 6000000000 | bytes 20971520 | tf_op jit(solution)/shard_map/key_side/pallas_call | solution.py:373
  106.4 26.8 %all_to_all.22.full_ref = bf16[32,96,128]{2,1,0:T(8,128)(2,1)S(1)} all-to-all(bf16[32,96,128]{2,1,0:T(8,128)(2,1)} %key_side.1), channel_id=1, replica_groups=mesh['bend'=2,'z'=8,'y'=4,'x'=4] {'z','y'}, dimensions={0} | all-to-all | bytes 1572864 | tf_op jit(solution)/shard_map/all_to_all | solution.py:384
  133.2 2.9 %collective-permute-start.21 = (bf16[16,96,128]{2,1,0:T(8,128)(2,1)S(1)}, bf16[16,96,128]{2,1,0:T(8,128)(2,1)S(1)}, u32[]{:S(2)}, u32[]{:S(2)}) collective-permute-start(bf16[16,96,128]{2,1,0:T(8,128)(2,1)S(1)} %constant_dynamic-slice_fusion), channel_id=1, source_target_pairs={{0,128},{128,0},{1,129},{129,1},{2,130},{130,2},{3,131},{131,3},{4... | collective-permute-start | bytes 1179656 | tf_op jit(solution)/shard_map/ppermute | solution.py:309
  136.1 1.3 collective-permute-done.21.other_ref
  137.4 1.1 unpack.1
  (57 shorter events, 0.3 us)
Async XLA Ops:
  4.0 6.1 %copy-start.5 = (bf16[32,64,128]{2,1,0:T(8,128)(2,1)S(1)}, bf16[32,64,128]{2,1,0:T(8,128)(2,1)}, u32[]{:S(2)}) copy-start(bf16[32,64,128]{2,1,0:T(8,128)(2,1)} %get-tuple-element.23) | copy-start | bytes 1572868
  4.0 6.1 %collective-permute-start = (bf16[16,64,128]{2,1,0:T(8,128)(2,1)}, bf16[16,64,128]{2,1,0:T(8,128)(2,1)S(1)}, u32[]{:S(2)}, u32[]{:S(2)}) collective-permute-start(bf16[16,64,128]{2,1,0:T(8,128)(2,1)} %get-tuple-element.24), channel_id=1, source_target_pairs={{0,128},{128,0},{1,129},{129,1},{2,130},{130,2},{3,131},{131,3},{4... | collective-permute-start | bytes 786440 | tf_op jit(solution)/shard_map/ppermute | solution.py:309
  10.2 26.2 %copy-start.20 = (bf16[16,64,128]{2,1,0:T(8,128)(2,1)S(1)}, bf16[16,64,128]{2,1,0:T(8,128)(2,1)}, u32[]{:S(2)}) copy-start(bf16[16,64,128]{2,1,0:T(8,128)(2,1)} %get-tuple-element.32) | copy-start | bytes 786436
  36.3 13.6 %copy-start.2 = (bf16[32,64,128]{2,1,0:T(8,128)(2,1)}, bf16[32,64,128]{2,1,0:T(8,128)(2,1)S(1)}, u32[]{:S(2)}) copy-start(bf16[32,64,128]{2,1,0:T(8,128)(2,1)S(1)} %all_to_all.20.refs_0_.kv_ref) | copy-start | bytes 1572868
  36.3 4.6 %collective-permute-start.4 = (bf16[16,64,128]{2,1,0:T(8,128)(2,1)S(1)}, bf16[16,64,128]{2,1,0:T(8,128)(2,1)S(1)}, u32[]{:S(2)}, u32[]{:S(2)}) collective-permute-start(bf16[16,64,128]{2,1,0:T(8,128)(2,1)S(1)} %copy-done.20), channel_id=1, source_target_pairs={{0,128},{128,0},{1,129},{129,1},{2,130},{130,2},{3,131},{131,3},{4... | collective-permute-start | bytes 786440 | tf_op jit(solution)/shard_map/ppermute | solution.py:309
  38.2 14.7 %collective-permute-start.1 = (bf16[32,64,128]{2,1,0:T(8,128)(2,1)S(1)}, bf16[32,64,128]{2,1,0:T(8,128)(2,1)S(1)}, u32[]{:S(2)}, u32[]{:S(2)}) collective-permute-start(bf16[32,64,128]{2,1,0:T(8,128)(2,1)S(1)} %all_to_all.20.refs_0_.kv_ref), channel_id=1, source_target_pairs={{0,1},{1,2},{2,3},{3,0},{4,5},{5,6},{6,7},{7,4},{8,9},{9,10},{10,1... | collective-permute-start | bytes 1572872 | tf_op jit(solution)/shard_map/ppermute | solution.py:313
  39.5 13.5 %collective-permute-start.2 = (bf16[32,64,128]{2,1,0:T(8,128)(2,1)S(1)}, bf16[32,64,128]{2,1,0:T(8,128)(2,1)S(1)}, u32[]{:S(2)}, u32[]{:S(2)}) collective-permute-start(bf16[32,64,128]{2,1,0:T(8,128)(2,1)S(1)} %all_to_all.20.refs_0_.kv_ref), channel_id=1, source_target_pairs={{0,3},{1,0},{2,1},{3,2},{4,7},{5,4},{6,5},{7,6},{8,11},{9,8},{10,9... | collective-permute-start | bytes 1572872 | tf_op jit(solution)/shard_map/ppermute | solution.py:313
  41.7 4.6 %copy-start = (s32[128,10]{0,1:T(8,128)S(1)}, s32[128,10]{0,1:T(8,128)}, u32[]{:S(2)}) copy-start(s32[128,10]{0,1:T(8,128)} %param.13) | copy-start | bytes 15364
  41.7 21.4 %all-to-all-start.1 = ((bf16[32,64,128]{2,1,0:T(8,128)(2,1)}), bf16[32,64,128]{2,1,0:T(8,128)(2,1)S(1)}, u32[]{:S(2)}, u32[]{:S(2)}) async-start(bf16[32,64,128]{2,1,0:T(8,128)(2,1)} %constant_dynamic-update-slice_fusion), calls=%async_computation.1 | async-start | bytes 1048576 | tf_op jit(solution)/shard_map/all_to_all | solution.py:336
  46.2 0.7 copy-start.1
  47.5 1.8 %collective-permute-start.3 = (s32[40,128]{1,0:T(8,128)S(1)}, s32[40,128]{1,0:T(8,128)S(1)}, u32[]{:S(2)}, u32[]{:S(2)}) collective-permute-start(s32[40,128]{1,0:T(8,128)S(1)} %tables.1), channel_id=1, source_target_pairs={{0,128},{128,0},{1,129},{129,1},{2,130},{130,2},{3,131},{131,3},{4... | collective-permute-start | bytes 61448 | tf_op jit(solution)/shard_map/ppermute | solution.py:309
  49.9 13.2 %collective-permute-start.7 = (bf16[32,64,128]{2,1,0:T(8,128)(2,1)S(1)}, bf16[32,64,128]{2,1,0:T(8,128)(2,1)S(1)}, u32[]{:S(2)}, u32[]{:S(2)}) collective-permute-start(bf16[32,64,128]{2,1,0:T(8,128)(2,1)S(1)} %all_to_all.20.refs_0_.kv_ref), channel_id=1, source_target_pairs={{0,128},{128,0},{1,129},{129,1},{2,130},{130,2},{3,131},{131,3},{4... | collective-permute-start | bytes 1572872 | tf_op jit(solution)/shard_map/ppermute | solution.py:309
  53.0 2.9 %copy-start.6 = (bf16[32,64,128]{2,1,0:T(8,128)(2,1)}, bf16[32,64,128]{2,1,0:T(8,128)(2,1)S(1)}, u32[]{:S(2)}) copy-start(bf16[32,64,128]{2,1,0:T(8,128)(2,1)S(1)} %collective-permute-done.1.refs_1_) | copy-start | bytes 1572868
  53.0 4.3 %copy-start.7 = (bf16[32,64,128]{2,1,0:T(8,128)(2,1)}, bf16[32,64,128]{2,1,0:T(8,128)(2,1)S(1)}, u32[]{:S(2)}) copy-start(bf16[32,64,128]{2,1,0:T(8,128)(2,1)S(1)} %collective-permute-done.2.refs_2_) | copy-start | bytes 1572868
  53.0 8.2 %collective-permute-start.5 = (bf16[16,64,128]{2,1,0:T(8,128)(2,1)S(1)}, bf16[16,64,128]{2,1,0:T(8,128)(2,1)S(1)}, u32[]{:S(2)}, u32[]{:S(2)}) collective-permute-start(bf16[16,64,128]{2,1,0:T(8,128)(2,1)S(1)} %slice.12), channel_id=1, source_target_pairs={{0,1},{1,2},{2,3},{3,0},{4,5},{5,6},{6,7},{7,4},{8,9},{9,10},{10,1... | collective-permute-start | bytes 786440 | tf_op jit(solution)/shard_map/ppermute | solution.py:318
  54.0 9.0 %collective-permute-start.6 = (bf16[16,64,128]{2,1,0:T(8,128)(2,1)S(1)}, bf16[16,64,128]{2,1,0:T(8,128)(2,1)}, u32[]{:S(2)}, u32[]{:S(2)}) collective-permute-start(bf16[16,64,128]{2,1,0:T(8,128)(2,1)S(1)} %slice.13), channel_id=1, source_target_pairs={{0,3},{1,0},{2,1},{3,2},{4,7},{5,4},{6,5},{7,6},{8,11},{9,8},{10,9... | collective-permute-start | bytes 786440 | tf_op jit(solution)/shard_map/ppermute | solution.py:319
  55.8 10.4 %collective-permute-start.8 = (bf16[32,64,128]{2,1,0:T(8,128)(2,1)S(1)}, bf16[32,64,128]{2,1,0:T(8,128)(2,1)}, u32[]{:S(2)}, u32[]{:S(2)}) collective-permute-start(bf16[32,64,128]{2,1,0:T(8,128)(2,1)S(1)} %collective-permute-done.1.refs_1_), channel_id=1, source_target_pairs={{0,128},{128,0},{1,129},{129,1},{2,130},{130,2},{3,131},{131,3},{4... | collective-permute-start | bytes 1572872 | tf_op jit(solution)/shard_map/ppermute | solution.py:309
  57.3 9.0 %collective-permute-start.9 = (bf16[32,64,128]{2,1,0:T(8,128)(2,1)S(1)}, bf16[32,64,128]{2,1,0:T(8,128)(2,1)}, u32[]{:S(2)}, u32[]{:S(2)}) collective-permute-start(bf16[32,64,128]{2,1,0:T(8,128)(2,1)S(1)} %collective-permute-done.2.refs_2_), channel_id=1, source_target_pairs={{0,128},{128,0},{1,129},{129,1},{2,130},{130,2},{3,131},{131,3},{4... | collective-permute-start | bytes 1572872 | tf_op jit(solution)/shard_map/ppermute | solution.py:309
  61.2 5.0 %copy-start.15 = (bf16[16,64,128]{2,1,0:T(8,128)(2,1)}, bf16[16,64,128]{2,1,0:T(8,128)(2,1)S(1)}, u32[]{:S(2)}) copy-start(bf16[16,64,128]{2,1,0:T(8,128)(2,1)S(1)} %collective-permute-done.5.refs_3_) | copy-start | bytes 786436
  61.2 3.1 %collective-permute-start.10 = (bf16[16,64,128]{2,1,0:T(8,128)(2,1)S(1)}, bf16[16,64,128]{2,1,0:T(8,128)(2,1)}, u32[]{:S(2)}, u32[]{:S(2)}) collective-permute-start(bf16[16,64,128]{2,1,0:T(8,128)(2,1)S(1)} %collective-permute-done.5.refs_3_), channel_id=1, source_target_pairs={{0,128},{128,0},{1,129},{129,1},{2,130},{130,2},{3,131},{131,3},{4... | collective-permute-start | bytes 786440 | tf_op jit(solution)/shard_map/ppermute | solution.py:309
  63.0 3.3 %collective-permute-start.11 = (bf16[16,64,128]{2,1,0:T(8,128)(2,1)}, bf16[16,64,128]{2,1,0:T(8,128)(2,1)}, u32[]{:S(2)}, u32[]{:S(2)}) collective-permute-start(bf16[16,64,128]{2,1,0:T(8,128)(2,1)} %collective-permute-done.6.refs_4_), channel_id=1, source_target_pairs={{0,128},{128,0},{1,129},{129,1},{2,130},{130,2},{3,131},{131,3},{4... | collective-permute-start | bytes 786440 | tf_op jit(solution)/shard_map/ppermute | solution.py:309
  63.1 3.2 %copy-start.3 = (bf16[32,64,128]{2,1,0:T(8,128)(2,1)}, bf16[32,64,128]{2,1,0:T(8,128)(2,1)S(1)}, u32[]{:S(2)}) copy-start(bf16[32,64,128]{2,1,0:T(8,128)(2,1)S(1)} %all-to-all-done.1.qg_ref.refs_0_) | copy-start | bytes 1572868
  63.1 3.2 %copy-start.11 = (bf16[32,64,128]{2,1,0:T(8,128)(2,1)}, bf16[32,64,128]{2,1,0:T(8,128)(2,1)S(1)}, u32[]{:S(2)}) copy-start(bf16[32,64,128]{2,1,0:T(8,128)(2,1)S(1)} %collective-permute-done.7.refs_5_) | copy-start | bytes 1572868
  63.1 15.2 %collective-permute-start.12 = (bf16[32,64,128]{2,1,0:T(8,128)(2,1)S(1)}, bf16[32,64,128]{2,1,0:T(8,128)(2,1)S(1)}, u32[]{:S(2)}, u32[]{:S(2)}) collective-permute-start(bf16[32,64,128]{2,1,0:T(8,128)(2,1)S(1)} %all-to-all-done.1.qg_ref.refs_0_), channel_id=1, source_target_pairs={{0,1},{1,2},{2,3},{3,0},{4,5},{5,6},{6,7},{7,4},{8,9},{9,10},{10,1... | collective-permute-start | bytes 1572872 | tf_op jit(solution)/shard_map/ppermute | solution.py:313
  64.3 14.1 %collective-permute-start.13 = (bf16[32,64,128]{2,1,0:T(8,128)(2,1)S(1)}, bf16[32,64,128]{2,1,0:T(8,128)(2,1)S(1)}, u32[]{:S(2)}, u32[]{:S(2)}) collective-permute-start(bf16[32,64,128]{2,1,0:T(8,128)(2,1)S(1)} %all-to-all-done.1.qg_ref.refs_0_), channel_id=1, source_target_pairs={{0,3},{1,0},{2,1},{3,2},{4,7},{5,4},{6,5},{7,6},{8,11},{9,8},{10,9... | collective-permute-start | bytes 1572872 | tf_op jit(solution)/shard_map/ppermute | solution.py:313
  78.3 5.5 %copy-start.8 = (bf16[32,64,128]{2,1,0:T(8,128)(2,1)}, bf16[32,64,128]{2,1,0:T(8,128)(2,1)S(1)}, u32[]{:S(2)}) copy-start(bf16[32,64,128]{2,1,0:T(8,128)(2,1)S(1)} %collective-permute-done.12.refs_1_) | copy-start | bytes 1572868
  78.4 5.6 %copy-start.9 = (bf16[32,64,128]{2,1,0:T(8,128)(2,1)}, bf16[32,64,128]{2,1,0:T(8,128)(2,1)S(1)}, u32[]{:S(2)}) copy-start(bf16[32,64,128]{2,1,0:T(8,128)(2,1)S(1)} %collective-permute-done.13.refs_2_) | copy-start | bytes 1572868
  78.4 2.9 %copy-start.4 = (bf16[32,64,128]{2,1,0:T(8,128)(2,1)S(1)}, bf16[32,64,128]{2,1,0:T(8,128)(2,1)}, u32[]{:S(2)}) copy-start(bf16[32,64,128]{2,1,0:T(8,128)(2,1)} %copy-done.3) | copy-start | bytes 1572868
  78.4 6.0 %copy-start.10 = (f32[8,32,128]{2,1,0:T(8,128)S(1)}, f32[8,32,128]{2,1,0:T(8,128)}, u32[]{:S(2)}) copy-start(f32[8,32,128]{2,1,0:T(8,128)} %get-tuple-element.37) | copy-start | bytes 393220
  78.4 14.2 %collective-permute-start.14 = (bf16[16,64,128]{2,1,0:T(8,128)(2,1)S(1)}, bf16[16,64,128]{2,1,0:T(8,128)(2,1)S(1)}, u32[]{:S(2)}, u32[]{:S(2)}) collective-permute-start(bf16[16,64,128]{2,1,0:T(8,128)(2,1)S(1)} %slice.14), channel_id=1, source_target_pairs={{0,1},{1,2},{2,3},{3,0},{4,5},{5,6},{6,7},{7,4},{8,9},{9,10},{10,1... | collective-permute-start | bytes 786440 | tf_op jit(solution)/shard_map/ppermute | solution.py:318
  78.5 14.1 %collective-permute-start.15 = (bf16[16,64,128]{2,1,0:T(8,128)(2,1)S(1)}, bf16[16,64,128]{2,1,0:T(8,128)(2,1)S(1)}, u32[]{:S(2)}, u32[]{:S(2)}) collective-permute-start(bf16[16,64,128]{2,1,0:T(8,128)(2,1)S(1)} %slice.15), channel_id=1, source_target_pairs={{0,3},{1,0},{2,1},{3,2},{4,7},{5,4},{6,5},{7,6},{8,11},{9,8},{10,9... | collective-permute-start | bytes 786440 | tf_op jit(solution)/shard_map/ppermute | solution.py:319
  81.3 12.0 %collective-permute-start.16 = (bf16[32,64,128]{2,1,0:T(8,128)(2,1)S(1)}, bf16[32,64,128]{2,1,0:T(8,128)(2,1)S(1)}, u32[]{:S(2)}, u32[]{:S(2)}) collective-permute-start(bf16[32,64,128]{2,1,0:T(8,128)(2,1)S(1)} %copy-done.4), channel_id=1, source_target_pairs={{0,128},{128,0},{1,129},{129,1},{2,130},{130,2},{3,131},{131,3},{4... | collective-permute-start | bytes 1572872 | tf_op jit(solution)/shard_map/ppermute | solution.py:309
  83.8 9.4 %collective-permute-start.17 = (bf16[32,64,128]{2,1,0:T(8,128)(2,1)S(1)}, bf16[32,64,128]{2,1,0:T(8,128)(2,1)S(1)}, u32[]{:S(2)}, u32[]{:S(2)}) collective-permute-start(bf16[32,64,128]{2,1,0:T(8,128)(2,1)S(1)} %collective-permute-done.12.refs_1_), channel_id=1, source_target_pairs={{0,128},{128,0},{1,129},{129,1},{2,130},{130,2},{3,131},{131,3},{4... | collective-permute-start | bytes 1572872 | tf_op jit(solution)/shard_map/ppermute | solution.py:309
  83.9 9.4 %collective-permute-start.18 = (bf16[32,64,128]{2,1,0:T(8,128)(2,1)S(1)}, bf16[32,64,128]{2,1,0:T(8,128)(2,1)S(1)}, u32[]{:S(2)}, u32[]{:S(2)}) collective-permute-start(bf16[32,64,128]{2,1,0:T(8,128)(2,1)S(1)} %collective-permute-done.13.refs_2_), channel_id=1, source_target_pairs={{0,128},{128,0},{1,129},{129,1},{2,130},{130,2},{3,131},{131,3},{4... | collective-permute-start | bytes 1572872 | tf_op jit(solution)/shard_map/ppermute | solution.py:309
  92.6 3.1 %copy-start.16 = (bf16[16,64,128]{2,1,0:T(8,128)(2,1)}, bf16[16,64,128]{2,1,0:T(8,128)(2,1)S(1)}, u32[]{:S(2)}) copy-start(bf16[16,64,128]{2,1,0:T(8,128)(2,1)S(1)} %collective-permute-done.14.refs_3_) | copy-start | bytes 786436
  92.7 3.1 %copy-start.17 = (bf16[16,64,128]{2,1,0:T(8,128)(2,1)}, bf16[16,64,128]{2,1,0:T(8,128)(2,1)S(1)}, u32[]{:S(2)}) copy-start(bf16[16,64,128]{2,1,0:T(8,128)(2,1)S(1)} %collective-permute-done.15.refs_4_) | copy-start | bytes 786436
  92.7 1.6 %collective-permute-start.19 = (bf16[16,64,128]{2,1,0:T(8,128)(2,1)S(1)}, bf16[16,64,128]{2,1,0:T(8,128)(2,1)S(1)}, u32[]{:S(2)}, u32[]{:S(2)}) collective-permute-start(bf16[16,64,128]{2,1,0:T(8,128)(2,1)S(1)} %collective-permute-done.14.refs_3_), channel_id=1, source_target_pairs={{0,128},{128,0},{1,129},{129,1},{2,130},{130,2},{3,131},{131,3},{4... | collective-permute-start | bytes 786440 | tf_op jit(solution)/shard_map/ppermute | solution.py:309
  93.1 1.5 %collective-permute-start.20 = (bf16[16,64,128]{2,1,0:T(8,128)(2,1)S(1)}, bf16[16,64,128]{2,1,0:T(8,128)(2,1)S(1)}, u32[]{:S(2)}, u32[]{:S(2)}) collective-permute-start(bf16[16,64,128]{2,1,0:T(8,128)(2,1)S(1)} %collective-permute-done.15.refs_4_), channel_id=1, source_target_pairs={{0,128},{128,0},{1,129},{129,1},{2,130},{130,2},{3,131},{131,3},{4... | collective-permute-start | bytes 786440 | tf_op jit(solution)/shard_map/ppermute | solution.py:309
  93.3 2.5 %copy-start.12 = (bf16[32,64,128]{2,1,0:T(8,128)(2,1)}, bf16[32,64,128]{2,1,0:T(8,128)(2,1)S(1)}, u32[]{:S(2)}) copy-start(bf16[32,64,128]{2,1,0:T(8,128)(2,1)S(1)} %collective-permute-done.16.refs_5_) | copy-start | bytes 1572868
  93.3 2.5 %copy-start.13 = (bf16[32,64,128]{2,1,0:T(8,128)(2,1)}, bf16[32,64,128]{2,1,0:T(8,128)(2,1)S(1)}, u32[]{:S(2)}) copy-start(bf16[32,64,128]{2,1,0:T(8,128)(2,1)S(1)} %collective-permute-done.17.refs_6_) | copy-start | bytes 1572868
  93.3 2.5 %copy-start.14 = (bf16[32,64,128]{2,1,0:T(8,128)(2,1)}, bf16[32,64,128]{2,1,0:T(8,128)(2,1)S(1)}, u32[]{:S(2)}) copy-start(bf16[32,64,128]{2,1,0:T(8,128)(2,1)S(1)} %collective-permute-done.18.refs_7_) | copy-start | bytes 1572868
  94.3 0.7 copy-start.18
  95.0 0.7 copy-start.19
  133.2 4.2 %collective-permute-start.21 = (bf16[16,96,128]{2,1,0:T(8,128)(2,1)S(1)}, bf16[16,96,128]{2,1,0:T(8,128)(2,1)S(1)}, u32[]{:S(2)}, u32[]{:S(2)}) collective-permute-start(bf16[16,96,128]{2,1,0:T(8,128)(2,1)S(1)} %constant_dynamic-slice_fusion), channel_id=1, source_target_pairs={{0,128},{128,0},{1,129},{129,1},{2,130},{130,2},{3,131},{131,3},{4... | collective-permute-start | bytes 1179656 | tf_op jit(solution)/shard_map/ppermute | solution.py:309

commit v4 on v3

--- a/solution.py
+++ b/solution.py
@@ -233,9 +233,7 @@
             dq_ref[ss[u]] = jnp.concatenate([dq[: HALF // 2, :HD], dq[HALF // 2 :, :HD]], axis=1)
             lse = tops[u] + jnp.log2(total)
             row = jnp.where(lane == sub, lse, 0.0) + jnp.where(lane == sub + HALF, delta, 0.0)
-            row = jnp.sum(row, axis=0, keepdims=True)
-            for i in range(2 * NX):
-                row_ref[i, pl.ds(ss[u], 1), :] = row
+            row_ref[pl.ds(ss[u], 1), :] = jnp.sum(row, axis=0, keepdims=True)
 
         skewed((products, weights, gradient))
         return carry
@@ -248,7 +246,7 @@
     c, x, copies = load_pieces(pieces, held, sems)
     lane_n = lax.broadcasted_iota(jnp.int32, (NSRC, 128), 1)
     for i in range(NX):
-        a, b = stats_ref[i], stats_ref[NX + i]
+        a, b = stats_ref[i, c], stats_ref[i, 1 - c]
         lse = jnp.where(lane_n < HALF, a, pltpu.roll(b, HALF, 1))
         delta = jnp.where(lane_n < HALF, pltpu.roll(a, HALF, 1), b)
         for s in range(NSRC):
@@ -353,7 +351,7 @@
         query_kernel,
         out_shape=(
             jax.ShapeDtypeStruct((NSRC, HALF // 2, 128), BF),
-            jax.ShapeDtypeStruct((2 * NX, NSRC, 128), F32),
+            jax.ShapeDtypeStruct((NSRC, 128), F32),
         ),
         in_specs=[SMEM, VMEM] + [ANY] * 10,
         out_specs=(VMEM, VMEM),
@@ -362,7 +360,8 @@
         cost_estimate=cost(6 * 10**9, 20 * 2**20),
         name="query_side",
     )(tab, qg, *kv_pieces)
-    stats = lax.all_to_all(rows, ("bend", "x"), 0, 0, tiled=True)
+    both = jnp.stack([rows, swap(rows)])
+    stats = lax.all_to_all(jnp.broadcast_to(both, (NX,) + both.shape), "x", 0, 0, tiled=True)
 
     qg_first = lax.optimization_barrier(qg_first + (rows,))[:2]
     qg_pieces = second_step(qg, *qg_first)

time: 139 us -> 139 us (level)
    ppermute x14 -> x15, starting transfers between devices: 16.5 us -> 17.6 us  [swap(): return lax.ppermute(a, 'bend', SWAP)]
    ppermute x14 -> x15, waiting for transfers between devices: 3.99 us -> 3.79 us  [swap(): return lax.ppermute(a, 'bend', SWAP)]
  transfers between devices with their start and end apart: 23 -> 24, of which waited for: 7 -> 7; matrix products, arithmetic and copies ran while one was open for 1% -> 1% of each run, Pallas kernels for 11% -> 11%
where the time goes in v4:
time: 139 us
  blocking collectives  61 us (44%)
  starting transfers between devices  33.2 us (24%)
  Pallas kernels  29.8 us (21%)
  waiting for transfers between devices  10.4 us (7%)
  local copies, waits for them, and re-layouts  2.35 us (2%)
  between operations  1.59 us (1%)
    all_to_all x1, blocking collectives, per_device(): back = lax.all_to_all(grads, ('z', 'y'), 0, 0, tiled=True)  26.7 us
    all_to_all x1, blocking collectives, per_device(): kv = lax.all_to_all(kv_out, ('z', 'y'), 0, 0, tiled=True)  26.1 us
    ppermute x15, starting transfers between devices, swap(): return lax.ppermute(a, 'bend', SWAP)  17.6 us
    pallas_call x1, Pallas kernels, per_device(): pl.pallas_call(query_kernel, out_shape=(jax.ShapeDtypeStruct((NSRC, HALF...  12 us
    pallas_call x1, Pallas kernels, per_device(): pl.pallas_call(key_kernel, out_shape=jax.ShapeDtypeStruct((NSRC, HALF + H...  10.6 us
    all_to_all x1, blocking collectives, per_device(): lax.all_to_all(jnp.broadcast_to(both, (NX,) + both.shape), 'x', 0, 0, til...  8.17 us
    pallas_call x2, Pallas kernels, pack(): pl.pallas_call(functools.partial(pack_kernel, masked), out_shape=(jax.Sha...  5.46 us
    ppermute x4, starting transfers between devices, first_step(): return (lax.ppermute(own, 'x', ring(1)), lax.ppermute(own, 'x', ring(-1)))  5.43 us
  transfers between devices with their start and end apart: 24, of which 7 were waited for; matrix products, arithmetic and copies ran while one was open for 1% of the time, Pallas kernels for 11%

profile of v4, /device:TPU:1, one launch (start us, length us, event | category | flops | bytes accessed | tf_op | source)
XLA Modules:
  0.0 138.9 jit_solution(10071976520954102003)
XLA Ops:
  1.3 2.7 %pack_kv.1 = (bf16[16,64,128]{2,1,0:T(8,128)(2,1)}, bf16[32,64,128]{2,1,0:T(8,128)(2,1)}) custom-call(s32[128]{0:T(128)} %ids.3, s32[1]{0:T(128)S(6)} %copy.12.count, bf16[128,1024]{1,0:T(8,128)(2,1)} %a_ref.2, bf16[128,1024]{1,0:T(8,128)(2,1)} %b_ref.2), custom_call_target="tpu_custom_call" | custom-call | bytes 1048576 | tf_op jit(solution)/shard_map/pack_kv/pallas_call | solution.py:95
  4.0 3.3 %collective-permute-start = (bf16[16,64,128]{2,1,0:T(8,128)(2,1)}, bf16[16,64,128]{2,1,0:T(8,128)(2,1)S(1)}, u32[]{:S(2)}, u32[]{:S(2)}) collective-permute-start(bf16[16,64,128]{2,1,0:T(8,128)(2,1)} %get-tuple-element.24), channel_id=1, source_target_pairs={{0,128},{128,0},{1,129},{129,1},{2,130},{130,2},{3,131},{131,3},{4... | collective-permute-start | bytes 786440 | tf_op jit(solution)/shard_map/ppermute | solution.py:307
  7.4 2.7 %pack_qg.1 = (bf16[16,64,128]{2,1,0:T(8,128)(2,1)}, bf16[32,64,128]{2,1,0:T(8,128)(2,1)}) custom-call(s32[128]{0:T(128)} %ids.3, s32[1]{0:T(128)S(6)} %copy.12.count, bf16[128,1024]{1,0:T(8,128)(2,1)} %a_ref.3, bf16[128,1024]{1,0:T(8,128)(2,1)} %b_ref.3), custom_call_target="tpu_custom_call" | custom-call | bytes 1048576 | tf_op jit(solution)/shard_map/pack_qg/pallas_call | solution.py:95
  10.2 0.0 copy-start.20
  10.2 26.1 %all_to_all.20.refs_0_.kv_ref = bf16[32,64,128]{2,1,0:T(8,128)(2,1)S(1)} all-to-all(bf16[32,64,128]{2,1,0:T(8,128)(2,1)S(1)} %constant_dynamic-update-slice_fusion.1), channel_id=1, replica_groups=mesh['bend'=2,'z'=8,'y'=4,'x'=4] {'z','y'}, dimensions={0} | all-to-all | bytes 1048576 | tf_op jit(solution)/shard_map/all_to_all | solution.py:331
  36.3 1.9 %collective-permute-start.4 = (bf16[16,64,128]{2,1,0:T(8,128)(2,1)S(1)}, bf16[16,64,128]{2,1,0:T(8,128)(2,1)S(1)}, u32[]{:S(2)}, u32[]{:S(2)}) collective-permute-start(bf16[16,64,128]{2,1,0:T(8,128)(2,1)S(1)} %copy-done.20), channel_id=1, source_target_pairs={{0,128},{128,0},{1,129},{129,1},{2,130},{130,2},{3,131},{131,3},{4... | collective-permute-start | bytes 786440 | tf_op jit(solution)/shard_map/ppermute | solution.py:307
  38.2 1.2 collective-permute-start.1
  39.5 1.5 %collective-permute-start.2 = (bf16[32,64,128]{2,1,0:T(8,128)(2,1)S(1)}, bf16[32,64,128]{2,1,0:T(8,128)(2,1)S(1)}, u32[]{:S(2)}, u32[]{:S(2)}) collective-permute-start(bf16[32,64,128]{2,1,0:T(8,128)(2,1)S(1)} %all_to_all.20.refs_0_.kv_ref), channel_id=1, source_target_pairs={{0,3},{1,0},{2,1},{3,2},{4,7},{5,4},{6,5},{7,6},{8,11},{9,8},{10,9... | collective-permute-start | bytes 1572872 | tf_op jit(solution)/shard_map/ppermute | solution.py:311
  40.9 0.8 constant_dynamic-update-slice_fusion
  41.7 4.5 %all-to-all-start.1 = ((bf16[32,64,128]{2,1,0:T(8,128)(2,1)}), bf16[32,64,128]{2,1,0:T(8,128)(2,1)S(1)}, u32[]{:S(2)}, u32[]{:S(2)}) async-start(bf16[32,64,128]{2,1,0:T(8,128)(2,1)} %constant_dynamic-update-slice_fusion), calls=%async_computation.1 | async-start | bytes 1048576 | tf_op jit(solution)/shard_map/all_to_all | solution.py:334
  46.3 0.0 copy-start.1
  46.3 0.6 copy-done.1
  46.9 0.6 tables.1
  47.5 1.0 collective-permute-start.3
  48.5 0.8 collective-permute-done.3
  49.3 0.6 broadcast_select_fusion.tab
  49.9 0.3 collective-permute-start.7
  50.3 2.7 %collective-permute-done.1.refs_1_ = bf16[32,64,128]{2,1,0:T(8,128)(2,1)S(1)} collective-permute-done((bf16[32,64,128]{2,1,0:T(8,128)(2,1)S(1)}, bf16[32,64,128]{2,1,0:T(8,128)(2,1)S(1)}, u32[]{:S(2)}, u32[]{:S(2)}) %collective-permute-start.1) | collective-permute-done | bytes 524320 | tf_op jit(solution)/shard_map/ppermute | solution.py:311
  53.0 1.0 collective-permute-start.5
  54.0 1.9 %collective-permute-start.6 = (bf16[16,64,128]{2,1,0:T(8,128)(2,1)S(1)}, bf16[16,64,128]{2,1,0:T(8,128)(2,1)}, u32[]{:S(2)}, u32[]{:S(2)}) collective-permute-start(bf16[16,64,128]{2,1,0:T(8,128)(2,1)S(1)} %slice.13), channel_id=1, source_target_pairs={{0,3},{1,0},{2,1},{3,2},{4,7},{5,4},{6,5},{7,6},{8,11},{9,8},{10,9... | collective-permute-start | bytes 786440 | tf_op jit(solution)/shard_map/ppermute | solution.py:317
  55.8 1.4 %collective-permute-start.8 = (bf16[32,64,128]{2,1,0:T(8,128)(2,1)S(1)}, bf16[32,64,128]{2,1,0:T(8,128)(2,1)}, u32[]{:S(2)}, u32[]{:S(2)}) collective-permute-start(bf16[32,64,128]{2,1,0:T(8,128)(2,1)S(1)} %collective-permute-done.1.refs_1_), channel_id=1, source_target_pairs={{0,128},{128,0},{1,129},{129,1},{2,130},{130,2},{3,131},{131,3},{4... | collective-permute-start | bytes 1572872 | tf_op jit(solution)/shard_map/ppermute | solution.py:307
  57.3 0.1 collective-permute-start.9
  57.4 3.9 %collective-permute-done.5.refs_3_ = bf16[16,64,128]{2,1,0:T(8,128)(2,1)S(1)} collective-permute-done((bf16[16,64,128]{2,1,0:T(8,128)(2,1)S(1)}, bf16[16,64,128]{2,1,0:T(8,128)(2,1)S(1)}, u32[]{:S(2)}, u32[]{:S(2)}) %collective-permute-start.5) | collective-permute-done | bytes 262176 | tf_op jit(solution)/shard_map/ppermute | solution.py:316
  61.2 1.8 %collective-permute-start.10 = (bf16[16,64,128]{2,1,0:T(8,128)(2,1)S(1)}, bf16[16,64,128]{2,1,0:T(8,128)(2,1)}, u32[]{:S(2)}, u32[]{:S(2)}) collective-permute-start(bf16[16,64,128]{2,1,0:T(8,128)(2,1)S(1)} %collective-permute-done.5.refs_3_), channel_id=1, source_target_pairs={{0,128},{128,0},{1,129},{129,1},{2,130},{130,2},{3,131},{131,3},{4... | collective-permute-start | bytes 786440 | tf_op jit(solution)/shard_map/ppermute | solution.py:307
  63.0 0.1 collective-permute-start.11
  63.1 0.8 collective-permute-start.12
  63.9 0.4 collective-permute-done.10.refs_8_
  64.3 2.0 %collective-permute-start.13 = (bf16[32,64,128]{2,1,0:T(8,128)(2,1)S(1)}, bf16[32,64,128]{2,1,0:T(8,128)(2,1)S(1)}, u32[]{:S(2)}, u32[]{:S(2)}) collective-permute-start(bf16[32,64,128]{2,1,0:T(8,128)(2,1)S(1)} %all-to-all-done.1.qg_ref.refs_0_), channel_id=1, source_target_pairs={{0,3},{1,0},{2,1},{3,2},{4,7},{5,4},{6,5},{7,6},{8,11},{9,8},{10,9... | collective-permute-start | bytes 1572872 | tf_op jit(solution)/shard_map/ppermute | solution.py:311
  66.3 12.0 %query_side.1 = (bf16[32,32,128]{2,1,0:T(8,128)(2,1)}, f32[32,128]{1,0:T(8,128)}) custom-call(s32[40,128]{1,0:T(8,128)} %broadcast_select_fusion.tab, bf16[32,64,128]{2,1,0:T(8,128)(2,1)} %copy-done.3, bf16[32,64,128]{2,1,0:T(8,128)(2,1)} %copy-done.2, bf16[32,64,128]{2,1,0:T(8,128)(2,1)} %copy-done.6, bf16[32,64,128]{2,1,0:T(8,128)(2,1)} %copy-done.7, ...), custom_call_target="tpu_custom_call" | custom-call | flops 6000000000 | bytes 20971520 | tf_op jit(solution)/shard_map/query_side/pallas_call | solution.py:350
  78.3 2.1 %collective-permute-start.16 = (f32[32,128]{1,0:T(8,128)}, f32[32,128]{1,0:T(8,128)S(1)}, u32[]{:S(2)}, u32[]{:S(2)}) collective-permute-start(f32[32,128]{1,0:T(8,128)} %get-tuple-element.37), channel_id=1, source_target_pairs={{0,128},{128,0},{1,129},{129,1},{2,130},{130,2},{3,131},{131,3},{4... | collective-permute-start | bytes 49160 | tf_op jit(solution)/shard_map/ppermute | solution.py:307
  80.5 0.0 copy-start.10
  80.5 0.1 collective-permute-start.14
  80.6 2.7 %collective-permute-start.15 = (bf16[16,64,128]{2,1,0:T(8,128)(2,1)S(1)}, bf16[16,64,128]{2,1,0:T(8,128)(2,1)S(1)}, u32[]{:S(2)}, u32[]{:S(2)}) collective-permute-start(bf16[16,64,128]{2,1,0:T(8,128)(2,1)S(1)} %slice.15), channel_id=1, source_target_pairs={{0,3},{1,0},{2,1},{3,2},{4,7},{5,4},{6,5},{7,6},{8,11},{9,8},{10,9... | collective-permute-start | bytes 786440 | tf_op jit(solution)/shard_map/ppermute | solution.py:317
  83.3 0.6 collective-permute-start.17
  83.9 0.0 collective-permute-start.18
  83.9 0.5 collective-permute-start.19
  84.5 8.2 %all_to_all.21.stats_ref = f32[4,2,32,128]{3,2,1,0:T(8,128)} all-to-all(f32[4,2,32,128]{3,2,1,0:T(8,128)S(1)} %broadcast_in_dim.7), channel_id=1, replica_groups=mesh['bend'=2,'z'=8,'y'=4,'x'=4] {'x'}, dimensions={0} | all-to-all | bytes 262144 | tf_op jit(solution)/shard_map/all_to_all | solution.py:364
  92.7 0.0 copy-start.17
  92.7 1.2 collective-permute-start.20
  93.9 0.3 collective-permute-start.21
  94.2 0.8 collective-permute-done.20.refs_8_
  95.0 0.4 collective-permute-done.21.refs_9_
  95.4 0.7 copy-done.19
  96.2 10.6 %key_side.1 = bf16[32,96,128]{2,1,0:T(8,128)(2,1)} custom-call(s32[40,128]{1,0:T(8,128)} %broadcast_select_fusion.tab, bf16[32,64,128]{2,1,0:T(8,128)(2,1)} %copy-done.2, bf16[32,32,128]{2,1,0:T(8,128)(2,1)} %get-tuple-element.35.dq_ref, f32[4,2,32,128]{3,2,1,0:T(8,128)} %all_to_all.21.stats_ref, bf16[32,64,128]{2,1,0:T(8,128)(2,1)} %copy-done.3, ...), custom_call_target="tpu_custom_call" | custom-call | flops 6000000000 | bytes 20971520 | tf_op jit(solution)/shard_map/key_side/pallas_call | solution.py:372
  106.8 26.7 %all_to_all.22.full_ref = bf16[32,96,128]{2,1,0:T(8,128)(2,1)S(1)} all-to-all(bf16[32,96,128]{2,1,0:T(8,128)(2,1)} %key_side.1), channel_id=1, replica_groups=mesh['bend'=2,'z'=8,'y'=4,'x'=4] {'z','y'}, dimensions={0} | all-to-all | bytes 1572864 | tf_op jit(solution)/shard_map/all_to_all | solution.py:383
  133.5 2.9 %collective-permute-start.22 = (bf16[16,96,128]{2,1,0:T(8,128)(2,1)S(1)}, bf16[16,96,128]{2,1,0:T(8,128)(2,1)S(1)}, u32[]{:S(2)}, u32[]{:S(2)}) collective-permute-start(bf16[16,96,128]{2,1,0:T(8,128)(2,1)S(1)} %constant_dynamic-slice_fusion), channel_id=1, source_target_pairs={{0,128},{128,0},{1,129},{129,1},{2,130},{130,2},{3,131},{131,3},{4... | collective-permute-start | bytes 1179656 | tf_op jit(solution)/shard_map/ppermute | solution.py:307
  136.4 1.3 collective-permute-done.22.other_ref
  137.8 1.1 unpack.1
  (61 shorter events, 0.3 us)
Async XLA Ops:
  4.0 6.1 %copy-start.5 = (bf16[32,64,128]{2,1,0:T(8,128)(2,1)S(1)}, bf16[32,64,128]{2,1,0:T(8,128)(2,1)}, u32[]{:S(2)}) copy-start(bf16[32,64,128]{2,1,0:T(8,128)(2,1)} %get-tuple-element.23) | copy-start | bytes 1572868
  4.0 6.1 %collective-permute-start = (bf16[16,64,128]{2,1,0:T(8,128)(2,1)}, bf16[16,64,128]{2,1,0:T(8,128)(2,1)S(1)}, u32[]{:S(2)}, u32[]{:S(2)}) collective-permute-start(bf16[16,64,128]{2,1,0:T(8,128)(2,1)} %get-tuple-element.24), channel_id=1, source_target_pairs={{0,128},{128,0},{1,129},{129,1},{2,130},{130,2},{3,131},{131,3},{4... | collective-permute-start | bytes 786440 | tf_op jit(solution)/shard_map/ppermute | solution.py:307
  10.2 26.2 %copy-start.20 = (bf16[16,64,128]{2,1,0:T(8,128)(2,1)S(1)}, bf16[16,64,128]{2,1,0:T(8,128)(2,1)}, u32[]{:S(2)}) copy-start(bf16[16,64,128]{2,1,0:T(8,128)(2,1)} %get-tuple-element.32) | copy-start | bytes 786436
  36.3 13.6 %copy-start.2 = (bf16[32,64,128]{2,1,0:T(8,128)(2,1)}, bf16[32,64,128]{2,1,0:T(8,128)(2,1)S(1)}, u32[]{:S(2)}) copy-start(bf16[32,64,128]{2,1,0:T(8,128)(2,1)S(1)} %all_to_all.20.refs_0_.kv_ref) | copy-start | bytes 1572868
  36.3 4.6 %collective-permute-start.4 = (bf16[16,64,128]{2,1,0:T(8,128)(2,1)S(1)}, bf16[16,64,128]{2,1,0:T(8,128)(2,1)S(1)}, u32[]{:S(2)}, u32[]{:S(2)}) collective-permute-start(bf16[16,64,128]{2,1,0:T(8,128)(2,1)S(1)} %copy-done.20), channel_id=1, source_target_pairs={{0,128},{128,0},{1,129},{129,1},{2,130},{130,2},{3,131},{131,3},{4... | collective-permute-start | bytes 786440 | tf_op jit(solution)/shard_map/ppermute | solution.py:307
  38.2 14.7 %collective-permute-start.1 = (bf16[32,64,128]{2,1,0:T(8,128)(2,1)S(1)}, bf16[32,64,128]{2,1,0:T(8,128)(2,1)S(1)}, u32[]{:S(2)}, u32[]{:S(2)}) collective-permute-start(bf16[32,64,128]{2,1,0:T(8,128)(2,1)S(1)} %all_to_all.20.refs_0_.kv_ref), channel_id=1, source_target_pairs={{0,1},{1,2},{2,3},{3,0},{4,5},{5,6},{6,7},{7,4},{8,9},{9,10},{10,1... | collective-permute-start | bytes 1572872 | tf_op jit(solution)/shard_map/ppermute | solution.py:311
  39.5 13.5 %collective-permute-start.2 = (bf16[32,64,128]{2,1,0:T(8,128)(2,1)S(1)}, bf16[32,64,128]{2,1,0:T(8,128)(2,1)S(1)}, u32[]{:S(2)}, u32[]{:S(2)}) collective-permute-start(bf16[32,64,128]{2,1,0:T(8,128)(2,1)S(1)} %all_to_all.20.refs_0_.kv_ref), channel_id=1, source_target_pairs={{0,3},{1,0},{2,1},{3,2},{4,7},{5,4},{6,5},{7,6},{8,11},{9,8},{10,9... | collective-permute-start | bytes 1572872 | tf_op jit(solution)/shard_map/ppermute | solution.py:311
  41.7 4.6 %copy-start = (s32[128,10]{0,1:T(8,128)S(1)}, s32[128,10]{0,1:T(8,128)}, u32[]{:S(2)}) copy-start(s32[128,10]{0,1:T(8,128)} %param.13) | copy-start | bytes 15364
  41.7 21.4 %all-to-all-start.1 = ((bf16[32,64,128]{2,1,0:T(8,128)(2,1)}), bf16[32,64,128]{2,1,0:T(8,128)(2,1)S(1)}, u32[]{:S(2)}, u32[]{:S(2)}) async-start(bf16[32,64,128]{2,1,0:T(8,128)(2,1)} %constant_dynamic-update-slice_fusion), calls=%async_computation.1 | async-start | bytes 1048576 | tf_op jit(solution)/shard_map/all_to_all | solution.py:334
  46.3 0.7 copy-start.1
  47.5 1.8 %collective-permute-start.3 = (s32[40,128]{1,0:T(8,128)S(1)}, s32[40,128]{1,0:T(8,128)S(1)}, u32[]{:S(2)}, u32[]{:S(2)}) collective-permute-start(s32[40,128]{1,0:T(8,128)S(1)} %tables.1), channel_id=1, source_target_pairs={{0,128},{128,0},{1,129},{129,1},{2,130},{130,2},{3,131},{131,3},{4... | collective-permute-start | bytes 61448 | tf_op jit(solution)/shard_map/ppermute | solution.py:307
  49.9 13.2 %collective-permute-start.7 = (bf16[32,64,128]{2,1,0:T(8,128)(2,1)S(1)}, bf16[32,64,128]{2,1,0:T(8,128)(2,1)S(1)}, u32[]{:S(2)}, u32[]{:S(2)}) collective-permute-start(bf16[32,64,128]{2,1,0:T(8,128)(2,1)S(1)} %all_to_all.20.refs_0_.kv_ref), channel_id=1, source_target_pairs={{0,128},{128,0},{1,129},{129,1},{2,130},{130,2},{3,131},{131,3},{4... | collective-permute-start | bytes 1572872 | tf_op jit(solution)/shard_map/ppermute | solution.py:307
  53.0 2.9 %copy-start.6 = (bf16[32,64,128]{2,1,0:T(8,128)(2,1)}, bf16[32,64,128]{2,1,0:T(8,128)(2,1)S(1)}, u32[]{:S(2)}) copy-start(bf16[32,64,128]{2,1,0:T(8,128)(2,1)S(1)} %collective-permute-done.1.refs_1_) | copy-start | bytes 1572868
  53.0 4.3 %copy-start.7 = (bf16[32,64,128]{2,1,0:T(8,128)(2,1)}, bf16[32,64,128]{2,1,0:T(8,128)(2,1)S(1)}, u32[]{:S(2)}) copy-start(bf16[32,64,128]{2,1,0:T(8,128)(2,1)S(1)} %collective-permute-done.2.refs_2_) | copy-start | bytes 1572868
  53.0 8.2 %collective-permute-start.5 = (bf16[16,64,128]{2,1,0:T(8,128)(2,1)S(1)}, bf16[16,64,128]{2,1,0:T(8,128)(2,1)S(1)}, u32[]{:S(2)}, u32[]{:S(2)}) collective-permute-start(bf16[16,64,128]{2,1,0:T(8,128)(2,1)S(1)} %slice.12), channel_id=1, source_target_pairs={{0,1},{1,2},{2,3},{3,0},{4,5},{5,6},{6,7},{7,4},{8,9},{9,10},{10,1... | collective-permute-start | bytes 786440 | tf_op jit(solution)/shard_map/ppermute | solution.py:316
  54.0 9.0 %collective-permute-start.6 = (bf16[16,64,128]{2,1,0:T(8,128)(2,1)S(1)}, bf16[16,64,128]{2,1,0:T(8,128)(2,1)}, u32[]{:S(2)}, u32[]{:S(2)}) collective-permute-start(bf16[16,64,128]{2,1,0:T(8,128)(2,1)S(1)} %slice.13), channel_id=1, source_target_pairs={{0,3},{1,0},{2,1},{3,2},{4,7},{5,4},{6,5},{7,6},{8,11},{9,8},{10,9... | collective-permute-start | bytes 786440 | tf_op jit(solution)/shard_map/ppermute | solution.py:317
  55.8 10.4 %collective-permute-start.8 = (bf16[32,64,128]{2,1,0:T(8,128)(2,1)S(1)}, bf16[32,64,128]{2,1,0:T(8,128)(2,1)}, u32[]{:S(2)}, u32[]{:S(2)}) collective-permute-start(bf16[32,64,128]{2,1,0:T(8,128)(2,1)S(1)} %collective-permute-done.1.refs_1_), channel_id=1, source_target_pairs={{0,128},{128,0},{1,129},{129,1},{2,130},{130,2},{3,131},{131,3},{4... | collective-permute-start | bytes 1572872 | tf_op jit(solution)/shard_map/ppermute | solution.py:307
  57.3 9.0 %collective-permute-start.9 = (bf16[32,64,128]{2,1,0:T(8,128)(2,1)S(1)}, bf16[32,64,128]{2,1,0:T(8,128)(2,1)}, u32[]{:S(2)}, u32[]{:S(2)}) collective-permute-start(bf16[32,64,128]{2,1,0:T(8,128)(2,1)S(1)} %collective-permute-done.2.refs_2_), channel_id=1, source_target_pairs={{0,128},{128,0},{1,129},{129,1},{2,130},{130,2},{3,131},{131,3},{4... | collective-permute-start | bytes 1572872 | tf_op jit(solution)/shard_map/ppermute | solution.py:307
  61.2 5.0 %copy-start.16 = (bf16[16,64,128]{2,1,0:T(8,128)(2,1)}, bf16[16,64,128]{2,1,0:T(8,128)(2,1)S(1)}, u32[]{:S(2)}) copy-start(bf16[16,64,128]{2,1,0:T(8,128)(2,1)S(1)} %collective-permute-done.5.refs_3_) | copy-start | bytes 786436
  61.2 3.1 %collective-permute-start.10 = (bf16[16,64,128]{2,1,0:T(8,128)(2,1)S(1)}, bf16[16,64,128]{2,1,0:T(8,128)(2,1)}, u32[]{:S(2)}, u32[]{:S(2)}) collective-permute-start(bf16[16,64,128]{2,1,0:T(8,128)(2,1)S(1)} %collective-permute-done.5.refs_3_), channel_id=1, source_target_pairs={{0,128},{128,0},{1,129},{129,1},{2,130},{130,2},{3,131},{131,3},{4... | collective-permute-start | bytes 786440 | tf_op jit(solution)/shard_map/ppermute | solution.py:307
  63.0 3.3 %collective-permute-start.11 = (bf16[16,64,128]{2,1,0:T(8,128)(2,1)}, bf16[16,64,128]{2,1,0:T(8,128)(2,1)}, u32[]{:S(2)}, u32[]{:S(2)}) collective-permute-start(bf16[16,64,128]{2,1,0:T(8,128)(2,1)} %collective-permute-done.6.refs_4_), channel_id=1, source_target_pairs={{0,128},{128,0},{1,129},{129,1},{2,130},{130,2},{3,131},{131,3},{4... | collective-permute-start | bytes 786440 | tf_op jit(solution)/shard_map/ppermute | solution.py:307
  63.1 3.2 %copy-start.3 = (bf16[32,64,128]{2,1,0:T(8,128)(2,1)}, bf16[32,64,128]{2,1,0:T(8,128)(2,1)S(1)}, u32[]{:S(2)}) copy-start(bf16[32,64,128]{2,1,0:T(8,128)(2,1)S(1)} %all-to-all-done.1.qg_ref.refs_0_) | copy-start | bytes 1572868
  63.1 3.2 %copy-start.11 = (bf16[32,64,128]{2,1,0:T(8,128)(2,1)}, bf16[32,64,128]{2,1,0:T(8,128)(2,1)S(1)}, u32[]{:S(2)}) copy-start(bf16[32,64,128]{2,1,0:T(8,128)(2,1)S(1)} %collective-permute-done.7.refs_5_) | copy-start | bytes 1572868
  63.1 17.3 %collective-permute-start.12 = (bf16[32,64,128]{2,1,0:T(8,128)(2,1)S(1)}, bf16[32,64,128]{2,1,0:T(8,128)(2,1)S(1)}, u32[]{:S(2)}, u32[]{:S(2)}) collective-permute-start(bf16[32,64,128]{2,1,0:T(8,128)(2,1)S(1)} %all-to-all-done.1.qg_ref.refs_0_), channel_id=1, source_target_pairs={{0,1},{1,2},{2,3},{3,0},{4,5},{5,6},{6,7},{7,4},{8,9},{9,10},{10,1... | collective-permute-start | bytes 1572872 | tf_op jit(solution)/shard_map/ppermute | solution.py:311
  64.3 16.1 %collective-permute-start.13 = (bf16[32,64,128]{2,1,0:T(8,128)(2,1)S(1)}, bf16[32,64,128]{2,1,0:T(8,128)(2,1)S(1)}, u32[]{:S(2)}, u32[]{:S(2)}) collective-permute-start(bf16[32,64,128]{2,1,0:T(8,128)(2,1)S(1)} %all-to-all-done.1.qg_ref.refs_0_), channel_id=1, source_target_pairs={{0,3},{1,0},{2,1},{3,2},{4,7},{5,4},{6,5},{7,6},{8,11},{9,8},{10,9... | collective-permute-start | bytes 1572872 | tf_op jit(solution)/shard_map/ppermute | solution.py:311
  78.3 5.0 %copy-start.4 = (bf16[32,64,128]{2,1,0:T(8,128)(2,1)S(1)}, bf16[32,64,128]{2,1,0:T(8,128)(2,1)}, u32[]{:S(2)}) copy-start(bf16[32,64,128]{2,1,0:T(8,128)(2,1)} %copy-done.3) | copy-start | bytes 1572868
  78.3 5.6 %collective-permute-start.16 = (f32[32,128]{1,0:T(8,128)}, f32[32,128]{1,0:T(8,128)S(1)}, u32[]{:S(2)}, u32[]{:S(2)}) collective-permute-start(f32[32,128]{1,0:T(8,128)} %get-tuple-element.37), channel_id=1, source_target_pairs={{0,128},{128,0},{1,129},{129,1},{2,130},{130,2},{3,131},{131,3},{4... | collective-permute-start | bytes 49160 | tf_op jit(solution)/shard_map/ppermute | solution.py:307
  80.4 4.0 %copy-start.8 = (bf16[32,64,128]{2,1,0:T(8,128)(2,1)}, bf16[32,64,128]{2,1,0:T(8,128)(2,1)S(1)}, u32[]{:S(2)}) copy-start(bf16[32,64,128]{2,1,0:T(8,128)(2,1)S(1)} %collective-permute-done.12.refs_1_) | copy-start | bytes 1572868
  80.4 4.0 %copy-start.9 = (bf16[32,64,128]{2,1,0:T(8,128)(2,1)}, bf16[32,64,128]{2,1,0:T(8,128)(2,1)S(1)}, u32[]{:S(2)}) copy-start(bf16[32,64,128]{2,1,0:T(8,128)(2,1)S(1)} %collective-permute-done.13.refs_2_) | copy-start | bytes 1572868
  80.5 4.0 %copy-start.10 = (f32[32,128]{1,0:T(8,128)S(1)}, f32[32,128]{1,0:T(8,128)}, u32[]{:S(2)}) copy-start(f32[32,128]{1,0:T(8,128)} %get-tuple-element.37) | copy-start | bytes 49156
  80.5 12.2 %collective-permute-start.14 = (bf16[16,64,128]{2,1,0:T(8,128)(2,1)S(1)}, bf16[16,64,128]{2,1,0:T(8,128)(2,1)S(1)}, u32[]{:S(2)}, u32[]{:S(2)}) collective-permute-start(bf16[16,64,128]{2,1,0:T(8,128)(2,1)S(1)} %slice.14), channel_id=1, source_target_pairs={{0,1},{1,2},{2,3},{3,0},{4,5},{5,6},{6,7},{7,4},{8,9},{9,10},{10,1... | collective-permute-start | bytes 786440 | tf_op jit(solution)/shard_map/ppermute | solution.py:316
  80.6 12.1 %collective-permute-start.15 = (bf16[16,64,128]{2,1,0:T(8,128)(2,1)S(1)}, bf16[16,64,128]{2,1,0:T(8,128)(2,1)S(1)}, u32[]{:S(2)}, u32[]{:S(2)}) collective-permute-start(bf16[16,64,128]{2,1,0:T(8,128)(2,1)S(1)} %slice.15), channel_id=1, source_target_pairs={{0,3},{1,0},{2,1},{3,2},{4,7},{5,4},{6,5},{7,6},{8,11},{9,8},{10,9... | collective-permute-start | bytes 786440 | tf_op jit(solution)/shard_map/ppermute | solution.py:317
  83.3 10.9 %collective-permute-start.17 = (bf16[32,64,128]{2,1,0:T(8,128)(2,1)S(1)}, bf16[32,64,128]{2,1,0:T(8,128)(2,1)S(1)}, u32[]{:S(2)}, u32[]{:S(2)}) collective-permute-start(bf16[32,64,128]{2,1,0:T(8,128)(2,1)S(1)} %copy-done.4), channel_id=1, source_target_pairs={{0,128},{128,0},{1,129},{129,1},{2,130},{130,2},{3,131},{131,3},{4... | collective-permute-start | bytes 1572872 | tf_op jit(solution)/shard_map/ppermute | solution.py:307
  83.9 10.3 %collective-permute-start.18 = (bf16[32,64,128]{2,1,0:T(8,128)(2,1)S(1)}, bf16[32,64,128]{2,1,0:T(8,128)(2,1)S(1)}, u32[]{:S(2)}, u32[]{:S(2)}) collective-permute-start(bf16[32,64,128]{2,1,0:T(8,128)(2,1)S(1)} %collective-permute-done.12.refs_1_), channel_id=1, source_target_pairs={{0,128},{128,0},{1,129},{129,1},{2,130},{130,2},{3,131},{131,3},{4... | collective-permute-start | bytes 1572872 | tf_op jit(solution)/shard_map/ppermute | solution.py:307
  83.9 10.3 %collective-permute-start.19 = (bf16[32,64,128]{2,1,0:T(8,128)(2,1)S(1)}, bf16[32,64,128]{2,1,0:T(8,128)(2,1)S(1)}, u32[]{:S(2)}, u32[]{:S(2)}) collective-permute-start(bf16[32,64,128]{2,1,0:T(8,128)(2,1)S(1)} %collective-permute-done.13.refs_2_), channel_id=1, source_target_pairs={{0,128},{128,0},{1,129},{129,1},{2,130},{130,2},{3,131},{131,3},{4... | collective-permute-start | bytes 1572872 | tf_op jit(solution)/shard_map/ppermute | solution.py:307
  92.7 3.5 %copy-start.15 = (bf16[16,64,128]{2,1,0:T(8,128)(2,1)}, bf16[16,64,128]{2,1,0:T(8,128)(2,1)S(1)}, u32[]{:S(2)}) copy-start(bf16[16,64,128]{2,1,0:T(8,128)(2,1)S(1)} %collective-permute-done.14.refs_3_) | copy-start | bytes 786436
  92.7 3.5 %copy-start.17 = (bf16[16,64,128]{2,1,0:T(8,128)(2,1)}, bf16[16,64,128]{2,1,0:T(8,128)(2,1)S(1)}, u32[]{:S(2)}) copy-start(bf16[16,64,128]{2,1,0:T(8,128)(2,1)S(1)} %collective-permute-done.15.refs_4_) | copy-start | bytes 786436
  92.7 2.4 %collective-permute-start.20 = (bf16[16,64,128]{2,1,0:T(8,128)(2,1)S(1)}, bf16[16,64,128]{2,1,0:T(8,128)(2,1)S(1)}, u32[]{:S(2)}, u32[]{:S(2)}) collective-permute-start(bf16[16,64,128]{2,1,0:T(8,128)(2,1)S(1)} %collective-permute-done.14.refs_3_), channel_id=1, source_target_pairs={{0,128},{128,0},{1,129},{129,1},{2,130},{130,2},{3,131},{131,3},{4... | collective-permute-start | bytes 786440 | tf_op jit(solution)/shard_map/ppermute | solution.py:307
  93.9 1.5 %collective-permute-start.21 = (bf16[16,64,128]{2,1,0:T(8,128)(2,1)S(1)}, bf16[16,64,128]{2,1,0:T(8,128)(2,1)S(1)}, u32[]{:S(2)}, u32[]{:S(2)}) collective-permute-start(bf16[16,64,128]{2,1,0:T(8,128)(2,1)S(1)} %collective-permute-done.15.refs_4_), channel_id=1, source_target_pairs={{0,128},{128,0},{1,129},{129,1},{2,130},{130,2},{3,131},{131,3},{4... | collective-permute-start | bytes 786440 | tf_op jit(solution)/shard_map/ppermute | solution.py:307
  94.2 1.9 %copy-start.12 = (bf16[32,64,128]{2,1,0:T(8,128)(2,1)}, bf16[32,64,128]{2,1,0:T(8,128)(2,1)S(1)}, u32[]{:S(2)}) copy-start(bf16[32,64,128]{2,1,0:T(8,128)(2,1)S(1)} %collective-permute-done.17.refs_5_) | copy-start | bytes 1572868
  94.2 1.9 %copy-start.13 = (bf16[32,64,128]{2,1,0:T(8,128)(2,1)}, bf16[32,64,128]{2,1,0:T(8,128)(2,1)S(1)}, u32[]{:S(2)}) copy-start(bf16[32,64,128]{2,1,0:T(8,128)(2,1)S(1)} %collective-permute-done.18.refs_6_) | copy-start | bytes 1572868
  94.2 1.9 %copy-start.14 = (bf16[32,64,128]{2,1,0:T(8,128)(2,1)}, bf16[32,64,128]{2,1,0:T(8,128)(2,1)S(1)}, u32[]{:S(2)}) copy-start(bf16[32,64,128]{2,1,0:T(8,128)(2,1)S(1)} %collective-permute-done.19.refs_7_) | copy-start | bytes 1572868
  95.0 1.1 copy-start.18
  95.4 0.7 copy-start.19
  133.5 4.3 %collective-permute-start.22 = (bf16[16,96,128]{2,1,0:T(8,128)(2,1)S(1)}, bf16[16,96,128]{2,1,0:T(8,128)(2,1)S(1)}, u32[]{:S(2)}, u32[]{:S(2)}) collective-permute-start(bf16[16,96,128]{2,1,0:T(8,128)(2,1)S(1)} %constant_dynamic-slice_fusion), channel_id=1, source_target_pairs={{0,128},{128,0},{1,129},{129,1},{2,130},{130,2},{3,131},{131,3},{4... | collective-permute-start | bytes 1179656 | tf_op jit(solution)/shard_map/ppermute | solution.py:307
